TPU v7x, 128 devices: a whole 4x4x4 slice. The times are simulated.
128 devices in a mesh: dp: 8 (over y, x_hi), tensor: 16 (over z, x_lo, core).
Axes of the slice: x: 4 (x_hi: 2, x_lo: 2; x = x_hi * 2 + x_lo), y: 4, z: 4, core: 2. Of those that a mesh axis runs over, the one named last changes fastest.
Arguments:
- acts: bfloat16 [64, 512, 28672], P('dp', None, 'tensor'), may hold values from -6 to 6
- grads: bfloat16 [64, 512, 8192], P('dp', None, 'tensor'), may hold values from -6 to 6
- proj_in: bfloat16 [28672, 64], P('tensor'), may hold values from -0.03125 to 0.03125
- proj_out: bfloat16 [8192, 64], P('tensor'), may hold values from -0.0625 to 0.0625
- queries: float32 [512, 4096], P('dp', 'tensor'), may hold values from -6 to 6
Outputs:
- scores: float32 [64, 512], P('dp')
All inputs are finite; a program needn't handle non-finite values.
Results may differ from a plain program's by a relative error of at most 0.0003.
Values sent between devices are 32-bit elements; how exact they have to be, the bound alone decides.
No kernel may reach another device: no remote copies, remote signals or barrier semaphores. Data moves between devices by JAX's collectives and lax.ppermute only.
A program may use at most 128 MiB of HBM per device.

v0:
```python
import jax
import jax.numpy as jnp
from jax import lax
from jax.sharding import PartitionSpec as P


def score_block(encoded, n_query):

    def add_block(carry, piece, start):
        block = jnp.einsum("ek,qk->eq", encoded, piece, precision=lax.Precision.HIGHEST)
        return block

    empty = jnp.zeros((encoded.shape[0], n_query), jnp.float32)
    return (add_block, empty)


def per_device(acts, grads, proj_in, proj_out, queries):
    examples, length, width_in = acts.shape
    width_out = grads.shape[2]
    rank = proj_in.shape[1]
    n_query = queries.shape[0] * lax.axis_size("dp")
    partial_in = jnp.dot(
        acts.reshape(examples * length, width_in), proj_in, preferred_element_type=jnp.float32
    )
    partial_out = jnp.dot(
        grads.reshape(examples * length, width_out), proj_out, preferred_element_type=jnp.float32
    )
    factor = length ** (-0.5)
    side_in, side_out = lax.psum((partial_in, partial_out), "tensor")
    encoded = jnp.einsum(
        "eti,etj->eij",
        side_out.reshape(examples, length, rank),
        side_in.reshape(examples, length, rank),
        precision=lax.Precision.HIGHEST,
    )
    encoded = (encoded * factor).reshape(examples, rank * rank)
    wide_queries = lax.all_gather(queries, "tensor", axis=1, tiled=True)
    add_block, empty = score_block(encoded, n_query)
    total = add_block(empty, lax.all_gather(wide_queries, "dp", axis=0, tiled=True), jnp.int32(0))
    return total / rank


def solution(mesh):
    in_specs = (
        P("dp", None, "tensor"),
        P("dp", None, "tensor"),
        P("tensor", None),
        P("tensor", None),
        P("dp", "tensor"),
    )
    out_specs = P("dp", None)
    return jax.shard_map(
        per_device, mesh=mesh, in_specs=in_specs, out_specs=out_specs, check_vma=False
    )
```

profile of v0, /device:TPU:0, one launch (start us, length us, event | category | flops | bytes accessed | tf_op | source)
XLA Modules:
  0.0 297.9 jit_solution(17590835780034399757)
XLA Ops:
  6.5 0.0 copy-start
  6.5 0.0 all-gather.3.cloned.1.call-start
  6.5 0.7 all-gather.3.cloned.1.call-update
  7.3 0.0 all-reduce.3.cloned.1.call-start
  7.3 3.6 %fusion = f32[4096,64]{0,1:T(8,128)S(1)} fusion(bf16[4096,512]{1,0:T(8,128)(2,1)} %bitcast.17, bf16[512,64]{0,1:T(8,128)(2,1)} %param.8), kind=kOutput, calls=%fused_computation.4 | convolution fusion | flops 268435456 | bytes 5308416 | tf_op jit(solution)/shard_map/dot_general | solution.py:25
  10.9 0.0 copy-done
  10.9 9.7 %fusion.1 = f32[4096,64]{0,1:T(8,128)S(1)} fusion(bf16[4096,1792]{1,0:T(8,128)(2,1)} %bitcast.16, bf16[1792,64]{0,1:T(8,128)(2,1)S(1)} %copy-done), kind=kOutput, calls=%fused_computation.5 | convolution fusion | flops 939524096 | bytes 15958016 | tf_op jit(solution)/shard_map/dot_general | solution.py:22
  20.5 1.7 copy_bitcast_fusion
  22.2 0.0 all-reduce.3.cloned.1.call-update
  22.2 0.0 all-gather.5.cloned.1.call-start
  22.3 21.8 %all-gather.3.cloned.1.call-done = f32[64,4096]{1,0:T(8,128)} async-done(((f32[64,256]{1,0:T(8,128)}), f32[64,4096]{1,0:T(8,128)}) %all-gather.3.cloned.1.call-update) | async-done | bytes 1048592 | tf_op jit(solution)/shard_map/all_gather | solution.py:37
  44.1 0.0 all-gather.5.cloned.1.call-update
  44.1 128.3 %all-reduce.3.cloned.1.call-done = (f32[8,512,64]{1,2,0:T(8,128)}, f32[8,512,64]{1,2,0:T(8,128)}) async-done(((f32[8,512,64]{1,2,0:T(8,128)}, f32[8,512,64]{1,2,0:T(8,128)}), (f32[8,512,64]{1,2,0:T(8,128)}, f32[8,512,64]{1,2,0:T(8,128)})) %all-reduce.3.cloned.1.call-update) | async-done | bytes 2097168 | tf_op jit(solution)/shard_map/psum | solution.py:29
  172.4 2.6 convolution_multiply_fusion
  175.0 0.1 reshape.19
  175.1 106.4 %all-gather.5.cloned.1.call-done = f32[512,4096]{1,0:T(8,128)} async-done(((f32[64,4096]{1,0:T(8,128)}), f32[512,4096]{1,0:T(8,128)}) %all-gather.5.cloned.1.call-update) | async-done | bytes 8388624 | tf_op jit(solution)/shard_map/all_gather | solution.py:39
  281.5 9.8 %convolution_multiply_fusion.1 = f32[8,512]{1,0:T(8,128)} fusion(f32[8,4096]{1,0:T(8,128)S(1)} %reshape.19, f32[512,4096]{1,0:T(8,128)} %all-gather.5.cloned.1.call-done), kind=kOutput, calls=%fused_computation.1 | convolution fusion | flops 201330688 | bytes 8536064 | tf_op jit(solution)/shard_map/ek,qk->eq/dot_general | solution.py:10
Async XLA Ops:
  6.5 4.3 %copy-start = (bf16[1792,64]{0,1:T(8,128)(2,1)S(1)}, bf16[1792,64]{0,1:T(8,128)(2,1)}, u32[]{:S(2)}) copy-start(bf16[1792,64]{0,1:T(8,128)(2,1)} %param.7) | copy-start | bytes 688132
  6.5 37.5 %all-gather.3.cloned.1.call-start = ((), (), s32[]{:S(2)}) async-start(), calls=%async_computation | async-start | bytes 1114112 | tf_op jit(solution)/shard_map/all_gather | solution.py:37
  7.3 165.1 %all-reduce.3.cloned.1.call-start = ((), (), s32[]{:S(2)}) async-start(), calls=%async_computation.2 | async-start | bytes 4194304 | tf_op jit(solution)/shard_map/psum | solution.py:29
  22.2 259.3 %all-gather.5.cloned.1.call-start = ((), (), s32[]{:S(2)}) async-start(), calls=%async_computation.1 | async-start | bytes 9437184 | tf_op jit(solution)/shard_map/all_gather | solution.py:39
Sparse Core Ops, SparseCore 0:
  9.0 35.0 all-gather.2
  46.6 125.7 all-reduce.2
  174.8 106.7 all-gather.4
where the time goes:
time: 298 us
  waiting for transfers between devices  257 us (86%)
  matrix products  25.6 us (9%)
  between operations  13.1 us (4%)
    psum x1, waiting for transfers between devices, per_device(): side_in, side_out = lax.psum((partial_in, partial_out), 'tensor')  128 us
    all_gather x1, waiting for transfers between devices, per_device(): lax.all_gather(wide_queries, 'dp', axis=0, tiled=True)  106 us
    all_gather x1, waiting for transfers between devices, per_device(): wide_queries = lax.all_gather(queries, 'tensor', axis=1, tiled=True)  21.8 us
    dot_general x1, matrix products, add_block(): jnp.einsum('ek,qk->eq', encoded, piece, precision=lax.Precision.HIGHEST)  9.8 us
    dot_general x1, matrix products, per_device(): jnp.dot(acts.reshape(examples * length, width_in), proj_in, preferred_ele...  9.67 us
  transfers between devices with their start and end apart: 3, of which 3 were waited for; matrix products, arithmetic and copies ran while one was open for 6% of the time, Pallas kernels for 0%

commit v1 on v0

v1 whole, which is shorter than its diff:
```python
import functools

import jax
import jax.numpy as jnp
from jax import lax
from jax.experimental import pallas as pl
from jax.experimental.pallas import tpu as pltpu
from jax.sharding import PartitionSpec as P

ROWS = 128
NT = (((1,), (1,)), ((), ()))
TN = (((0,), (0,)), ((), ()))


def place():
    t = lax.axis_index("tensor")
    return t // 4, (t // 2) % 2, t % 2


def example_of(position, x_first, z, x):
    if x_first:
        dx, dz = position // 4, position % 4
    else:
        dz, dx = position // 2, position % 2
    return 2 * ((z + dz) % 4) + (x + dx) % 2


def project_kernel(half, mine, x_first, cuts, acts, grads, pin, pout, *rest):
    received = rest[0] if mine else None
    outs = rest[1:-3] if mine else rest[:-3]
    held_a, held_g, sem = rest[-3:]
    z, x, core = place()
    part = core if mine else 1 - core
    row = half * 2 * ROWS + part * ROWS
    copies = []
    for p in range(8):
        e = example_of(p, x_first, z, x)
        where = pl.ds(pl.multiple_of(row, ROWS), ROWS)
        ca = pltpu.make_async_copy(acts.at[e, where, :], held_a.at[pl.ds(p * ROWS, ROWS), :], sem.at[0, p])
        cg = pltpu.make_async_copy(grads.at[e, where, :], held_g.at[pl.ds(p * ROWS, ROWS), :], sem.at[1, p])
        cg.start()
        ca.start()
        copies.append((ca, cg))
    for g in range(2):
        for ca, cg in copies[4 * g : 4 * g + 4]:
            cg.wait()
            ca.wait()
        rows = pl.ds(g * 4 * ROWS, 4 * ROWS)
        so = lax.dot_general(held_g[rows, :], pout[...], NT, preferred_element_type=jnp.float32)
        si = lax.dot_general(held_a[rows, :], pin[...], NT, preferred_element_type=jnp.float32)
        both = jnp.concatenate([so, si], axis=1).reshape(4, ROWS, 128)
        if mine:
            both = both + received[pl.ds(4 * g, 4)]
        for k, ref in enumerate(outs):
            lo, hi = max(cuts[k], 4 * g), min(cuts[k + 1], 4 * g + 4)
            if lo < hi:
                ref[lo - cuts[k] : hi - cuts[k]] = both[lo - 4 * g : hi - 4 * g]


def project(half, mine, x_first, cuts, acts, grads, pin, pout, received=None):
    any_space = pl.BlockSpec(memory_space=pl.ANY)
    vmem = pl.BlockSpec(memory_space=pltpu.VMEM)
    args = (acts, grads, pin, pout) + ((received,) if mine else ())
    return pl.pallas_call(
        functools.partial(project_kernel, half, mine, x_first, cuts),
        out_shape=[
            jax.ShapeDtypeStruct((b - a, ROWS, 128), jnp.float32) for a, b in zip(cuts, cuts[1:])
        ],
        in_specs=[any_space, any_space, vmem, vmem] + ([vmem] if mine else []),
        out_specs=[vmem] * (len(cuts) - 1),
        scratch_shapes=[
            pltpu.VMEM((8 * ROWS, acts.shape[2]), acts.dtype),
            pltpu.VMEM((8 * ROWS, grads.shape[2]), grads.dtype),
            pltpu.SemaphoreType.DMA((2, 8)),
        ],
        compiler_params=pltpu.CompilerParams(vmem_limit_bytes=40 << 20),
        name=f"project_{half}_{'keep' if mine else 'send'}",
    )(*args)


def encode_kernel(own0, a1, a2, a3, own1, b1, out, enc):
    z, x, _ = place()
    m0 = (own0[...] + a2[...]) + (a1[...] + a3[...])
    m1 = own1[...] + b1[...]
    m = jnp.concatenate([m0, m1], axis=0)
    enc[...] = lax.dot_general(
        m[:, :64], m[:, 64:], TN, precision=lax.Precision.HIGHEST, preferred_element_type=jnp.float32
    )
    for p in range(8):
        g = example_of(p, True, z, x)
        out[p] = enc[pl.ds(pl.multiple_of(8 * g, 8), 8), :]


def encode(*args):
    return pl.pallas_call(
        encode_kernel,
        out_shape=jax.ShapeDtypeStruct((8, 8, 64), jnp.float32),
        scratch_shapes=[pltpu.VMEM((64, 64), jnp.float32)],
        name="encode",
    )(*args)


def score_kernel(scale, own, other, r1, r2, r3, q_own, q_other, out, tiles):
    z, x, core = place()
    y = lax.axis_index("dp") // 2
    for dz, pair in enumerate((None, r1, r2, r3)):
        for dx in range(2):
            e = 2 * ((z - dz + 4) % 4) + (x + dx) % 2
            tile = (own, other)[dx][0] if pair is None else pair[dx]
            tiles[pl.ds(pl.multiple_of(8 * e, 8), 8), :] = tile
    low = jnp.concatenate([tiles[pl.ds(i, 8, stride=8), :] for i in range(4)], axis=1)
    high = jnp.concatenate([tiles[pl.ds(i, 8, stride=8), :] for i in range(4, 8)], axis=1)
    mine = jnp.where(core == 0, low, high) * scale
    theirs = jnp.where(core == 0, high, low) * scale
    for dy in range(4):
        rows = pl.ds(128 * dy, 128)
        a = lax.dot_general(
            mine, q_own[rows, :], NT, precision=lax.Precision.HIGHEST, preferred_element_type=jnp.float32
        )
        b = lax.dot_general(
            theirs, q_other[rows, :], NT, precision=lax.Precision.HIGHEST, preferred_element_type=jnp.float32
        )
        out[:, pl.ds(pl.multiple_of(128 * ((y - dy + 4) % 4), 128), 128)] = a + b


def score(scale, *args):
    return pl.pallas_call(
        functools.partial(score_kernel, scale),
        out_shape=jax.ShapeDtypeStruct((8, 512), jnp.float32),
        scratch_shapes=[pltpu.VMEM((64, 64), jnp.float32)],
        name="score",
    )(*args)


def move(value, axis, to):
    n = lax.axis_size(axis)
    return lax.ppermute(value, axis, [(i, to(i)) for i in range(n)])


def to_core(value):
    return move(value, "tensor", lambda t: t ^ 1)


def to_x(value):
    return move(value, "tensor", lambda t: t ^ 2)


def to_z(value, dz):
    return move(value, "tensor", lambda t: (t + 4 * dz) % 16)


def per_device(acts, grads, proj_in, proj_out, queries):
    length = acts.shape[1]
    rank = proj_in.shape[1]
    pin, pout = proj_in.T, proj_out.T

    with jax.named_scope("sides"):
        (send0,) = project(0, False, True, (0, 8), acts, grads, pin, pout)
        got0 = to_core(send0)
        (send1,) = project(1, False, False, (0, 8), acts, grads, pin, pout)
        got1 = to_core(send1)
        near0, far0 = project(0, True, True, (0, 4, 8), acts, grads, pin, pout, got0)
        other0 = to_x(far0)
        near1, z1, z2, z3 = project(1, True, False, (0, 2, 4, 6, 8), acts, grads, pin, pout, got1)
        z1, z2, z3 = to_z(z1, 1), to_z(z2, 2), to_z(z3, 3)
        sum0 = near0 + other0
        w1, w2, w3 = to_z(sum0[1], 1), to_z(sum0[2], 2), to_z(sum0[3], 3)
        sum1 = (near1 + z2) + (z1 + z3)
        v1 = to_x(sum1[1])

    with jax.named_scope("queries"):
        x_hi = lax.axis_index("dp") % 2
        beside = move(queries, "dp", lambda d: d ^ 1)
        pair = jnp.where(
            x_hi == 0, jnp.concatenate([queries, beside]), jnp.concatenate([beside, queries])
        )
        rest = [move(pair, "dp", lambda d, dy=dy: (d + 2 * dy) % 8) for dy in (1, 2, 3)]
        q_own = jnp.concatenate([pair] + rest)
        q_other = to_core(q_own)

    with jax.named_scope("encode"):
        encoded = encode(sum0[0], w1, w2, w3, sum1[0], v1)
        encoded = encoded + to_core(encoded)
        keep, send = encoded[:4], encoded[4:]
        other = to_x(send)
        out = [to_z(jnp.stack([keep[dz], other[dz]]), dz) for dz in (1, 2, 3)]

    with jax.named_scope("scores"):
        part = score(length ** (-0.5) / rank, keep, other, *out, q_own, q_other)
        part = part + to_x(part)
        s1, s2, s3 = to_z(part, 1), to_z(part, 2), to_z(part, 3)
        return (part + s2) + (s1 + s3)


def solution(mesh):
    in_specs = (
        P("dp", None, "tensor"),
        P("dp", None, "tensor"),
        P("tensor", None),
        P("tensor", None),
        P("dp", "tensor"),
    )
    out_specs = P("dp", None)
    return jax.shard_map(
        per_device, mesh=mesh, in_specs=in_specs, out_specs=out_specs, check_vma=False
    )
```

time: 298 us -> 91 us (0.31)
  waiting for transfers between devices: 257 us -> 22.7 us
  starting transfers between devices: 0.08 us -> 32.1 us
  matrix products: 25.6 us -> 0 us
  Pallas kernels: 0 us -> 23.9 us
  between operations: 13.1 us -> 0.19 us
  local copies, waits for them, and re-layouts: 1.78 us -> 9.25 us
    psum x1 -> x0, waiting for transfers between devices: 128 us -> none  [per_device(): side_in, side_out = lax.psum((partial_in, partial_out), 'tensor')]
    all_gather x2 -> x0, waiting for transfers between devices: 128 us -> none  [the longest x1 106 us: per_device(): lax.all_gather(wide_queries, 'dp', axis=0, tiled=True)]
    ppermute x0 -> x24, starting transfers between devices: none -> 32.1 us  [move(): return lax.ppermute(value, axis, [(i, to(i)) for i in range(n)])]
    dot_general x4 -> x0, matrix products: 25.6 us -> none  [the longest x1 9.8 us: add_block(): jnp.einsum('ek,qk->eq', encoded, piece, precision=lax.Precision.HIGHEST)]
    pallas_call x0 -> x6, Pallas kernels: none -> 23.9 us  [the longest x4 19.1 us: project(): pl.pallas_call(functools.partial(project_kernel, half, mine, x_first, cut...]
    ppermute x0 -> x24, waiting for transfers between devices: none -> 22.7 us  [move(): return lax.ppermute(value, axis, [(i, to(i)) for i in range(n)])]
    unnamed x2 -> x34, local copies, waits for them, and re-layouts: 0.01 us -> 7.38 us
  transfers between devices with their start and end apart: 3 -> 24, of which waited for: 3 -> 11; matrix products, arithmetic and copies ran while one was open for 6% -> 3% of each run, Pallas kernels for 0% -> 18%
where the time goes in v1:
time: 91 us; the launch traced here: 90.4 us
  starting transfers between devices  32.1 us (35%)
  Pallas kernels  23.9 us (26%)
  waiting for transfers between devices  22.7 us (25%)
  local copies, waits for them, and re-layouts  9.25 us (10%)
  other arithmetic  2.22 us (2%)
    ppermute x24, starting transfers between devices, move(): return lax.ppermute(value, axis, [(i, to(i)) for i in range(n)])  32.1 us
    ppermute x24, waiting for transfers between devices, move(): return lax.ppermute(value, axis, [(i, to(i)) for i in range(n)])  22.7 us
    pallas_call x4, Pallas kernels, project(): pl.pallas_call(functools.partial(project_kernel, half, mine, x_first, cut...  19.1 us
    unnamed x34, local copies, waits for them, and re-layouts  7.38 us
    pallas_call x1, Pallas kernels, score(): pl.pallas_call(functools.partial(score_kernel, scale), out_shape=jax.Shap...  2.89 us
    pallas_call x1, Pallas kernels, encode(): pl.pallas_call(encode_kernel, out_shape=jax.ShapeDtypeStruct((8, 8, 64),...  1.92 us
  transfers between devices with their start and end apart: 24, of which 11 were waited for; matrix products, arithmetic and copies ran while one was open for 3% of the time, Pallas kernels for 18%

profile of v1, /device:TPU:0, one launch (start us, length us, event | category | flops | bytes accessed | tf_op | source)
XLA Modules:
  0.0 90.4 jit_solution(16950418596754725004)
XLA Ops:
  0.0 2.2 %copy-done = bf16[8,512,512]{2,1,0:T(8,128)(2,1)S(1)} copy-done((bf16[8,512,512]{2,1,0:T(8,128)(2,1)S(1)}, bf16[8,512,512]{2,1,0:T(8,128)(2,1)}, u32[]{:S(2)}) %copy-start) | copy-done | bytes 4194328
  2.2 0.9 %copy-done.2 = bf16[1792,64]{0,1:T(8,128)(2,1)S(1)} copy-done((bf16[1792,64]{0,1:T(8,128)(2,1)S(1)}, bf16[1792,64]{0,1:T(8,128)(2,1)}, u32[]{:S(2)}) %copy-start.2) | copy-done | bytes 229400
  3.1 0.8 copy-done.4
  4.0 4.8 %project_1_send.1 = f32[8,128,128]{2,1,0:T(8,128)S(1)} custom-call(bf16[8,512,1792]{2,1,0:T(8,128)(2,1)} %acts.7, bf16[8,512,512]{2,1,0:T(8,128)(2,1)S(1)} %copy-done, bf16[64,1792]{1,0:T(8,128)(2,1)S(1)} %bitcast.14, bf16[64,512]{1,0:T(8,128)(2,1)S(1)} %bitcast.18), custom_call_target="tpu_custom_call" | custom-call | tf_op jit(solution)/shard_map/sides/project_1_send/pallas_call | solution.py:64
  8.8 4.8 %project_0_send.1 = f32[8,128,128]{2,1,0:T(8,128)S(1)} custom-call(bf16[8,512,1792]{2,1,0:T(8,128)(2,1)} %acts.7, bf16[8,512,512]{2,1,0:T(8,128)(2,1)S(1)} %copy-done, bf16[64,1792]{1,0:T(8,128)(2,1)S(1)} %bitcast.15, bf16[64,512]{1,0:T(8,128)(2,1)S(1)} %bitcast.19), custom_call_target="tpu_custom_call" | custom-call | tf_op jit(solution)/shard_map/sides/project_0_send/pallas_call | solution.py:64
  14.2 4.8 %project_1_keep.1 = (f32[2,128,128]{2,1,0:T(8,128)S(1)}, f32[2,128,128]{2,1,0:T(8,128)S(1)}, f32[2,128,128]{2,1,0:T(8,128)S(1)}, f32[2,128,128]{2,1,0:T(8,128)S(1)}) custom-call(bf16[8,512,1792]{2,1,0:T(8,128)(2,1)} %acts.7, bf16[8,512,512]{2,1,0:T(8,128)(2,1)S(1)} %copy-done, bf16[64,1792]{1,0:T(8,128)(2,1)S(1)} %bitcast.16, bf16[64,512]{1,0:T(8,128)(2,1)S(1)} %bitcast.20, ...), custom_call_target="tpu_custom_call" | custom-call | tf_op jit(solution)/shard_map/sides/project_1_keep/pallas_call | solution.py:64
  19.0 4.0 %collective-permute-start.6 = (f32[2,128,128]{2,1,0:T(8,128)S(1)}, f32[2,128,128]{2,1,0:T(8,128)S(1)}, u32[]{:S(2)}, u32[]{:S(2)}) collective-permute-start(f32[2,128,128]{2,1,0:T(8,128)S(1)} %get-tuple-element.14), channel_id=1, source_target_pairs={{0,8},{1,9},{2,10},{3,11},{4,12},{5,13},{6,14},{7,15},{8,0},{9,1},... | collective-permute-start | bytes 393224 | tf_op jit(solution)/shard_map/sides/ppermute | solution.py:137
  23.0 1.0 %collective-permute-start.7 = (f32[2,128,128]{2,1,0:T(8,128)S(1)}, f32[2,128,128]{2,1,0:T(8,128)S(1)}, u32[]{:S(2)}, u32[]{:S(2)}) collective-permute-start(f32[2,128,128]{2,1,0:T(8,128)S(1)} %get-tuple-element.15), channel_id=1, source_target_pairs={{0,4},{1,5},{2,6},{3,7},{4,8},{5,9},{6,10},{7,11},{8,12},{9,13},{1... | collective-permute-start | bytes 393224 | tf_op jit(solution)/shard_map/sides/ppermute | solution.py:137
  24.1 2.2 %collective-permute-start.8 = (f32[2,128,128]{2,1,0:T(8,128)S(1)}, f32[2,128,128]{2,1,0:T(8,128)S(1)}, u32[]{:S(2)}, u32[]{:S(2)}) collective-permute-start(f32[2,128,128]{2,1,0:T(8,128)S(1)} %get-tuple-element.16), channel_id=1, source_target_pairs={{0,12},{1,13},{2,14},{3,15},{4,0},{5,1},{6,2},{7,3},{8,4},{9,5},{1... | collective-permute-start | bytes 393224 | tf_op jit(solution)/shard_map/sides/ppermute | solution.py:137
  26.3 3.0 %collective-permute-start.15 = (f32[64,256]{1,0:T(8,128)S(1)}, f32[64,256]{1,0:T(8,128)S(1)}, u32[]{:S(2)}, u32[]{:S(2)}) collective-permute-start(f32[64,256]{1,0:T(8,128)S(1)} %copy-done.8), channel_id=1, source_target_pairs={{0,16},{16,0},{32,48},{48,32},{64,80},{80,64},{96,112},{112,96},{1... | collective-permute-start | bytes 196616 | tf_op jit(solution)/shard_map/queries/ppermute | solution.py:137
  29.3 2.2 %copy-done.1 = bf16[8,512,512]{2,1,0:T(8,128)(2,1)S(1)} copy-done((bf16[8,512,512]{2,1,0:T(8,128)(2,1)S(1)}, bf16[8,512,512]{2,1,0:T(8,128)(2,1)}, u32[]{:S(2)}) %copy-start.1) | copy-done | bytes 4194328
  31.5 4.8 %project_0_keep.1 = (f32[4,128,128]{2,1,0:T(8,128)S(1)}, f32[4,128,128]{2,1,0:T(8,128)S(1)}) custom-call(bf16[8,512,1792]{2,1,0:T(8,128)(2,1)} %acts.7, bf16[8,512,512]{2,1,0:T(8,128)(2,1)S(1)} %copy-done.1, bf16[64,1792]{1,0:T(8,128)(2,1)S(1)} %bitcast.17, bf16[64,512]{1,0:T(8,128)(2,1)S(1)} %bitcast.21, f32[8,128,128]{2,1,0:T(8,128)S(1)} %collective-permute-done.rest_0_), custom_call_target="tpu_custom_call" | custom-call | tf_op jit(solution)/shard_map/sides/project_0_keep/pallas_call | solution.py:64
  37.6 1.4 %collective-permute-start.9 = (f32[128,128]{1,0:T(8,128)S(1)}, f32[128,128]{1,0:T(8,128)S(1)}, u32[]{:S(2)}, u32[]{:S(2)}) collective-permute-start(f32[128,128]{1,0:T(8,128)S(1)} %get-tuple-element.21), channel_id=1, source_target_pairs={{0,2},{1,3},{2,0},{3,1},{4,6},{5,7},{6,4},{7,5},{8,10},{9,11},{10,... | collective-permute-start | bytes 196616 | tf_op jit(solution)/shard_map/sides/ppermute | solution.py:137
  39.1 5.2 %collective-permute-done.1 = f32[4,128,128]{2,1,0:T(8,128)S(1)} collective-permute-done((f32[4,128,128]{2,1,0:T(8,128)S(1)}, f32[4,128,128]{2,1,0:T(8,128)S(1)}, u32[]{:S(2)}, u32[]{:S(2)}) %collective-permute-start.1) | collective-permute-done | bytes 262176 | tf_op jit(solution)/shard_map/sides/ppermute | solution.py:137
  44.9 1.6 %collective-permute-start.16 = (f32[128,256]{1,0:T(8,128)S(1)}, f32[128,256]{1,0:T(8,128)S(1)}, u32[]{:S(2)}, u32[]{:S(2)}) collective-permute-start(f32[128,256]{1,0:T(8,128)S(1)} %maximum_select_fusion), channel_id=1, source_target_pairs={{0,32},{16,48},{32,64},{48,80},{64,96},{80,112},{96,0},{112,16},{1... | collective-permute-start | bytes 393224 | tf_op jit(solution)/shard_map/queries/ppermute | solution.py:137
  46.6 2.9 %collective-permute-start.17 = (f32[128,256]{1,0:T(8,128)S(1)}, f32[128,256]{1,0:T(8,128)S(1)}, u32[]{:S(2)}, u32[]{:S(2)}) collective-permute-start(f32[128,256]{1,0:T(8,128)S(1)} %maximum_select_fusion), channel_id=1, source_target_pairs={{0,64},{16,80},{32,96},{48,112},{64,0},{80,16},{96,32},{112,48},{1... | collective-permute-start | bytes 393224 | tf_op jit(solution)/shard_map/queries/ppermute | solution.py:137
  49.5 1.3 %collective-permute-start.18 = (f32[128,256]{1,0:T(8,128)S(1)}, f32[128,256]{1,0:T(8,128)S(1)}, u32[]{:S(2)}, u32[]{:S(2)}) collective-permute-start(f32[128,256]{1,0:T(8,128)S(1)} %maximum_select_fusion), channel_id=1, source_target_pairs={{0,96},{16,112},{32,0},{48,16},{64,32},{80,48},{96,64},{112,80},{1... | collective-permute-start | bytes 393224 | tf_op jit(solution)/shard_map/queries/ppermute | solution.py:137
  50.8 1.7 %collective-permute-start.3 = (f32[128,128]{1,0:T(8,128)S(1)}, f32[128,128]{1,0:T(8,128)S(1)}, u32[]{:S(2)}, u32[]{:S(2)}) collective-permute-start(f32[128,128]{1,0:T(8,128)S(1)} %get-tuple-element.18), channel_id=1, source_target_pairs={{0,8},{1,9},{2,10},{3,11},{4,12},{5,13},{6,14},{7,15},{8,0},{9,1},... | collective-permute-start | bytes 196616 | tf_op jit(solution)/shard_map/sides/ppermute | solution.py:137
  52.6 1.6 %collective-permute-start.4 = (f32[128,128]{1,0:T(8,128)S(1)}, f32[128,128]{1,0:T(8,128)S(1)}, u32[]{:S(2)}, u32[]{:S(2)}) collective-permute-start(f32[128,128]{1,0:T(8,128)S(1)} %get-tuple-element.17), channel_id=1, source_target_pairs={{0,12},{1,13},{2,14},{3,15},{4,0},{5,1},{6,2},{7,3},{8,4},{9,5},{1... | collective-permute-start | bytes 196616 | tf_op jit(solution)/shard_map/sides/ppermute | solution.py:137
  54.2 2.4 %collective-permute-done.3.a2 = f32[128,128]{1,0:T(8,128)S(1)} collective-permute-done((f32[128,128]{1,0:T(8,128)S(1)}, f32[128,128]{1,0:T(8,128)S(1)}, u32[]{:S(2)}, u32[]{:S(2)}) %collective-permute-start.3) | collective-permute-done | bytes 65568 | tf_op jit(solution)/shard_map/sides/ppermute | solution.py:137
  56.6 1.3 %collective-permute-done.4.a3 = f32[128,128]{1,0:T(8,128)S(1)} collective-permute-done((f32[128,128]{1,0:T(8,128)S(1)}, f32[128,128]{1,0:T(8,128)S(1)}, u32[]{:S(2)}, u32[]{:S(2)}) %collective-permute-start.4) | collective-permute-done | bytes 65568 | tf_op jit(solution)/shard_map/sides/ppermute | solution.py:137
  58.5 1.9 %encode.1 = f32[8,8,64]{2,1,0:T(8,128)} custom-call(f32[128,128]{1,0:T(8,128)} %get-tuple-element.20.own0, f32[128,128]{1,0:T(8,128)} %copy-done.10, f32[128,128]{1,0:T(8,128)} %copy-done.11, f32[128,128]{1,0:T(8,128)} %copy-done.12, f32[128,128]{1,0:T(8,128)} %get-tuple-element.22.own1, f32[128,128]{1,0:T(8,128)} %copy-done.9), custom_call_target="tpu_custom_call" | custom-call | tf_op jit(solution)/shard_map/encode/encode/pallas_call | solution.py:95
  61.8 0.8 add.35
  63.8 3.1 %collective-permute-done.11.other = f32[4,8,64]{2,1,0:T(8,128)S(1)} collective-permute-done((f32[4,8,64]{2,1,0:T(8,128)S(1)}, f32[4,8,64]{2,1,0:T(8,128)S(1)}, u32[]{:S(2)}, u32[]{:S(2)}) %collective-permute-start.11) | collective-permute-done | bytes 8224 | tf_op jit(solution)/shard_map/encode/ppermute | solution.py:137
  67.0 2.5 %collective-permute-start.14 = (f32[2,8,64]{2,1,0:T(8,128)S(1)}, f32[2,8,64]{2,1,0:T(8,128)S(1)}, u32[]{:S(2)}, u32[]{:S(2)}) collective-permute-start(f32[2,8,64]{2,1,0:T(8,128)S(1)} %pad_maximum_fusion.3), channel_id=1, source_target_pairs={{0,12},{1,13},{2,14},{3,15},{4,0},{5,1},{6,2},{7,3},{8,4},{9,5},{1... | collective-permute-start | bytes 12296 | tf_op jit(solution)/shard_map/encode/ppermute | solution.py:137
  69.5 0.9 %collective-permute-start.13 = (f32[2,8,64]{2,1,0:T(8,128)S(1)}, f32[2,8,64]{2,1,0:T(8,128)S(1)}, u32[]{:S(2)}, u32[]{:S(2)}) collective-permute-start(f32[2,8,64]{2,1,0:T(8,128)S(1)} %pad_maximum_fusion.2), channel_id=1, source_target_pairs={{0,8},{1,9},{2,10},{3,11},{4,12},{5,13},{6,14},{7,15},{8,0},{9,1},... | collective-permute-start | bytes 12296 | tf_op jit(solution)/shard_map/encode/ppermute | solution.py:137
  70.9 3.8 %collective-permute-done.13.r2 = f32[2,8,64]{2,1,0:T(8,128)S(1)} collective-permute-done((f32[2,8,64]{2,1,0:T(8,128)S(1)}, f32[2,8,64]{2,1,0:T(8,128)S(1)}, u32[]{:S(2)}, u32[]{:S(2)}) %collective-permute-start.13) | collective-permute-done | bytes 4128 | tf_op jit(solution)/shard_map/encode/ppermute | solution.py:137
  75.9 2.9 %score.1 = f32[8,512]{1,0:T(8,128)} custom-call(f32[4,8,64]{2,1,0:T(8,128)} %get-tuple-element.27.own, f32[4,8,64]{2,1,0:T(8,128)} %copy-done.13, f32[2,8,64]{2,1,0:T(8,128)} %copy-done.16, f32[2,8,64]{2,1,0:T(8,128)} %copy-done.15, f32[2,8,64]{2,1,0:T(8,128)} %copy-done.14, f32[512,256]{1,0:T(8,128)} %copy-done.6, f32[512,256]{1,0:T(8,128)} %copy-done.7), custom_call_target="tpu_custom_call" | custom-call | tf_op jit(solution)/shard_map/scores/score/pallas_call | solution.py:127
  79.4 3.4 %collective-permute-done.20 = f32[8,512]{1,0:T(8,128)S(1)} collective-permute-done((f32[8,512]{1,0:T(8,128)}, f32[8,512]{1,0:T(8,128)S(1)}, u32[]{:S(2)}, u32[]{:S(2)}) %collective-permute-start.20) | collective-permute-done | bytes 16416 | tf_op jit(solution)/shard_map/scores/ppermute | solution.py:137
  83.4 1.4 %collective-permute-start.21 = (f32[8,512]{1,0:T(8,128)S(1)}, f32[8,512]{1,0:T(8,128)S(1)}, u32[]{:S(2)}, u32[]{:S(2)}) collective-permute-start(f32[8,512]{1,0:T(8,128)S(1)} %add.37), channel_id=1, source_target_pairs={{0,8},{1,9},{2,10},{3,11},{4,12},{5,13},{6,14},{7,15},{8,0},{9,1},... | collective-permute-start | bytes 49160 | tf_op jit(solution)/shard_map/scores/ppermute | solution.py:137
  84.8 3.2 %collective-permute-start.23 = (f32[8,512]{1,0:T(8,128)S(1)}, f32[8,512]{1,0:T(8,128)S(1)}, u32[]{:S(2)}, u32[]{:S(2)}) collective-permute-start(f32[8,512]{1,0:T(8,128)S(1)} %add.37), channel_id=1, source_target_pairs={{0,12},{1,13},{2,14},{3,15},{4,0},{5,1},{6,2},{7,3},{8,4},{9,5},{1... | collective-permute-start | bytes 49160 | tf_op jit(solution)/shard_map/scores/ppermute | solution.py:137
  88.7 1.1 %collective-permute-done.22 = f32[8,512]{1,0:T(8,128)S(1)} collective-permute-done((f32[8,512]{1,0:T(8,128)S(1)}, f32[8,512]{1,0:T(8,128)S(1)}, u32[]{:S(2)}, u32[]{:S(2)}) %collective-permute-start.22) | collective-permute-done | bytes 16416 | tf_op jit(solution)/shard_map/scores/ppermute | solution.py:137
  (71 shorter events, 10.1 us)
Async XLA Ops:
  8.7 5.5 %collective-permute-start.5 = (f32[8,128,128]{2,1,0:T(8,128)S(1)}, f32[8,128,128]{2,1,0:T(8,128)S(1)}, u32[]{:S(2)}, u32[]{:S(2)}) collective-permute-start(f32[8,128,128]{2,1,0:T(8,128)S(1)} %project_1_send.1), channel_id=1, source_target_pairs={{0,1},{1,0},{2,3},{3,2},{4,5},{5,4},{6,7},{7,6},{8,9},{9,8},{10,11... | collective-permute-start | bytes 1572872 | tf_op jit(solution)/shard_map/sides/ppermute | solution.py:137
  13.7 12.6 %copy-start.8 = (f32[64,256]{1,0:T(8,128)S(1)}, f32[64,256]{1,0:T(8,128)}, u32[]{:S(2)}) copy-start(f32[64,256]{1,0:T(8,128)} %param.9) | copy-start | bytes 196612
  13.7 15.6 %copy-start.3 = (bf16[1792,64]{0,1:T(8,128)(2,1)S(1)}, bf16[1792,64]{0,1:T(8,128)(2,1)}, u32[]{:S(2)}) copy-start(bf16[1792,64]{0,1:T(8,128)(2,1)} %param.7) | copy-start | bytes 688132
  13.7 15.6 %copy-start.5 = (bf16[512,64]{0,1:T(8,128)(2,1)S(1)}, bf16[512,64]{0,1:T(8,128)(2,1)}, u32[]{:S(2)}) copy-start(bf16[512,64]{0,1:T(8,128)(2,1)} %param.8) | copy-start | bytes 196612
  13.7 15.6 %collective-permute-start = (f32[8,128,128]{2,1,0:T(8,128)S(1)}, f32[8,128,128]{2,1,0:T(8,128)S(1)}, u32[]{:S(2)}, u32[]{:S(2)}) collective-permute-start(f32[8,128,128]{2,1,0:T(8,128)S(1)} %project_0_send.1), channel_id=1, source_target_pairs={{0,1},{1,0},{2,3},{3,2},{4,5},{5,4},{6,7},{7,6},{8,9},{9,8},{10,11... | collective-permute-start | bytes 1572872 | tf_op jit(solution)/shard_map/sides/ppermute | solution.py:137
  19.0 18.0 %collective-permute-start.6 = (f32[2,128,128]{2,1,0:T(8,128)S(1)}, f32[2,128,128]{2,1,0:T(8,128)S(1)}, u32[]{:S(2)}, u32[]{:S(2)}) collective-permute-start(f32[2,128,128]{2,1,0:T(8,128)S(1)} %get-tuple-element.14), channel_id=1, source_target_pairs={{0,8},{1,9},{2,10},{3,11},{4,12},{5,13},{6,14},{7,15},{8,0},{9,1},... | collective-permute-start | bytes 393224 | tf_op jit(solution)/shard_map/sides/ppermute | solution.py:137
  23.0 13.9 %collective-permute-start.7 = (f32[2,128,128]{2,1,0:T(8,128)S(1)}, f32[2,128,128]{2,1,0:T(8,128)S(1)}, u32[]{:S(2)}, u32[]{:S(2)}) collective-permute-start(f32[2,128,128]{2,1,0:T(8,128)S(1)} %get-tuple-element.15), channel_id=1, source_target_pairs={{0,4},{1,5},{2,6},{3,7},{4,8},{5,9},{6,10},{7,11},{8,12},{9,13},{1... | collective-permute-start | bytes 393224 | tf_op jit(solution)/shard_map/sides/ppermute | solution.py:137
  24.1 12.9 %collective-permute-start.8 = (f32[2,128,128]{2,1,0:T(8,128)S(1)}, f32[2,128,128]{2,1,0:T(8,128)S(1)}, u32[]{:S(2)}, u32[]{:S(2)}) collective-permute-start(f32[2,128,128]{2,1,0:T(8,128)S(1)} %get-tuple-element.16), channel_id=1, source_target_pairs={{0,12},{1,13},{2,14},{3,15},{4,0},{5,1},{6,2},{7,3},{8,4},{9,5},{1... | collective-permute-start | bytes 393224 | tf_op jit(solution)/shard_map/sides/ppermute | solution.py:137
  26.3 18.6 %collective-permute-start.15 = (f32[64,256]{1,0:T(8,128)S(1)}, f32[64,256]{1,0:T(8,128)S(1)}, u32[]{:S(2)}, u32[]{:S(2)}) collective-permute-start(f32[64,256]{1,0:T(8,128)S(1)} %copy-done.8), channel_id=1, source_target_pairs={{0,16},{16,0},{32,48},{48,32},{64,80},{80,64},{96,112},{112,96},{1... | collective-permute-start | bytes 196616 | tf_op jit(solution)/shard_map/queries/ppermute | solution.py:137
  36.3 7.9 %collective-permute-start.1 = (f32[4,128,128]{2,1,0:T(8,128)S(1)}, f32[4,128,128]{2,1,0:T(8,128)S(1)}, u32[]{:S(2)}, u32[]{:S(2)}) collective-permute-start(f32[4,128,128]{2,1,0:T(8,128)S(1)} %get-tuple-element.12), channel_id=1, source_target_pairs={{0,2},{1,3},{2,0},{3,1},{4,6},{5,7},{6,4},{7,5},{8,10},{9,11},{10,... | collective-permute-start | bytes 786440 | tf_op jit(solution)/shard_map/sides/ppermute | solution.py:137
  37.6 13.2 %collective-permute-start.9 = (f32[128,128]{1,0:T(8,128)S(1)}, f32[128,128]{1,0:T(8,128)S(1)}, u32[]{:S(2)}, u32[]{:S(2)}) collective-permute-start(f32[128,128]{1,0:T(8,128)S(1)} %get-tuple-element.21), channel_id=1, source_target_pairs={{0,2},{1,3},{2,0},{3,1},{4,6},{5,7},{6,4},{7,5},{8,10},{9,11},{10,... | collective-permute-start | bytes 196616 | tf_op jit(solution)/shard_map/sides/ppermute | solution.py:137
  44.9 7.7 %collective-permute-start.2 = (f32[128,128]{1,0:T(8,128)S(1)}, f32[128,128]{1,0:T(8,128)S(1)}, u32[]{:S(2)}, u32[]{:S(2)}) collective-permute-start(f32[128,128]{1,0:T(8,128)S(1)} %get-tuple-element.19), channel_id=1, source_target_pairs={{0,4},{1,5},{2,6},{3,7},{4,8},{5,9},{6,10},{7,11},{8,12},{9,13},{1... | collective-permute-start | bytes 196616 | tf_op jit(solution)/shard_map/sides/ppermute | solution.py:137
  44.9 15.5 %collective-permute-start.16 = (f32[128,256]{1,0:T(8,128)S(1)}, f32[128,256]{1,0:T(8,128)S(1)}, u32[]{:S(2)}, u32[]{:S(2)}) collective-permute-start(f32[128,256]{1,0:T(8,128)S(1)} %maximum_select_fusion), channel_id=1, source_target_pairs={{0,32},{16,48},{32,64},{48,80},{64,96},{80,112},{96,0},{112,16},{1... | collective-permute-start | bytes 393224 | tf_op jit(solution)/shard_map/queries/ppermute | solution.py:137
  46.6 13.9 %collective-permute-start.17 = (f32[128,256]{1,0:T(8,128)S(1)}, f32[128,256]{1,0:T(8,128)S(1)}, u32[]{:S(2)}, u32[]{:S(2)}) collective-permute-start(f32[128,256]{1,0:T(8,128)S(1)} %maximum_select_fusion), channel_id=1, source_target_pairs={{0,64},{16,80},{32,96},{48,112},{64,0},{80,16},{96,32},{112,48},{1... | collective-permute-start | bytes 393224 | tf_op jit(solution)/shard_map/queries/ppermute | solution.py:137
  49.5 11.0 %collective-permute-start.18 = (f32[128,256]{1,0:T(8,128)S(1)}, f32[128,256]{1,0:T(8,128)S(1)}, u32[]{:S(2)}, u32[]{:S(2)}) collective-permute-start(f32[128,256]{1,0:T(8,128)S(1)} %maximum_select_fusion), channel_id=1, source_target_pairs={{0,96},{16,112},{32,0},{48,16},{64,32},{80,48},{96,64},{112,80},{1... | collective-permute-start | bytes 393224 | tf_op jit(solution)/shard_map/queries/ppermute | solution.py:137
  50.8 7.0 %copy-start.9 = (f32[128,128]{1,0:T(8,128)}, f32[128,128]{1,0:T(8,128)S(1)}, u32[]{:S(2)}) copy-start(f32[128,128]{1,0:T(8,128)S(1)} %collective-permute-done.9.b1) | copy-start | bytes 196612
  50.8 5.8 %collective-permute-start.3 = (f32[128,128]{1,0:T(8,128)S(1)}, f32[128,128]{1,0:T(8,128)S(1)}, u32[]{:S(2)}, u32[]{:S(2)}) collective-permute-start(f32[128,128]{1,0:T(8,128)S(1)} %get-tuple-element.18), channel_id=1, source_target_pairs={{0,8},{1,9},{2,10},{3,11},{4,12},{5,13},{6,14},{7,15},{8,0},{9,1},... | collective-permute-start | bytes 196616 | tf_op jit(solution)/shard_map/sides/ppermute | solution.py:137
  52.6 5.3 %copy-start.10 = (f32[128,128]{1,0:T(8,128)}, f32[128,128]{1,0:T(8,128)S(1)}, u32[]{:S(2)}) copy-start(f32[128,128]{1,0:T(8,128)S(1)} %collective-permute-done.2.a1) | copy-start | bytes 196612
  52.6 5.3 %collective-permute-start.4 = (f32[128,128]{1,0:T(8,128)S(1)}, f32[128,128]{1,0:T(8,128)S(1)}, u32[]{:S(2)}, u32[]{:S(2)}) collective-permute-start(f32[128,128]{1,0:T(8,128)S(1)} %get-tuple-element.17), channel_id=1, source_target_pairs={{0,12},{1,13},{2,14},{3,15},{4,0},{5,1},{6,2},{7,3},{8,4},{9,5},{1... | collective-permute-start | bytes 196616 | tf_op jit(solution)/shard_map/sides/ppermute | solution.py:137
  60.4 1.4 %collective-permute-start.10 = (f32[8,8,64]{2,1,0:T(8,128)}, f32[8,8,64]{2,1,0:T(8,128)S(1)}, u32[]{:S(2)}, u32[]{:S(2)}) collective-permute-start(f32[8,8,64]{2,1,0:T(8,128)} %encode.1), channel_id=1, source_target_pairs={{0,1},{1,0},{2,3},{3,2},{4,5},{5,4},{6,7},{7,6},{8,9},{9,8},{10,11... | collective-permute-start | bytes 49160 | tf_op jit(solution)/shard_map/encode/ppermute | solution.py:137
  60.5 14.8 %copy-start.6 = (f32[512,256]{1,0:T(8,128)}, f32[512,256]{1,0:T(8,128)S(1)}, u32[]{:S(2)}) copy-start(f32[512,256]{1,0:T(8,128)S(1)} %pad_maximum_fusion.q_own) | copy-start | bytes 1572868
  60.5 10.0 %collective-permute-start.19 = (f32[512,256]{1,0:T(8,128)S(1)}, f32[512,256]{1,0:T(8,128)S(1)}, u32[]{:S(2)}, u32[]{:S(2)}) collective-permute-start(f32[512,256]{1,0:T(8,128)S(1)} %pad_maximum_fusion.q_own), channel_id=1, source_target_pairs={{0,1},{1,0},{2,3},{3,2},{4,5},{5,4},{6,7},{7,6},{8,9},{9,8},{10,11... | collective-permute-start | bytes 1572872 | tf_op jit(solution)/shard_map/queries/ppermute | solution.py:137
  63.2 3.7 %collective-permute-start.11 = (f32[4,8,64]{2,1,0:T(8,128)S(1)}, f32[4,8,64]{2,1,0:T(8,128)S(1)}, u32[]{:S(2)}, u32[]{:S(2)}) collective-permute-start(f32[4,8,64]{2,1,0:T(8,128)S(1)} %get-tuple-element.26), channel_id=1, source_target_pairs={{0,2},{1,3},{2,0},{3,1},{4,6},{5,7},{6,4},{7,5},{8,10},{9,11},{10,... | collective-permute-start | bytes 24584 | tf_op jit(solution)/shard_map/encode/ppermute | solution.py:137
  66.9 8.4 %copy-start.13 = (f32[4,8,64]{2,1,0:T(8,128)}, f32[4,8,64]{2,1,0:T(8,128)S(1)}, u32[]{:S(2)}) copy-start(f32[4,8,64]{2,1,0:T(8,128)S(1)} %collective-permute-done.11.other) | copy-start | bytes 24580
  67.0 3.9 %collective-permute-start.14 = (f32[2,8,64]{2,1,0:T(8,128)S(1)}, f32[2,8,64]{2,1,0:T(8,128)S(1)}, u32[]{:S(2)}, u32[]{:S(2)}) collective-permute-start(f32[2,8,64]{2,1,0:T(8,128)S(1)} %pad_maximum_fusion.3), channel_id=1, source_target_pairs={{0,12},{1,13},{2,14},{3,15},{4,0},{5,1},{6,2},{7,3},{8,4},{9,5},{1... | collective-permute-start | bytes 12296 | tf_op jit(solution)/shard_map/encode/ppermute | solution.py:137
  69.5 5.2 %collective-permute-start.13 = (f32[2,8,64]{2,1,0:T(8,128)S(1)}, f32[2,8,64]{2,1,0:T(8,128)S(1)}, u32[]{:S(2)}, u32[]{:S(2)}) collective-permute-start(f32[2,8,64]{2,1,0:T(8,128)S(1)} %pad_maximum_fusion.2), channel_id=1, source_target_pairs={{0,8},{1,9},{2,10},{3,11},{4,12},{5,13},{6,14},{7,15},{8,0},{9,1},... | collective-permute-start | bytes 12296 | tf_op jit(solution)/shard_map/encode/ppermute | solution.py:137
  70.4 4.9 %collective-permute-start.12 = (f32[2,8,64]{2,1,0:T(8,128)S(1)}, f32[2,8,64]{2,1,0:T(8,128)S(1)}, u32[]{:S(2)}, u32[]{:S(2)}) collective-permute-start(f32[2,8,64]{2,1,0:T(8,128)S(1)} %pad_maximum_fusion.1), channel_id=1, source_target_pairs={{0,4},{1,5},{2,6},{3,7},{4,8},{5,9},{6,10},{7,11},{8,12},{9,13},{1... | collective-permute-start | bytes 12296 | tf_op jit(solution)/shard_map/encode/ppermute | solution.py:137
  70.5 4.8 %copy-start.7 = (f32[512,256]{1,0:T(8,128)}, f32[512,256]{1,0:T(8,128)S(1)}, u32[]{:S(2)}) copy-start(f32[512,256]{1,0:T(8,128)S(1)} %collective-permute-done.19.q_other) | copy-start | bytes 1572868
  78.8 3.9 %collective-permute-start.20 = (f32[8,512]{1,0:T(8,128)}, f32[8,512]{1,0:T(8,128)S(1)}, u32[]{:S(2)}, u32[]{:S(2)}) collective-permute-start(f32[8,512]{1,0:T(8,128)} %score.1), channel_id=1, source_target_pairs={{0,2},{1,3},{2,0},{3,1},{4,6},{5,7},{6,4},{7,5},{8,10},{9,11},{10,... | collective-permute-start | bytes 49160 | tf_op jit(solution)/shard_map/scores/ppermute | solution.py:137
  83.4 5.2 %collective-permute-start.21 = (f32[8,512]{1,0:T(8,128)S(1)}, f32[8,512]{1,0:T(8,128)S(1)}, u32[]{:S(2)}, u32[]{:S(2)}) collective-permute-start(f32[8,512]{1,0:T(8,128)S(1)} %add.37), channel_id=1, source_target_pairs={{0,8},{1,9},{2,10},{3,11},{4,12},{5,13},{6,14},{7,15},{8,0},{9,1},... | collective-permute-start | bytes 49160 | tf_op jit(solution)/shard_map/scores/ppermute | solution.py:137
  84.8 4.9 %collective-permute-start.22 = (f32[8,512]{1,0:T(8,128)S(1)}, f32[8,512]{1,0:T(8,128)S(1)}, u32[]{:S(2)}, u32[]{:S(2)}) collective-permute-start(f32[8,512]{1,0:T(8,128)S(1)} %add.37), channel_id=1, source_target_pairs={{0,4},{1,5},{2,6},{3,7},{4,8},{5,9},{6,10},{7,11},{8,12},{9,13},{1... | collective-permute-start | bytes 49160 | tf_op jit(solution)/shard_map/scores/ppermute | solution.py:137
  84.8 4.9 %collective-permute-start.23 = (f32[8,512]{1,0:T(8,128)S(1)}, f32[8,512]{1,0:T(8,128)S(1)}, u32[]{:S(2)}, u32[]{:S(2)}) collective-permute-start(f32[8,512]{1,0:T(8,128)S(1)} %add.37), channel_id=1, source_target_pairs={{0,12},{1,13},{2,14},{3,15},{4,0},{5,1},{6,2},{7,3},{8,4},{9,5},{1... | collective-permute-start | bytes 49160 | tf_op jit(solution)/shard_map/scores/ppermute | solution.py:137
  (9 other events, 13.8 us)

commit v2 on v0

v2 whole, which is shorter than its diff:
```python
import functools

import jax
import jax.numpy as jnp
from jax import lax
from jax.experimental import pallas as pl
from jax.experimental.pallas import tpu as pltpu
from jax.sharding import PartitionSpec as P

NT = (((1,), (1,)), ((), ()))
CHIPS = [[c + 2 * chip for chip in range(8)] for c in range(2)]


def project_kernel(mine, acts, grads, pin, pout, *rest):
    if mine:
        out, held_a, held_g, held_pin, held_pout, sem, p_sem = rest
    else:
        passed, out, passed_out, held_a, held_g, held_pin, held_pout, sem, p_sem = rest
    examples, rank, rows = out.shape[0], out.shape[1] // 2, out.shape[2]
    core = lax.axis_index("tensor") % 2
    part = core if mine else 1 - core
    copies = [
        pltpu.make_async_copy(pout, held_pout, p_sem.at[0]),
        pltpu.make_async_copy(pin, held_pin, p_sem.at[1]),
    ]
    for e in range(examples):
        for k in range(2):
            here = pl.ds(pl.multiple_of(part * rows + k * (rows // 2), rows // 2), rows // 2)
            to = pl.ds(e * rows + k * (rows // 2), rows // 2)
            copies.append(pltpu.make_async_copy(grads.at[e, here, :], held_g.at[to, :], sem.at[0, e, k]))
            copies.append(pltpu.make_async_copy(acts.at[e, here, :], held_a.at[to, :], sem.at[1, e, k]))
    for copy in copies:
        copy.start()
    if not mine:
        passed_out[...] = passed[...]
    for copy in copies[:2]:
        copy.wait()
    for e in range(0, examples, 2):
        for copy in copies[2 + 4 * e : 10 + 4 * e]:
            copy.wait()
        block = pl.ds(e * rows, 2 * rows)
        so = lax.dot_general(held_pout[...], held_g[block, :], NT, preferred_element_type=jnp.float32)
        si = lax.dot_general(held_pin[...], held_a[block, :], NT, preferred_element_type=jnp.float32)
        for k in range(2):
            out[e + k, :rank, :] = so[:, k * rows : (k + 1) * rows]
            out[e + k, rank:, :] = si[:, k * rows : (k + 1) * rows]


def project(mine, acts, grads, pin, pout, *passed):
    examples, length, width_in = acts.shape
    rows = length // 2
    hbm = pl.BlockSpec(memory_space=pl.ANY)
    vmem = pl.BlockSpec(memory_space=pltpu.VMEM)
    return pl.pallas_call(
        functools.partial(project_kernel, mine),
        out_shape=[
            jax.ShapeDtypeStruct((examples, 2 * pin.shape[0], rows), jnp.float32),
            *(jax.ShapeDtypeStruct(p.shape, p.dtype) for p in passed),
        ],
        in_specs=[hbm] * 4 + [vmem] * len(passed),
        out_specs=[vmem] * (1 + len(passed)),
        scratch_shapes=[
            pltpu.VMEM((examples * rows, width_in), acts.dtype),
            pltpu.VMEM((examples * rows, grads.shape[2]), grads.dtype),
            pltpu.VMEM(pin.shape, pin.dtype),
            pltpu.VMEM(pout.shape, pout.dtype),
            pltpu.SemaphoreType.DMA((2, examples, 2)),
            pltpu.SemaphoreType.DMA((2,)),
        ],
        compiler_params=pltpu.CompilerParams(vmem_limit_bytes=51 << 20),
        name="project_own" if mine else "project_other",
    )(acts, grads, pin, pout, *passed)


def merge_kernel(own, got, queries, beside, total, pair):
    total[...] = own[...] + got[...]
    n = queries.shape[0]
    x_hi = lax.axis_index("dp") % 2
    pair[pl.ds(pl.multiple_of(x_hi * n, n), n), :] = queries[...]
    pair[pl.ds(pl.multiple_of((1 - x_hi) * n, n), n), :] = beside[...]


def merge(own, got, queries, beside):
    n, k = queries.shape
    vmem = pl.BlockSpec(memory_space=pltpu.VMEM)
    return pl.pallas_call(
        merge_kernel,
        out_shape=[
            jax.ShapeDtypeStruct(own.shape, jnp.float32),
            jax.ShapeDtypeStruct((2 * n, k), jnp.float32),
        ],
        in_specs=[vmem] * 4,
        out_specs=[vmem] * 2,
        compiler_params=pltpu.CompilerParams(vmem_limit_bytes=16 << 20),
        name="merge",
    )(own, got, queries, beside)


def encode_kernel(sides, out):
    total = ((sides[0] + sides[1]) + (sides[2] + sides[3])) + ((sides[4] + sides[5]) + (sides[6] + sides[7]))
    rank = total.shape[0] // 2
    enc = lax.dot_general(
        total[:rank], total[rank:], NT, precision=lax.Precision.HIGHEST, preferred_element_type=jnp.float32
    )
    take = rank // out.shape[0]
    out[...] = jnp.zeros_like(out)
    for t in range(out.shape[0]):
        out[t, :take, :rank] = enc[take * t : take * (t + 1), :]


def encode(sides):
    return pl.pallas_call(
        encode_kernel,
        out_shape=jax.ShapeDtypeStruct((16, 8, 128), jnp.float32),
        in_specs=[pl.BlockSpec(memory_space=pltpu.VMEM)],
        out_specs=pl.BlockSpec(memory_space=pltpu.VMEM),
        compiler_params=pltpu.CompilerParams(vmem_limit_bytes=8 << 20),
        name="encode",
    )(sides)


def score_kernel(scale, slices, q0, q1, q2, q3, out, tiles):
    y = lax.axis_index("dp") // 2
    for e in range(8):
        tiles[pl.ds(8 * e, 8), :] = slices[2 * e] + slices[2 * e + 1]
    enc = jnp.concatenate([tiles[pl.ds(i, 8, stride=8), :][:, :64] for i in range(4)], axis=1) * scale
    for dy, queries in enumerate((q0, q1, q2, q3)):
        part = lax.dot_general(
            enc, queries[...], NT, precision=lax.Precision.HIGHEST, preferred_element_type=jnp.float32
        )
        columns = pl.ds(pl.multiple_of((y - dy + 4) % 4 * 128, 128), 128)
        for t in range(out.shape[0]):
            out[t, :, columns] = part


def score(scale, slices, *queries):
    return pl.pallas_call(
        functools.partial(score_kernel, scale),
        out_shape=jax.ShapeDtypeStruct((16, 8, 4 * queries[0].shape[0]), jnp.float32),
        in_specs=[pl.BlockSpec(memory_space=pltpu.VMEM)] * 5,
        out_specs=pl.BlockSpec(memory_space=pltpu.VMEM),
        scratch_shapes=[pltpu.VMEM((64, 128), jnp.float32)],
        compiler_params=pltpu.CompilerParams(vmem_limit_bytes=8 << 20),
        name="score",
    )(slices, *queries)


def per_device(acts, grads, proj_in, proj_out, queries):
    length = acts.shape[1]
    rank = proj_in.shape[1]
    pin, pout = proj_in.T, proj_out.T

    with jax.named_scope("sides"):
        other, queries = project(False, acts, grads, pin, pout, queries)
        beside = lax.ppermute(queries, "dp", [(d, d ^ 1) for d in range(8)])
        got = lax.ppermute(other, "tensor", [(t, t ^ 1) for t in range(16)])
        (own,) = project(True, acts, grads, pin, pout)
        total, pair = merge(own, got, queries, beside)
        sides = lax.all_to_all(total, "tensor", 0, 0, tiled=True, axis_index_groups=CHIPS)

    with jax.named_scope("queries"):
        wide = [pair] + [
            lax.ppermute(pair, "dp", [(d, (d + 2 * dy) % 8) for d in range(8)]) for dy in (1, 2, 3)
        ]

    with jax.named_scope("encode"):
        slices = lax.all_to_all(encode(sides), "tensor", 0, 0, tiled=True)

    with jax.named_scope("scores"):
        parts = lax.all_to_all(
            score(length ** (-0.5) / rank, slices, *wide), "tensor", 0, 0, tiled=True
        )
        return jnp.sum(parts, axis=0)


def solution(mesh):
    in_specs = (
        P("dp", None, "tensor"),
        P("dp", None, "tensor"),
        P("tensor", None),
        P("tensor", None),
        P("dp", "tensor"),
    )
    out_specs = P("dp", None)
    return jax.shard_map(
        per_device, mesh=mesh, in_specs=in_specs, out_specs=out_specs, check_vma=False
    )
```

time: 298 us -> 62.7 us (0.21)
  waiting for transfers between devices: 257 us -> 17.5 us
  matrix products: 25.6 us -> 0 us
  starting transfers between devices: 0.08 us -> 16.7 us
  Pallas kernels: 0 us -> 13.7 us
  between operations: 13.1 us -> 0.08 us
  blocking collectives: 0 us -> 10.7 us
    psum x1 -> x0, waiting for transfers between devices: 128 us -> none  [per_device(): side_in, side_out = lax.psum((partial_in, partial_out), 'tensor')]
    all_gather x2 -> x0, waiting for transfers between devices: 128 us -> none  [the longest x1 106 us: per_device(): lax.all_gather(wide_queries, 'dp', axis=0, tiled=True)]
    dot_general x4 -> x0, matrix products: 25.6 us -> none  [the longest x1 9.8 us: add_block(): jnp.einsum('ek,qk->eq', encoded, piece, precision=lax.Precision.HIGHEST)]
    all_to_all x0 -> x2, waiting for transfers between devices: none -> 17.5 us  [the longest x1 11.4 us: per_device(): lax.all_to_all(total, 'tensor', 0, 0, tiled=True, axis_index_groups=CHIPS)]
    pallas_call x0 -> x5, Pallas kernels: none -> 13.7 us  [the longest x2 11.2 us: project(): pl.pallas_call(functools.partial(project_kernel, mine), out_shape=[jax.Sh...]
    all_to_all x0 -> x1, blocking collectives: none -> 10.7 us  [per_device(): lax.all_to_all(score(length ** (-0.5) / rank, slices, *wide), 'tensor', 0...]
    all_to_all x0 -> x2, starting transfers between devices: none -> 8.84 us  [the longest x1 5.35 us: per_device(): lax.all_to_all(total, 'tensor', 0, 0, tiled=True, axis_index_groups=CHIPS)]
    ppermute x0 -> x5, starting transfers between devices: none -> 7.9 us  [the longest x3 4.63 us: per_device(): lax.ppermute(pair, 'dp', [(d, (d + 2 * dy) % 8) for d in range(8)])]
  transfers between devices with their start and end apart: 3 -> 7, of which waited for: 3 -> 2; matrix products, arithmetic and copies ran while one was open for 6% -> 0% of each run, Pallas kernels for 0% -> 10%
where the time goes in v2:
time: 62.7 us; the launch traced here: 61.9 us
  waiting for transfers between devices  17.5 us (28%)
  starting transfers between devices  16.7 us (27%)
  Pallas kernels  13.7 us (22%)
  blocking collectives  10.7 us (17%)
  local copies, waits for them, and re-layouts  2.62 us (4%)
  other arithmetic  0.63 us (1%)
    all_to_all x1, waiting for transfers between devices, per_device(): lax.all_to_all(total, 'tensor', 0, 0, tiled=True, axis_index_groups=CHIPS)  11.4 us
    pallas_call x2, Pallas kernels, project(): pl.pallas_call(functools.partial(project_kernel, mine), out_shape=[jax.Sh...  11.2 us
    all_to_all x1, blocking collectives, per_device(): lax.all_to_all(score(length ** (-0.5) / rank, slices, *wide), 'tensor', 0...  10.7 us
    all_to_all x1, waiting for transfers between devices, per_device(): slices = lax.all_to_all(encode(sides), 'tensor', 0, 0, tiled=True)  6.07 us
    all_to_all x1, starting transfers between devices, per_device(): lax.all_to_all(total, 'tensor', 0, 0, tiled=True, axis_index_groups=CHIPS)  5.35 us
    ppermute x3, starting transfers between devices, per_device(): lax.ppermute(pair, 'dp', [(d, (d + 2 * dy) % 8) for d in range(8)])  4.63 us
    all_to_all x1, starting transfers between devices, per_device(): slices = lax.all_to_all(encode(sides), 'tensor', 0, 0, tiled=True)  3.49 us
    ppermute x1, starting transfers between devices, per_device(): beside = lax.ppermute(queries, 'dp', [(d, d ^ 1) for d in range(8)])  3.19 us
  transfers between devices with their start and end apart: 7, of which 2 were waited for; matrix products, arithmetic and copies ran while one was open for 0% of the time, Pallas kernels for 10%

profile of v2, /device:TPU:0, one launch (start us, length us, event | category | flops | bytes accessed | tf_op | source)
XLA Modules:
  0.0 61.9 jit_solution(10198652111247835825)
XLA Ops:
  0.0 0.0 copy-start
  0.0 0.9 %copy-done = bf16[1792,64]{0,1:T(8,128)(2,1)S(1)} copy-done((bf16[1792,64]{0,1:T(8,128)(2,1)S(1)}, bf16[1792,64]{0,1:T(8,128)(2,1)}, u32[]{:S(2)}) %copy-start) | copy-done | bytes 229400
  0.9 0.0 copy-start.1
  0.9 0.8 %copy-done.1 = bf16[512,64]{0,1:T(8,128)(2,1)S(1)} copy-done((bf16[512,64]{0,1:T(8,128)(2,1)S(1)}, bf16[512,64]{0,1:T(8,128)(2,1)}, u32[]{:S(2)}) %copy-start.1) | copy-done | bytes 65560
  1.8 0.0 copy-start.2
  1.8 0.8 %copy-done.2 = f32[64,256]{1,0:T(8,128)S(1)} copy-done((f32[64,256]{1,0:T(8,128)S(1)}, f32[64,256]{1,0:T(8,128)}, u32[]{:S(2)}) %copy-start.2) | copy-done | bytes 65560
  2.6 5.6 %project_other.1 = (f32[8,128,256]{2,1,0:T(8,128)S(1)}, f32[64,256]{1,0:T(8,128)S(1)}) custom-call(bf16[8,512,1792]{2,1,0:T(8,128)(2,1)} %acts.3, bf16[8,512,512]{2,1,0:T(8,128)(2,1)} %grads.3, bf16[64,1792]{1,0:T(8,128)(2,1)S(1)} %bitcast.2, bf16[64,512]{1,0:T(8,128)(2,1)S(1)} %bitcast.4, f32[64,256]{1,0:T(8,128)S(1)} %copy-done.2), custom_call_target="tpu_custom_call" | custom-call | tf_op jit(solution)/shard_map/sides/project_other/pallas_call | solution.py:54
  8.2 0.1 collective-permute-start
  8.3 3.2 %collective-permute-start.1 = (f32[64,256]{1,0:T(8,128)S(1)}, f32[64,256]{1,0:T(8,128)S(1)}, u32[]{:S(2)}, u32[]{:S(2)}) collective-permute-start(f32[64,256]{1,0:T(8,128)S(1)} %get-tuple-element.10.queries), channel_id=1, source_target_pairs={{0,16},{16,0},{32,48},{48,32},{64,80},{80,64},{96,112},{112,96},{1... | collective-permute-start | bytes 196616 | tf_op jit(solution)/shard_map/sides/ppermute | solution.py:155
  11.5 5.6 %project_own.1.own = f32[8,128,256]{2,1,0:T(8,128)S(1)} custom-call(bf16[8,512,1792]{2,1,0:T(8,128)(2,1)} %acts.3, bf16[8,512,512]{2,1,0:T(8,128)(2,1)} %grads.3, bf16[64,1792]{1,0:T(8,128)(2,1)S(1)} %bitcast.3, bf16[64,512]{1,0:T(8,128)(2,1)S(1)} %bitcast.5), custom_call_target="tpu_custom_call" | custom-call | tf_op jit(solution)/shard_map/sides/project_own/pallas_call | solution.py:54
  17.1 0.0 collective-permute-done.1.beside
  17.1 0.0 collective-permute-done.got
  17.1 1.1 %merge.1 = (f32[8,128,256]{2,1,0:T(8,128)}, f32[128,256]{1,0:T(8,128)S(1)}) custom-call(f32[8,128,256]{2,1,0:T(8,128)S(1)} %project_own.1.own, f32[8,128,256]{2,1,0:T(8,128)S(1)} %collective-permute-done.got, f32[64,256]{1,0:T(8,128)S(1)} %get-tuple-element.10.queries, f32[64,256]{1,0:T(8,128)S(1)} %collective-permute-done.1.beside), custom_call_target="tpu_custom_call" | custom-call | tf_op jit(solution)/shard_map/sides/merge/pallas_call | solution.py:86
  18.2 5.4 %all-to-all-start = ((f32[8,128,256]{2,1,0:T(8,128)}), f32[8,128,256]{2,1,0:T(8,128)S(1)}, u32[]{:S(2)}, u32[]{:S(2)}) async-start(f32[8,128,256]{2,1,0:T(8,128)} %get-tuple-element.11), calls=%async_computation | async-start | bytes 2097152 | tf_op jit(solution)/shard_map/sides/all_to_all | solution.py:159
  23.6 3.0 %collective-permute-start.4 = (f32[128,256]{1,0:T(8,128)S(1)}, f32[128,256]{1,0:T(8,128)S(1)}, u32[]{:S(2)}, u32[]{:S(2)}) collective-permute-start(f32[128,256]{1,0:T(8,128)S(1)} %get-tuple-element.12.q0), channel_id=1, source_target_pairs={{0,96},{16,112},{32,0},{48,16},{64,32},{80,48},{96,64},{112,80},{1... | collective-permute-start | bytes 393224 | tf_op jit(solution)/shard_map/queries/ppermute | solution.py:163
  26.6 0.6 %collective-permute-start.3 = (f32[128,256]{1,0:T(8,128)S(1)}, f32[128,256]{1,0:T(8,128)S(1)}, u32[]{:S(2)}, u32[]{:S(2)}) collective-permute-start(f32[128,256]{1,0:T(8,128)S(1)} %get-tuple-element.12.q0), channel_id=1, source_target_pairs={{0,64},{16,80},{32,96},{48,112},{64,0},{80,16},{96,32},{112,48},{1... | collective-permute-start | bytes 393224 | tf_op jit(solution)/shard_map/queries/ppermute | solution.py:163
  27.2 1.0 %collective-permute-start.2 = (f32[128,256]{1,0:T(8,128)S(1)}, f32[128,256]{1,0:T(8,128)S(1)}, u32[]{:S(2)}, u32[]{:S(2)}) collective-permute-start(f32[128,256]{1,0:T(8,128)S(1)} %get-tuple-element.12.q0), channel_id=1, source_target_pairs={{0,32},{16,48},{32,64},{48,80},{64,96},{80,112},{96,0},{112,16},{1... | collective-permute-start | bytes 393224 | tf_op jit(solution)/shard_map/queries/ppermute | solution.py:163
  28.2 11.4 %all-to-all-done.sides = f32[8,128,256]{2,1,0:T(8,128)S(1)} async-done(((f32[8,128,256]{2,1,0:T(8,128)}), f32[8,128,256]{2,1,0:T(8,128)S(1)}, u32[]{:S(2)}, u32[]{:S(2)}) %all-to-all-start) | async-done | bytes 1048608 | tf_op jit(solution)/shard_map/sides/all_to_all | solution.py:159
  39.6 0.8 %encode.1 = f32[16,8,128]{2,1,0:T(8,128)} custom-call(f32[8,128,256]{2,1,0:T(8,128)S(1)} %all-to-all-done.sides), custom_call_target="tpu_custom_call" | custom-call | tf_op jit(solution)/shard_map/encode/encode/pallas_call | solution.py:112
  40.5 3.5 %all-to-all-start.1 = ((f32[16,8,128]{2,1,0:T(8,128)}), f32[16,8,128]{2,1,0:T(8,128)S(1)}, u32[]{:S(2)}, u32[]{:S(2)}) async-start(f32[16,8,128]{2,1,0:T(8,128)} %encode.1), calls=%async_computation.1 | async-start | bytes 131072 | tf_op jit(solution)/shard_map/encode/all_to_all | solution.py:167
  44.0 0.0 collective-permute-done.4.q3
  44.0 0.0 collective-permute-done.3.q2
  44.0 0.0 collective-permute-done.2.q1
  44.0 6.1 %all-to-all-done.1.slices = f32[16,8,128]{2,1,0:T(8,128)S(1)} async-done(((f32[16,8,128]{2,1,0:T(8,128)}), f32[16,8,128]{2,1,0:T(8,128)S(1)}, u32[]{:S(2)}, u32[]{:S(2)}) %all-to-all-start.1) | async-done | bytes 65568 | tf_op jit(solution)/shard_map/encode/all_to_all | solution.py:167
  50.1 0.6 score.1
  50.6 10.7 %all_to_all.15 = f32[16,8,512]{2,1,0:T(8,128)S(1)} all-to-all(f32[16,8,512]{2,1,0:T(8,128)S(1)} %score.1), channel_id=1, replica_groups=mesh['dp'=8,'tensor'=16] {'tensor'}, dimensions={0} | all-to-all | bytes 524288 | tf_op jit(solution)/shard_map/scores/all_to_all | solution.py:170
  61.3 0.6 %reduce_sum.9 = f32[8,512]{1,0:T(8,128)} reduce(f32[16,8,512]{2,1,0:T(8,128)S(1)} %all_to_all.15, f32[]{:T(128)} %constant.0.clone.1), dimensions={0}, to_apply=%region_0.0 | reduce | flops 61440 | bytes 278532 | tf_op jit(solution)/shard_map/scores/reduce_sum | solution.py:173
Async XLA Ops:
  0.0 0.9 %copy-start = (bf16[1792,64]{0,1:T(8,128)(2,1)S(1)}, bf16[1792,64]{0,1:T(8,128)(2,1)}, u32[]{:S(2)}) copy-start(bf16[1792,64]{0,1:T(8,128)(2,1)} %param.7) | copy-start | bytes 688132
  0.9 0.8 %copy-start.1 = (bf16[512,64]{0,1:T(8,128)(2,1)S(1)}, bf16[512,64]{0,1:T(8,128)(2,1)}, u32[]{:S(2)}) copy-start(bf16[512,64]{0,1:T(8,128)(2,1)} %param.8) | copy-start | bytes 196612
  1.8 0.8 %copy-start.2 = (f32[64,256]{1,0:T(8,128)S(1)}, f32[64,256]{1,0:T(8,128)}, u32[]{:S(2)}) copy-start(f32[64,256]{1,0:T(8,128)} %rest_0_.1) | copy-start | bytes 196612
  8.2 8.9 %collective-permute-start = (f32[8,128,256]{2,1,0:T(8,128)S(1)}, f32[8,128,256]{2,1,0:T(8,128)S(1)}, u32[]{:S(2)}, u32[]{:S(2)}) collective-permute-start(f32[8,128,256]{2,1,0:T(8,128)S(1)} %get-tuple-element.9), channel_id=1, source_target_pairs={{0,1},{1,0},{2,3},{3,2},{4,5},{5,4},{6,7},{7,6},{8,9},{9,8},{10,11... | collective-permute-start | bytes 3145736 | tf_op jit(solution)/shard_map/sides/ppermute | solution.py:156
  8.3 8.8 %collective-permute-start.1 = (f32[64,256]{1,0:T(8,128)S(1)}, f32[64,256]{1,0:T(8,128)S(1)}, u32[]{:S(2)}, u32[]{:S(2)}) collective-permute-start(f32[64,256]{1,0:T(8,128)S(1)} %get-tuple-element.10.queries), channel_id=1, source_target_pairs={{0,16},{16,0},{32,48},{48,32},{64,80},{80,64},{96,112},{112,96},{1... | collective-permute-start | bytes 196616 | tf_op jit(solution)/shard_map/sides/ppermute | solution.py:155
  18.2 21.4 %all-to-all-start = ((f32[8,128,256]{2,1,0:T(8,128)}), f32[8,128,256]{2,1,0:T(8,128)S(1)}, u32[]{:S(2)}, u32[]{:S(2)}) async-start(f32[8,128,256]{2,1,0:T(8,128)} %get-tuple-element.11), calls=%async_computation | async-start | bytes 2097152 | tf_op jit(solution)/shard_map/sides/all_to_all | solution.py:159
  23.6 20.4 %collective-permute-start.4 = (f32[128,256]{1,0:T(8,128)S(1)}, f32[128,256]{1,0:T(8,128)S(1)}, u32[]{:S(2)}, u32[]{:S(2)}) collective-permute-start(f32[128,256]{1,0:T(8,128)S(1)} %get-tuple-element.12.q0), channel_id=1, source_target_pairs={{0,96},{16,112},{32,0},{48,16},{64,32},{80,48},{96,64},{112,80},{1... | collective-permute-start | bytes 393224 | tf_op jit(solution)/shard_map/queries/ppermute | solution.py:163
  26.6 17.4 %collective-permute-start.3 = (f32[128,256]{1,0:T(8,128)S(1)}, f32[128,256]{1,0:T(8,128)S(1)}, u32[]{:S(2)}, u32[]{:S(2)}) collective-permute-start(f32[128,256]{1,0:T(8,128)S(1)} %get-tuple-element.12.q0), channel_id=1, source_target_pairs={{0,64},{16,80},{32,96},{48,112},{64,0},{80,16},{96,32},{112,48},{1... | collective-permute-start | bytes 393224 | tf_op jit(solution)/shard_map/queries/ppermute | solution.py:163
  27.2 16.8 %collective-permute-start.2 = (f32[128,256]{1,0:T(8,128)S(1)}, f32[128,256]{1,0:T(8,128)S(1)}, u32[]{:S(2)}, u32[]{:S(2)}) collective-permute-start(f32[128,256]{1,0:T(8,128)S(1)} %get-tuple-element.12.q0), channel_id=1, source_target_pairs={{0,32},{16,48},{32,64},{48,80},{64,96},{80,112},{96,0},{112,16},{1... | collective-permute-start | bytes 393224 | tf_op jit(solution)/shard_map/queries/ppermute | solution.py:163
  40.5 9.6 %all-to-all-start.1 = ((f32[16,8,128]{2,1,0:T(8,128)}), f32[16,8,128]{2,1,0:T(8,128)S(1)}, u32[]{:S(2)}, u32[]{:S(2)}) async-start(f32[16,8,128]{2,1,0:T(8,128)} %encode.1), calls=%async_computation.1 | async-start | bytes 131072 | tf_op jit(solution)/shard_map/encode/all_to_all | solution.py:167

commit v3 on v2

v3 whole, which is shorter than its diff:
```python
import functools

import jax
import jax.numpy as jnp
from jax import lax
from jax.experimental import pallas as pl
from jax.experimental.pallas import tpu as pltpu
from jax.sharding import PartitionSpec as P

NT = (((1,), (1,)), ((), ()))
CHIPS = [[c + 2 * chip for chip in range(8)] for c in range(2)]
HBM = pl.BlockSpec(memory_space=pltpu.HBM)
VMEM = pl.BlockSpec(memory_space=pltpu.VMEM)


def in_hbm(value):
    return pltpu.with_memory_space_constraint(value, pltpu.HBM)


def limit(mib):
    return pltpu.CompilerParams(vmem_limit_bytes=mib << 20)


def shape(*dims):
    return jax.ShapeDtypeStruct(dims, jnp.float32)


def project_kernel(mine, acts, grads, pin, pout, *rest):
    if mine:
        out, held_a, held_g, held_pin, held_pout, sem, p_sem = rest
    else:
        queries, out, passed, held_a, held_g, held_pin, held_pout, sem, p_sem = rest
    examples, rank, rows = out.shape[0], out.shape[1] // 2, out.shape[2]
    core = lax.axis_index("tensor") % 2
    part = core if mine else 1 - core
    weights = [
        pltpu.make_async_copy(pout, held_pout, p_sem.at[0]),
        pltpu.make_async_copy(pin, held_pin, p_sem.at[1]),
    ]
    blocks = []
    for e in range(examples):
        for k in range(2):
            here = pl.ds(pl.multiple_of(part * rows + k * (rows // 2), rows // 2), rows // 2)
            to = pl.ds(e * rows + k * (rows // 2), rows // 2)
            blocks.append(pltpu.make_async_copy(grads.at[e, here, :], held_g.at[to, :], sem.at[0, e, k]))
            blocks.append(pltpu.make_async_copy(acts.at[e, here, :], held_a.at[to, :], sem.at[1, e, k]))
    for copy in weights + blocks[:8]:
        copy.start()
    for copy in weights:
        copy.wait()
    if not mine:
        across = pltpu.make_async_copy(queries, passed, p_sem.at[2])
        blocks.append(across)
    for copy in blocks[8:]:
        copy.start()
    for e in range(0, examples, 2):
        for copy in blocks[4 * e : 8 + 4 * e]:
            copy.wait()
        block = pl.ds(e * rows, 2 * rows)
        so = lax.dot_general(held_pout[...], held_g[block, :], NT, preferred_element_type=jnp.float32)
        si = lax.dot_general(held_pin[...], held_a[block, :], NT, preferred_element_type=jnp.float32)
        for k in range(2):
            out[e + k, :rank, :] = so[:, k * rows : (k + 1) * rows]
            out[e + k, rank:, :] = si[:, k * rows : (k + 1) * rows]
    if not mine:
        across.wait()


def project(mine, acts, grads, pin, pout, *passed):
    examples, length, width_in = acts.shape
    rows = length // 2
    return pl.pallas_call(
        functools.partial(project_kernel, mine),
        out_shape=[shape(examples, 2 * pin.shape[0], rows)] + [shape(*p.shape) for p in passed],
        in_specs=[HBM] * (4 + len(passed)),
        out_specs=[VMEM] * (1 + len(passed)),
        scratch_shapes=[
            pltpu.VMEM((examples * rows, width_in), acts.dtype),
            pltpu.VMEM((examples * rows, grads.shape[2]), grads.dtype),
            pltpu.VMEM(pin.shape, pin.dtype),
            pltpu.VMEM(pout.shape, pout.dtype),
            pltpu.SemaphoreType.DMA((2, examples, 2)),
            pltpu.SemaphoreType.DMA((3,)),
        ],
        compiler_params=limit(24),
        name="project_own" if mine else "project_other",
    )(*(in_hbm(v) for v in (acts, grads, pin, pout) + passed))


def merge_kernel(own, got, queries, beside, total, pair):
    total[...] = own[...] + got[...]
    n = queries.shape[0]
    x_hi = lax.axis_index("dp") % 2
    pair[pl.ds(pl.multiple_of(x_hi * n, n), n), :] = queries[...]
    pair[pl.ds(pl.multiple_of((1 - x_hi) * n, n), n), :] = beside[...]


def merge(own, got, queries, beside):
    n, k = queries.shape
    return pl.pallas_call(
        merge_kernel,
        out_shape=[shape(*own.shape), shape(2 * n, k)],
        in_specs=[VMEM] * 4,
        out_specs=[VMEM] * 2,
        compiler_params=limit(8),
        name="merge",
    )(own, got, queries, beside)


def encode_kernel(sides, q0, q1, q2, q3, out, near):
    for dy, block in enumerate((q0, q1, q2, q3)):
        near[pl.ds(dy * block.shape[0], block.shape[0]), :] = block[...]
    total = ((sides[0] + sides[1]) + (sides[2] + sides[3])) + ((sides[4] + sides[5]) + (sides[6] + sides[7]))
    rank = total.shape[0] // 2
    enc = lax.dot_general(
        total[:rank], total[rank:], NT, precision=lax.Precision.HIGHEST, preferred_element_type=jnp.float32
    )
    out[...] = jnp.zeros_like(out)
    for t in range(16):
        out[t, :, :rank] = enc[8 * (t // 2) : 8 * (t // 2) + 8, :]


def encode(sides, *blocks):
    n, k = blocks[0].shape
    return pl.pallas_call(
        encode_kernel,
        out_shape=[shape(16, 8, 128), shape(4 * n, k)],
        in_specs=[VMEM] * 5,
        out_specs=[VMEM] * 2,
        compiler_params=limit(8),
        name="encode",
    )(sides, *blocks)


def score_kernel(scale, slices, near, far, out, tiles):
    core = lax.axis_index("tensor") % 2
    y = lax.axis_index("dp") // 2
    for e in range(8):
        tiles[pl.ds(8 * e, 8), :] = slices[2 * e] + slices[2 * e + 1]
    rows = [tiles[pl.ds(i, 8, stride=8), :][:, :64] for i in range(8)]
    low, high = jnp.concatenate(rows[:4], axis=1), jnp.concatenate(rows[4:], axis=1)
    mine = jnp.where(core == 0, low, high) * scale
    theirs = jnp.where(core == 0, high, low) * scale

    def dot(enc, block):
        return lax.dot_general(
            enc, block[...], NT, precision=lax.Precision.HIGHEST, preferred_element_type=jnp.float32
        )

    part = dot(mine, near) + dot(theirs, far)
    for dy in range(4):
        columns = pl.ds(pl.multiple_of((y - dy + 4) % 4 * 128, 128), 128)
        for g in range(8):
            out[g, :, columns] = part[:, 128 * dy : 128 * dy + 128]


def score(scale, slices, near, far):
    return pl.pallas_call(
        functools.partial(score_kernel, scale),
        out_shape=shape(8, 8, 512),
        in_specs=[VMEM] * 3,
        out_specs=VMEM,
        scratch_shapes=[pltpu.VMEM((64, 128), jnp.float32)],
        compiler_params=limit(8),
        name="score",
    )(slices, near, far)


def to_core(value):
    return lax.ppermute(value, "tensor", [(t, t ^ 1) for t in range(16)])


def per_device(acts, grads, proj_in, proj_out, queries):
    length = acts.shape[1]
    rank = proj_in.shape[1]
    pin, pout = proj_in.T, proj_out.T

    with jax.named_scope("sides"):
        other, queries = project(False, acts, grads, pin, pout, queries)
        beside = lax.ppermute(queries, "dp", [(d, d ^ 1) for d in range(8)])
        got = to_core(other)
        (own,) = project(True, acts, grads, pin, pout)
        total, pair = merge(own, got, queries, beside)
        sides = lax.all_to_all(total, "tensor", 0, 0, tiled=True, axis_index_groups=CHIPS)

    with jax.named_scope("queries"):
        blocks = [pair] + [
            lax.ppermute(pair, "dp", [(d, (d + 2 * dy) % 8) for d in range(8)]) for dy in (1, 2, 3)
        ]

    with jax.named_scope("encode"):
        encoded, near = encode(sides, *blocks)
        slices = lax.all_to_all(encoded, "tensor", 0, 0, tiled=True)
        far = to_core(near)

    with jax.named_scope("scores"):
        part = score(length ** (-0.5) / rank, slices, near, far)
        parts = lax.all_to_all(part, "tensor", 0, 0, tiled=True, axis_index_groups=CHIPS)
        return jnp.sum(parts, axis=0)


def solution(mesh):
    in_specs = (
        P("dp", None, "tensor"),
        P("dp", None, "tensor"),
        P("tensor", None),
        P("tensor", None),
        P("dp", "tensor"),
    )
    out_specs = P("dp", None)
    return jax.shard_map(
        per_device, mesh=mesh, in_specs=in_specs, out_specs=out_specs, check_vma=False
    )
```

time: 62.7 us -> 58 us (0.925)
  blocking collectives: 10.7 us -> 17.9 us
  waiting for transfers between devices: 17.5 us -> 11.5 us
  starting transfers between devices: 16.7 us -> 13.3 us
  local copies, waits for them, and re-layouts: 2.62 us -> 0 us
    ppermute x3, waiting for transfers between devices: 0.01 us -> 7.71 us  [per_device(): lax.ppermute(pair, 'dp', [(d, (d + 2 * dy) % 8) for d in range(8)])]
    all_to_all x1, waiting for transfers between devices: 11.4 us -> 3.74 us  [per_device(): lax.all_to_all(total, 'tensor', 0, 0, tiled=True, axis_index_groups=CHIPS)]
    all_to_all x1 -> x2, blocking collectives: 10.7 us -> 17.9 us  [the longest x1 9.09 us: per_device(): lax.all_to_all(part, 'tensor', 0, 0, tiled=True, axis_index_groups=CHIPS)]
    all_to_all x1 -> x0, waiting for transfers between devices: 6.07 us -> none  [per_device(): slices = lax.all_to_all(encode(sides), 'tensor', 0, 0, tiled=True)]
    all_to_all x1 -> x0, starting transfers between devices: 3.49 us -> none  [per_device(): slices = lax.all_to_all(encode(sides), 'tensor', 0, 0, tiled=True)]
    unnamed x6 -> x0, local copies, waits for them, and re-layouts: 2.62 us -> none
    pallas_call x5, Pallas kernels: 13.7 us -> 14.3 us  [the longest x2 12.1 us: project(): pl.pallas_call(functools.partial(project_kernel, mine), out_shape=[shape(...]
  transfers between devices with their start and end apart: 7 -> 7, of which waited for: 2 -> 4; matrix products, arithmetic and copies ran while one was open for 0% -> 0% of each run, Pallas kernels for 10% -> 10%
where the time goes in v3:
time: 58 us; the launch traced here: 57.7 us
  blocking collectives  17.9 us (31%)
  Pallas kernels  14.3 us (25%)
  starting transfers between devices  13.3 us (23%)
  waiting for transfers between devices  11.5 us (20%)
  other arithmetic  0.62 us (1%)
    pallas_call x2, Pallas kernels, project(): pl.pallas_call(functools.partial(project_kernel, mine), out_shape=[shape(...  12.1 us
    all_to_all x1, blocking collectives, per_device(): lax.all_to_all(part, 'tensor', 0, 0, tiled=True, axis_index_groups=CHIPS)  9.09 us
    all_to_all x1, blocking collectives, per_device(): slices = lax.all_to_all(encoded, 'tensor', 0, 0, tiled=True)  8.85 us
    ppermute x3, waiting for transfers between devices, per_device(): lax.ppermute(pair, 'dp', [(d, (d + 2 * dy) % 8) for d in range(8)])  7.71 us
    all_to_all x1, starting transfers between devices, per_device(): lax.all_to_all(total, 'tensor', 0, 0, tiled=True, axis_index_groups=CHIPS)  5.34 us
    ppermute x3, starting transfers between devices, per_device(): lax.ppermute(pair, 'dp', [(d, (d + 2 * dy) % 8) for d in range(8)])  4.61 us
    all_to_all x1, waiting for transfers between devices, per_device(): lax.all_to_all(total, 'tensor', 0, 0, tiled=True, axis_index_groups=CHIPS)  3.74 us
    ppermute x1, starting transfers between devices, per_device(): beside = lax.ppermute(queries, 'dp', [(d, d ^ 1) for d in range(8)])  3.18 us
  transfers between devices with their start and end apart: 7, of which 4 were waited for; matrix products, arithmetic and copies ran while one was open for 0% of the time, Pallas kernels for 10%

profile of v3, /device:TPU:0, one launch (start us, length us, event | category | flops | bytes accessed | tf_op | source)
XLA Modules:
  0.0 57.7 jit_solution(2656756320241248686)
XLA Ops:
  0.0 6.0 %project_other.1 = (f32[8,128,256]{2,1,0:T(8,128)S(1)}, f32[64,256]{1,0:T(8,128)S(1)}) custom-call(bf16[8,512,1792]{2,1,0:T(8,128)(2,1)} %acts.3, bf16[8,512,512]{2,1,0:T(8,128)(2,1)} %grads.3, bf16[64,1792]{1,0:T(8,128)(2,1)} %bitcast.2, bf16[64,512]{1,0:T(8,128)(2,1)} %bitcast.4, f32[64,256]{1,0:T(8,128)} %rest_0_.1), custom_call_target="tpu_custom_call" | custom-call | tf_op jit(solution)/shard_map/sides/project_other/pallas_call | solution.py:72
  6.0 0.1 collective-permute-start
  6.1 3.2 %collective-permute-start.1 = (f32[64,256]{1,0:T(8,128)S(1)}, f32[64,256]{1,0:T(8,128)S(1)}, u32[]{:S(2)}, u32[]{:S(2)}) collective-permute-start(f32[64,256]{1,0:T(8,128)S(1)} %get-tuple-element.12.queries), channel_id=1, source_target_pairs={{0,16},{16,0},{32,48},{48,32},{64,80},{80,64},{96,112},{112,96},{1... | collective-permute-start | bytes 196616 | tf_op jit(solution)/shard_map/sides/ppermute | solution.py:180
  9.3 6.0 %project_own.1.own = f32[8,128,256]{2,1,0:T(8,128)S(1)} custom-call(bf16[8,512,1792]{2,1,0:T(8,128)(2,1)} %acts.3, bf16[8,512,512]{2,1,0:T(8,128)(2,1)} %grads.3, bf16[64,1792]{1,0:T(8,128)(2,1)} %bitcast.3, bf16[64,512]{1,0:T(8,128)(2,1)} %bitcast.5), custom_call_target="tpu_custom_call" | custom-call | tf_op jit(solution)/shard_map/sides/project_own/pallas_call | solution.py:72
  15.3 0.0 collective-permute-done.1.beside
  15.4 0.0 collective-permute-done.got
  15.4 1.1 %merge.1 = (f32[8,128,256]{2,1,0:T(8,128)}, f32[128,256]{1,0:T(8,128)S(1)}) custom-call(f32[8,128,256]{2,1,0:T(8,128)S(1)} %project_own.1.own, f32[8,128,256]{2,1,0:T(8,128)S(1)} %collective-permute-done.got, f32[64,256]{1,0:T(8,128)S(1)} %get-tuple-element.12.queries, f32[64,256]{1,0:T(8,128)S(1)} %collective-permute-done.1.beside), custom_call_target="tpu_custom_call" | custom-call | tf_op jit(solution)/shard_map/sides/merge/pallas_call | solution.py:100
  16.5 5.3 %all-to-all-start = ((f32[8,128,256]{2,1,0:T(8,128)}), f32[8,128,256]{2,1,0:T(8,128)S(1)}, u32[]{:S(2)}, u32[]{:S(2)}) async-start(f32[8,128,256]{2,1,0:T(8,128)} %get-tuple-element.13), calls=%async_computation | async-start | bytes 2097152 | tf_op jit(solution)/shard_map/sides/all_to_all | solution.py:184
  21.8 3.0 %collective-permute-start.4 = (f32[128,256]{1,0:T(8,128)S(1)}, f32[128,256]{1,0:T(8,128)S(1)}, u32[]{:S(2)}, u32[]{:S(2)}) collective-permute-start(f32[128,256]{1,0:T(8,128)S(1)} %get-tuple-element.14.q0), channel_id=1, source_target_pairs={{0,96},{16,112},{32,0},{48,16},{64,32},{80,48},{96,64},{112,80},{1... | collective-permute-start | bytes 393224 | tf_op jit(solution)/shard_map/queries/ppermute | solution.py:188
  24.8 0.6 %collective-permute-start.3 = (f32[128,256]{1,0:T(8,128)S(1)}, f32[128,256]{1,0:T(8,128)S(1)}, u32[]{:S(2)}, u32[]{:S(2)}) collective-permute-start(f32[128,256]{1,0:T(8,128)S(1)} %get-tuple-element.14.q0), channel_id=1, source_target_pairs={{0,64},{16,80},{32,96},{48,112},{64,0},{80,16},{96,32},{112,48},{1... | collective-permute-start | bytes 393224 | tf_op jit(solution)/shard_map/queries/ppermute | solution.py:188
  25.4 1.0 %collective-permute-start.2 = (f32[128,256]{1,0:T(8,128)S(1)}, f32[128,256]{1,0:T(8,128)S(1)}, u32[]{:S(2)}, u32[]{:S(2)}) collective-permute-start(f32[128,256]{1,0:T(8,128)S(1)} %get-tuple-element.14.q0), channel_id=1, source_target_pairs={{0,32},{16,48},{32,64},{48,80},{64,96},{80,112},{96,0},{112,16},{1... | collective-permute-start | bytes 393224 | tf_op jit(solution)/shard_map/queries/ppermute | solution.py:188
  26.4 4.0 %collective-permute-done.4.q3 = f32[128,256]{1,0:T(8,128)S(1)} collective-permute-done((f32[128,256]{1,0:T(8,128)S(1)}, f32[128,256]{1,0:T(8,128)S(1)}, u32[]{:S(2)}, u32[]{:S(2)}) %collective-permute-start.4) | collective-permute-done | bytes 131104 | tf_op jit(solution)/shard_map/queries/ppermute | solution.py:188
  30.4 2.3 %collective-permute-done.3.q2 = f32[128,256]{1,0:T(8,128)S(1)} collective-permute-done((f32[128,256]{1,0:T(8,128)S(1)}, f32[128,256]{1,0:T(8,128)S(1)}, u32[]{:S(2)}, u32[]{:S(2)}) %collective-permute-start.3) | collective-permute-done | bytes 131104 | tf_op jit(solution)/shard_map/queries/ppermute | solution.py:188
  32.7 1.4 %collective-permute-done.2.q1 = f32[128,256]{1,0:T(8,128)S(1)} collective-permute-done((f32[128,256]{1,0:T(8,128)S(1)}, f32[128,256]{1,0:T(8,128)S(1)}, u32[]{:S(2)}, u32[]{:S(2)}) %collective-permute-start.2) | collective-permute-done | bytes 131104 | tf_op jit(solution)/shard_map/queries/ppermute | solution.py:188
  34.1 3.7 %all-to-all-done.sides = f32[8,128,256]{2,1,0:T(8,128)S(1)} async-done(((f32[8,128,256]{2,1,0:T(8,128)}), f32[8,128,256]{2,1,0:T(8,128)S(1)}, u32[]{:S(2)}, u32[]{:S(2)}) %all-to-all-start) | async-done | bytes 1048608 | tf_op jit(solution)/shard_map/sides/all_to_all | solution.py:184
  37.9 0.3 encode.1
  38.1 0.1 collective-permute-start.5
  38.2 8.8 %all_to_all.15.slices = f32[16,8,128]{2,1,0:T(8,128)S(1)} all-to-all(f32[16,8,128]{2,1,0:T(8,128)S(1)} %get-tuple-element.15), channel_id=1, replica_groups=mesh['dp'=8,'tensor'=16] {'tensor'}, dimensions={0} | all-to-all | bytes 131072 | tf_op jit(solution)/shard_map/encode/all_to_all | solution.py:193
  47.1 0.0 collective-permute-done.5.far
  47.1 0.9 %score.1 = f32[8,8,512]{2,1,0:T(8,128)S(1)} custom-call(f32[16,8,128]{2,1,0:T(8,128)S(1)} %all_to_all.15.slices, f32[512,256]{1,0:T(8,128)S(1)} %get-tuple-element.16.near, f32[512,256]{1,0:T(8,128)S(1)} %collective-permute-done.5.far), custom_call_target="tpu_custom_call" | custom-call | tf_op jit(solution)/shard_map/scores/score/pallas_call | solution.py:158
  48.0 9.1 %all_to_all.16 = f32[8,8,512]{2,1,0:T(8,128)S(1)} all-to-all(f32[8,8,512]{2,1,0:T(8,128)S(1)} %score.1), channel_id=1, replica_groups={{0,2,4,6,8,10,12,14},{1,3,5,7,9,11,13,15},{16,18,20,22,24,26,28,30},{17..., dimensions={0} | all-to-all | bytes 262144 | tf_op jit(solution)/shard_map/scores/all_to_all | solution.py:198
  57.1 0.6 %reduce_sum.9 = f32[8,512]{1,0:T(8,128)} reduce(f32[8,8,512]{2,1,0:T(8,128)S(1)} %all_to_all.16, f32[]{:T(128)} %constant.0.clone.1), dimensions={0}, to_apply=%region_0.0 | reduce | flops 28672 | bytes 147460 | tf_op jit(solution)/shard_map/scores/reduce_sum | solution.py:199
Async XLA Ops:
  6.0 9.3 %collective-permute-start = (f32[8,128,256]{2,1,0:T(8,128)S(1)}, f32[8,128,256]{2,1,0:T(8,128)S(1)}, u32[]{:S(2)}, u32[]{:S(2)}) collective-permute-start(f32[8,128,256]{2,1,0:T(8,128)S(1)} %get-tuple-element.11), channel_id=1, source_target_pairs={{0,1},{1,0},{2,3},{3,2},{4,5},{5,4},{6,7},{7,6},{8,9},{9,8},{10,11... | collective-permute-start | bytes 3145736 | tf_op jit(solution)/shard_map/sides/ppermute | solution.py:170
  6.1 9.2 %collective-permute-start.1 = (f32[64,256]{1,0:T(8,128)S(1)}, f32[64,256]{1,0:T(8,128)S(1)}, u32[]{:S(2)}, u32[]{:S(2)}) collective-permute-start(f32[64,256]{1,0:T(8,128)S(1)} %get-tuple-element.12.queries), channel_id=1, source_target_pairs={{0,16},{16,0},{32,48},{48,32},{64,80},{80,64},{96,112},{112,96},{1... | collective-permute-start | bytes 196616 | tf_op jit(solution)/shard_map/sides/ppermute | solution.py:180
  16.5 21.4 %all-to-all-start = ((f32[8,128,256]{2,1,0:T(8,128)}), f32[8,128,256]{2,1,0:T(8,128)S(1)}, u32[]{:S(2)}, u32[]{:S(2)}) async-start(f32[8,128,256]{2,1,0:T(8,128)} %get-tuple-element.13), calls=%async_computation | async-start | bytes 2097152 | tf_op jit(solution)/shard_map/sides/all_to_all | solution.py:184
  21.8 8.6 %collective-permute-start.4 = (f32[128,256]{1,0:T(8,128)S(1)}, f32[128,256]{1,0:T(8,128)S(1)}, u32[]{:S(2)}, u32[]{:S(2)}) collective-permute-start(f32[128,256]{1,0:T(8,128)S(1)} %get-tuple-element.14.q0), channel_id=1, source_target_pairs={{0,96},{16,112},{32,0},{48,16},{64,32},{80,48},{96,64},{112,80},{1... | collective-permute-start | bytes 393224 | tf_op jit(solution)/shard_map/queries/ppermute | solution.py:188
  24.8 7.9 %collective-permute-start.3 = (f32[128,256]{1,0:T(8,128)S(1)}, f32[128,256]{1,0:T(8,128)S(1)}, u32[]{:S(2)}, u32[]{:S(2)}) collective-permute-start(f32[128,256]{1,0:T(8,128)S(1)} %get-tuple-element.14.q0), channel_id=1, source_target_pairs={{0,64},{16,80},{32,96},{48,112},{64,0},{80,16},{96,32},{112,48},{1... | collective-permute-start | bytes 393224 | tf_op jit(solution)/shard_map/queries/ppermute | solution.py:188
  25.4 8.7 %collective-permute-start.2 = (f32[128,256]{1,0:T(8,128)S(1)}, f32[128,256]{1,0:T(8,128)S(1)}, u32[]{:S(2)}, u32[]{:S(2)}) collective-permute-start(f32[128,256]{1,0:T(8,128)S(1)} %get-tuple-element.14.q0), channel_id=1, source_target_pairs={{0,32},{16,48},{32,64},{48,80},{64,96},{80,112},{96,0},{112,16},{1... | collective-permute-start | bytes 393224 | tf_op jit(solution)/shard_map/queries/ppermute | solution.py:188
  38.1 8.9 %collective-permute-start.5 = (f32[512,256]{1,0:T(8,128)S(1)}, f32[512,256]{1,0:T(8,128)S(1)}, u32[]{:S(2)}, u32[]{:S(2)}) collective-permute-start(f32[512,256]{1,0:T(8,128)S(1)} %get-tuple-element.16.near), channel_id=1, source_target_pairs={{0,1},{1,0},{2,3},{3,2},{4,5},{5,4},{6,7},{7,6},{8,9},{9,8},{10,11... | collective-permute-start | bytes 1572872 | tf_op jit(solution)/shard_map/encode/ppermute | solution.py:170

commit v4 on v3

--- a/solution.py
+++ b/solution.py
@@ -9,6 +9,7 @@
 
 NT = (((1,), (1,)), ((), ()))
 CHIPS = [[c + 2 * chip for chip in range(8)] for c in range(2)]
+AHEAD = 4
 HBM = pl.BlockSpec(memory_space=pltpu.HBM)
 VMEM = pl.BlockSpec(memory_space=pltpu.VMEM)
 
@@ -25,66 +26,97 @@
     return jax.ShapeDtypeStruct(dims, jnp.float32)
 
 
-def project_kernel(mine, acts, grads, pin, pout, *rest):
+def project_kernel(mine, ahead, acts, grads, *rest):
     if mine:
-        out, held_a, held_g, held_pin, held_pout, sem, p_sem = rest
+        held_pin, held_pout, ahead_a, ahead_g, out, held_a, held_g, sem = rest
     else:
-        queries, out, passed, held_a, held_g, held_pin, held_pout, sem, p_sem = rest
+        pin, pout, queries, out, passed, held_pin, held_pout, ahead_a, ahead_g, held_a, held_g, sem, p_sem = rest
     examples, rank, rows = out.shape[0], out.shape[1] // 2, out.shape[2]
     core = lax.axis_index("tensor") % 2
     part = core if mine else 1 - core
-    weights = [
-        pltpu.make_async_copy(pout, held_pout, p_sem.at[0]),
-        pltpu.make_async_copy(pin, held_pin, p_sem.at[1]),
-    ]
-    blocks = []
-    for e in range(examples):
-        for k in range(2):
-            here = pl.ds(pl.multiple_of(part * rows + k * (rows // 2), rows // 2), rows // 2)
-            to = pl.ds(e * rows + k * (rows // 2), rows // 2)
-            blocks.append(pltpu.make_async_copy(grads.at[e, here, :], held_g.at[to, :], sem.at[0, e, k]))
-            blocks.append(pltpu.make_async_copy(acts.at[e, here, :], held_a.at[to, :], sem.at[1, e, k]))
-    for copy in weights + blocks[:8]:
-        copy.start()
-    for copy in weights:
-        copy.wait()
-    if not mine:
-        across = pltpu.make_async_copy(queries, passed, p_sem.at[2])
-        blocks.append(across)
-    for copy in blocks[8:]:
-        copy.start()
-    for e in range(0, examples, 2):
-        for copy in blocks[4 * e : 8 + 4 * e]:
+
+    def fetch(e, part, to_a, to_g, slot):
+        here = pl.ds(pl.multiple_of(part * rows, rows), rows)
+        to = pl.ds(slot * rows, rows)
+        return [
+            pltpu.make_async_copy(grads.at[e, here, :], to_g.at[to, :], sem.at[0, e]),
+            pltpu.make_async_copy(acts.at[e, here, :], to_a.at[to, :], sem.at[1, e]),
+        ]
+
+    skip = ahead if mine else 0
+    blocks = [fetch(e, part, held_a, held_g, e - skip) for e in range(skip, examples)]
+    if mine:
+        for block in blocks:
+            for copy in block:
+                copy.start()
+    else:
+        weights = [
+            pltpu.make_async_copy(pout, held_pout, p_sem.at[0]),
+            pltpu.make_async_copy(pin, held_pin, p_sem.at[1]),
+        ]
+        for copy in weights + blocks[0] + blocks[1]:
+            copy.start()
+        for copy in weights:
             copy.wait()
-        block = pl.ds(e * rows, 2 * rows)
-        so = lax.dot_general(held_pout[...], held_g[block, :], NT, preferred_element_type=jnp.float32)
-        si = lax.dot_general(held_pin[...], held_a[block, :], NT, preferred_element_type=jnp.float32)
+        for block in blocks[2:]:
+            for copy in block:
+                copy.start()
+
+    def multiply(e, from_a, from_g, slot):
+        at = pl.ds(slot * rows, 2 * rows)
+        so = lax.dot_general(held_pout[...], from_g[at, :], NT, preferred_element_type=jnp.float32)
+        si = lax.dot_general(held_pin[...], from_a[at, :], NT, preferred_element_type=jnp.float32)
         for k in range(2):
             out[e + k, :rank, :] = so[:, k * rows : (k + 1) * rows]
             out[e + k, rank:, :] = si[:, k * rows : (k + 1) * rows]
+
+    if mine:
+        for e in range(0, ahead, 2):
+            multiply(e, ahead_a, ahead_g, e)
+    later = []
+    for e in range(skip, examples, 2):
+        for copy in blocks[e - skip] + blocks[e + 1 - skip]:
+            copy.wait()
+        if not mine and e == 2:
+            later = [pltpu.make_async_copy(queries, passed, p_sem.at[2])]
+            for k in range(ahead):
+                to = pl.ds(k * rows, rows)
+                here = pl.ds(pl.multiple_of(core * rows, rows), rows)
+                later.append(pltpu.make_async_copy(grads.at[k, here, :], ahead_g.at[to, :], sem.at[2, k]))
+                later.append(pltpu.make_async_copy(acts.at[k, here, :], ahead_a.at[to, :], sem.at[3, k]))
+            for copy in later:
+                copy.start()
+        multiply(e, held_a, held_g, e - skip)
+    for copy in later:
+        copy.wait()
+
+
+def project(mine, ahead, acts, grads, *more):
+    examples, length, width_in = acts.shape
+    width_out = grads.shape[2]
+    rows = length // 2
+    kept = (examples - ahead if mine else examples) * rows
+    out_shape = [pltpu.VMEM((examples, 2 * more[0].shape[0], rows), jnp.float32)]
+    scratch_shapes = [
+        pltpu.VMEM((kept, width_in), acts.dtype),
+        pltpu.VMEM((kept, width_out), grads.dtype),
+        pltpu.SemaphoreType.DMA((4, examples)),
+    ]
     if not mine:
-        across.wait()
-
-
-def project(mine, acts, grads, pin, pout, *passed):
-    examples, length, width_in = acts.shape
-    rows = length // 2
-    return pl.pallas_call(
-        functools.partial(project_kernel, mine),
-        out_shape=[shape(examples, 2 * pin.shape[0], rows)] + [shape(*p.shape) for p in passed],
-        in_specs=[HBM] * (4 + len(passed)),
-        out_specs=[VMEM] * (1 + len(passed)),
-        scratch_shapes=[
-            pltpu.VMEM((examples * rows, width_in), acts.dtype),
-            pltpu.VMEM((examples * rows, grads.shape[2]), grads.dtype),
-            pltpu.VMEM(pin.shape, pin.dtype),
-            pltpu.VMEM(pout.shape, pout.dtype),
-            pltpu.SemaphoreType.DMA((2, examples, 2)),
-            pltpu.SemaphoreType.DMA((3,)),
-        ],
+        pin, pout, queries = more
+        out_shape += [pltpu.VMEM(v.shape, v.dtype) for v in (queries, pin, pout)]
+        out_shape += [pltpu.VMEM((ahead * rows, v.shape[2]), v.dtype) for v in (acts, grads)]
+        scratch_shapes.append(pltpu.SemaphoreType.DMA((3,)))
+        more = [in_hbm(v) for v in more]
+    return pl.pallas_call(
+        functools.partial(project_kernel, mine, ahead),
+        out_shape=out_shape,
+        in_specs=[HBM] * 2 + [VMEM if mine else HBM] * len(more),
+        out_specs=[VMEM] * len(out_shape),
+        scratch_shapes=scratch_shapes,
         compiler_params=limit(24),
         name="project_own" if mine else "project_other",
-    )(*(in_hbm(v) for v in (acts, grads, pin, pout) + passed))
+    )(in_hbm(acts), in_hbm(grads), *more)
 
 
 def merge_kernel(own, got, queries, beside, total, pair):
@@ -99,7 +131,7 @@
     n, k = queries.shape
     return pl.pallas_call(
         merge_kernel,
-        out_shape=[shape(*own.shape), shape(2 * n, k)],
+        out_shape=[pltpu.VMEM(own.shape, jnp.float32), pltpu.VMEM((2 * n, k), jnp.float32)],
         in_specs=[VMEM] * 4,
         out_specs=[VMEM] * 2,
         compiler_params=limit(8),
@@ -142,10 +174,16 @@
     mine = jnp.where(core == 0, low, high) * scale
     theirs = jnp.where(core == 0, high, low) * scale
 
+    def halves(value):
+        high = value.astype(jnp.bfloat16)
+        return high, (value - high.astype(jnp.float32)).astype(jnp.bfloat16)
+
     def dot(enc, block):
-        return lax.dot_general(
-            enc, block[...], NT, precision=lax.Precision.HIGHEST, preferred_element_type=jnp.float32
-        )
+        (a, b), (c, d) = halves(enc), halves(block[...])
+        both = jnp.concatenate([a, b], axis=0)
+        by_high = lax.dot_general(both, c, NT, preferred_element_type=jnp.float32)
+        by_low = lax.dot_general(both, d, NT, preferred_element_type=jnp.float32)
+        return by_high[:8] + (by_high[8:] + by_low[:8] + by_low[8:])
 
     part = dot(mine, near) + dot(theirs, far)
     for dy in range(4):
@@ -176,10 +214,10 @@
     pin, pout = proj_in.T, proj_out.T
 
     with jax.named_scope("sides"):
-        other, queries = project(False, acts, grads, pin, pout, queries)
+        other, queries, *first = project(False, AHEAD, acts, grads, pin, pout, queries)
         beside = lax.ppermute(queries, "dp", [(d, d ^ 1) for d in range(8)])
         got = to_core(other)
-        (own,) = project(True, acts, grads, pin, pout)
+        (own,) = project(True, AHEAD, acts, grads, *first)
         total, pair = merge(own, got, queries, beside)
         sides = lax.all_to_all(total, "tensor", 0, 0, tiled=True, axis_index_groups=CHIPS)
 

time: 58 us -> 56.1 us (0.967)
  Pallas kernels: 14.3 us -> 12.5 us
    pallas_call x3, Pallas kernels: 13.1 us -> 11.8 us  [the longest x2 10.7 us: project(): pl.pallas_call(functools.partial(project_kernel, mine, ahead), out_shape=...]
  transfers between devices with their start and end apart: 7 -> 7, of which waited for: 4 -> 4; matrix products, arithmetic and copies ran while one was open for 0% -> 0% of each run, Pallas kernels for 10% -> 9%
where the time goes in v4:
time: 56.1 us; the launch traced here: 55.9 us
  blocking collectives  17.9 us (32%)
  starting transfers between devices  13.3 us (24%)
  Pallas kernels  12.5 us (22%)
  waiting for transfers between devices  11.5 us (20%)
  other arithmetic  0.62 us (1%)
    pallas_call x2, Pallas kernels, project(): pl.pallas_call(functools.partial(project_kernel, mine, ahead), out_shape=...  10.7 us
    all_to_all x1, blocking collectives, per_device(): lax.all_to_all(part, 'tensor', 0, 0, tiled=True, axis_index_groups=CHIPS)  9.08 us
    all_to_all x1, blocking collectives, per_device(): slices = lax.all_to_all(encoded, 'tensor', 0, 0, tiled=True)  8.85 us
    ppermute x3, waiting for transfers between devices, per_device(): lax.ppermute(pair, 'dp', [(d, (d + 2 * dy) % 8) for d in range(8)])  7.71 us
    all_to_all x1, starting transfers between devices, per_device(): lax.all_to_all(total, 'tensor', 0, 0, tiled=True, axis_index_groups=CHIPS)  5.33 us
    ppermute x3, starting transfers between devices, per_device(): lax.ppermute(pair, 'dp', [(d, (d + 2 * dy) % 8) for d in range(8)])  4.61 us
    all_to_all x1, waiting for transfers between devices, per_device(): lax.all_to_all(total, 'tensor', 0, 0, tiled=True, axis_index_groups=CHIPS)  3.75 us
    ppermute x1, starting transfers between devices, per_device(): beside = lax.ppermute(queries, 'dp', [(d, d ^ 1) for d in range(8)])  3.19 us
  transfers between devices with their start and end apart: 7, of which 4 were waited for; matrix products, arithmetic and copies ran while one was open for 0% of the time, Pallas kernels for 9%

profile of v4, /device:TPU:0, one launch (start us, length us, event | category | flops | bytes accessed | tf_op | source)
XLA Modules:
  0.0 55.9 jit_solution(9336618463034292269)
XLA Ops:
  0.0 5.8 %project_other.1 = (f32[8,128,256]{2,1,0:T(8,128)S(1)}, f32[64,256]{1,0:T(8,128)S(1)}, bf16[64,1792]{1,0:T(8,128)(2,1)S(1)}, bf16[64,512]{1,0:T(8,128)(2,1)S(1)}...) custom-call(bf16[8,512,1792]{2,1,0:T(8,128)(2,1)} %acts.3, bf16[8,512,512]{2,1,0:T(8,128)(2,1)} %grads.3, ...), custom_call_target="tpu_custom_call" | custom-call | tf_op jit(solution)/shard_map/sides/project_other/pallas_call | solution.py:111
  5.9 0.1 collective-permute-start
  6.0 3.2 %collective-permute-start.1 = (f32[64,256]{1,0:T(8,128)S(1)}, f32[64,256]{1,0:T(8,128)S(1)}, u32[]{:S(2)}, u32[]{:S(2)}) collective-permute-start(f32[64,256]{1,0:T(8,128)S(1)} %get-tuple-element.20.queries), channel_id=1, source_target_pairs={{0,16},{16,0},{32,48},{48,32},{64,80},{80,64},{96,112},{112,96},{1... | collective-permute-start | bytes 196616 | tf_op jit(solution)/shard_map/sides/ppermute | solution.py:218
  9.1 4.9 %project_own.1.own = f32[8,128,256]{2,1,0:T(8,128)S(1)} custom-call(bf16[8,512,1792]{2,1,0:T(8,128)(2,1)} %acts.3, bf16[8,512,512]{2,1,0:T(8,128)(2,1)} %grads.3, bf16[64,1792]{1,0:T(8,128)(2,1)S(1)} %get-tuple-element.15.rest_0_, bf16[64,512]{1,0:T(8,128)(2,1)S(1)} %get-tuple-element.16.rest_1_, bf16[1024,1792]{1,0:T(8,128)(2,1)S(1)} %get-tuple-element.17.rest_2_, ...), custom_call_target="tpu_custom_call" | custom-call | tf_op jit(solution)/shard_map/sides/project_own/pallas_call | solution.py:111
  14.0 0.0 collective-permute-done.1.beside
  14.1 0.0 collective-permute-done.got
  14.1 1.1 %merge.1 = (f32[8,128,256]{2,1,0:T(8,128)}, f32[128,256]{1,0:T(8,128)S(1)}) custom-call(f32[8,128,256]{2,1,0:T(8,128)S(1)} %project_own.1.own, f32[8,128,256]{2,1,0:T(8,128)S(1)} %collective-permute-done.got, f32[64,256]{1,0:T(8,128)S(1)} %get-tuple-element.20.queries, f32[64,256]{1,0:T(8,128)S(1)} %collective-permute-done.1.beside), custom_call_target="tpu_custom_call" | custom-call | tf_op jit(solution)/shard_map/sides/merge/pallas_call | solution.py:132
  15.1 5.3 %all-to-all-start = ((f32[8,128,256]{2,1,0:T(8,128)}), f32[8,128,256]{2,1,0:T(8,128)S(1)}, u32[]{:S(2)}, u32[]{:S(2)}) async-start(f32[8,128,256]{2,1,0:T(8,128)} %get-tuple-element.21), calls=%async_computation | async-start | bytes 2097152 | tf_op jit(solution)/shard_map/sides/all_to_all | solution.py:222
  20.5 3.0 %collective-permute-start.4 = (f32[128,256]{1,0:T(8,128)S(1)}, f32[128,256]{1,0:T(8,128)S(1)}, u32[]{:S(2)}, u32[]{:S(2)}) collective-permute-start(f32[128,256]{1,0:T(8,128)S(1)} %get-tuple-element.22.q0), channel_id=1, source_target_pairs={{0,96},{16,112},{32,0},{48,16},{64,32},{80,48},{96,64},{112,80},{1... | collective-permute-start | bytes 393224 | tf_op jit(solution)/shard_map/queries/ppermute | solution.py:226
  23.5 0.6 %collective-permute-start.3 = (f32[128,256]{1,0:T(8,128)S(1)}, f32[128,256]{1,0:T(8,128)S(1)}, u32[]{:S(2)}, u32[]{:S(2)}) collective-permute-start(f32[128,256]{1,0:T(8,128)S(1)} %get-tuple-element.22.q0), channel_id=1, source_target_pairs={{0,64},{16,80},{32,96},{48,112},{64,0},{80,16},{96,32},{112,48},{1... | collective-permute-start | bytes 393224 | tf_op jit(solution)/shard_map/queries/ppermute | solution.py:226
  24.1 1.0 %collective-permute-start.2 = (f32[128,256]{1,0:T(8,128)S(1)}, f32[128,256]{1,0:T(8,128)S(1)}, u32[]{:S(2)}, u32[]{:S(2)}) collective-permute-start(f32[128,256]{1,0:T(8,128)S(1)} %get-tuple-element.22.q0), channel_id=1, source_target_pairs={{0,32},{16,48},{32,64},{48,80},{64,96},{80,112},{96,0},{112,16},{1... | collective-permute-start | bytes 393224 | tf_op jit(solution)/shard_map/queries/ppermute | solution.py:226
  25.1 4.0 %collective-permute-done.4.q3 = f32[128,256]{1,0:T(8,128)S(1)} collective-permute-done((f32[128,256]{1,0:T(8,128)S(1)}, f32[128,256]{1,0:T(8,128)S(1)}, u32[]{:S(2)}, u32[]{:S(2)}) %collective-permute-start.4) | collective-permute-done | bytes 131104 | tf_op jit(solution)/shard_map/queries/ppermute | solution.py:226
  29.1 2.3 %collective-permute-done.3.q2 = f32[128,256]{1,0:T(8,128)S(1)} collective-permute-done((f32[128,256]{1,0:T(8,128)S(1)}, f32[128,256]{1,0:T(8,128)S(1)}, u32[]{:S(2)}, u32[]{:S(2)}) %collective-permute-start.3) | collective-permute-done | bytes 131104 | tf_op jit(solution)/shard_map/queries/ppermute | solution.py:226
  31.4 1.4 %collective-permute-done.2.q1 = f32[128,256]{1,0:T(8,128)S(1)} collective-permute-done((f32[128,256]{1,0:T(8,128)S(1)}, f32[128,256]{1,0:T(8,128)S(1)}, u32[]{:S(2)}, u32[]{:S(2)}) %collective-permute-start.2) | collective-permute-done | bytes 131104 | tf_op jit(solution)/shard_map/queries/ppermute | solution.py:226
  32.8 3.7 %all-to-all-done.sides = f32[8,128,256]{2,1,0:T(8,128)S(1)} async-done(((f32[8,128,256]{2,1,0:T(8,128)}), f32[8,128,256]{2,1,0:T(8,128)S(1)}, u32[]{:S(2)}, u32[]{:S(2)}) %all-to-all-start) | async-done | bytes 1048608 | tf_op jit(solution)/shard_map/sides/all_to_all | solution.py:222
  36.5 0.3 encode.1
  36.8 0.1 collective-permute-start.5
  36.9 8.8 %all_to_all.15.slices = f32[16,8,128]{2,1,0:T(8,128)S(1)} all-to-all(f32[16,8,128]{2,1,0:T(8,128)S(1)} %get-tuple-element.23), channel_id=1, replica_groups=mesh['dp'=8,'tensor'=16] {'tensor'}, dimensions={0} | all-to-all | bytes 131072 | tf_op jit(solution)/shard_map/encode/all_to_all | solution.py:231
  45.7 0.0 collective-permute-done.5.far
  45.8 0.4 score.1
  46.2 9.1 %all_to_all.16 = f32[8,8,512]{2,1,0:T(8,128)S(1)} all-to-all(f32[8,8,512]{2,1,0:T(8,128)S(1)} %score.1), channel_id=1, replica_groups={{0,2,4,6,8,10,12,14},{1,3,5,7,9,11,13,15},{16,18,20,22,24,26,28,30},{17..., dimensions={0} | all-to-all | bytes 262144 | tf_op jit(solution)/shard_map/scores/all_to_all | solution.py:236
  55.3 0.6 %reduce_sum.9 = f32[8,512]{1,0:T(8,128)} reduce(f32[8,8,512]{2,1,0:T(8,128)S(1)} %all_to_all.16, f32[]{:T(128)} %constant.0.clone.1), dimensions={0}, to_apply=%region_0.0 | reduce | flops 28672 | bytes 147460 | tf_op jit(solution)/shard_map/scores/reduce_sum | solution.py:237
Async XLA Ops:
  5.9 8.2 %collective-permute-start = (f32[8,128,256]{2,1,0:T(8,128)S(1)}, f32[8,128,256]{2,1,0:T(8,128)S(1)}, u32[]{:S(2)}, u32[]{:S(2)}) collective-permute-start(f32[8,128,256]{2,1,0:T(8,128)S(1)} %get-tuple-element.19), channel_id=1, source_target_pairs={{0,1},{1,0},{2,3},{3,2},{4,5},{5,4},{6,7},{7,6},{8,9},{9,8},{10,11... | collective-permute-start | bytes 3145736 | tf_op jit(solution)/shard_map/sides/ppermute | solution.py:208
  6.0 8.1 %collective-permute-start.1 = (f32[64,256]{1,0:T(8,128)S(1)}, f32[64,256]{1,0:T(8,128)S(1)}, u32[]{:S(2)}, u32[]{:S(2)}) collective-permute-start(f32[64,256]{1,0:T(8,128)S(1)} %get-tuple-element.20.queries), channel_id=1, source_target_pairs={{0,16},{16,0},{32,48},{48,32},{64,80},{80,64},{96,112},{112,96},{1... | collective-permute-start | bytes 196616 | tf_op jit(solution)/shard_map/sides/ppermute | solution.py:218
  15.1 21.4 %all-to-all-start = ((f32[8,128,256]{2,1,0:T(8,128)}), f32[8,128,256]{2,1,0:T(8,128)S(1)}, u32[]{:S(2)}, u32[]{:S(2)}) async-start(f32[8,128,256]{2,1,0:T(8,128)} %get-tuple-element.21), calls=%async_computation | async-start | bytes 2097152 | tf_op jit(solution)/shard_map/sides/all_to_all | solution.py:222
  20.5 8.6 %collective-permute-start.4 = (f32[128,256]{1,0:T(8,128)S(1)}, f32[128,256]{1,0:T(8,128)S(1)}, u32[]{:S(2)}, u32[]{:S(2)}) collective-permute-start(f32[128,256]{1,0:T(8,128)S(1)} %get-tuple-element.22.q0), channel_id=1, source_target_pairs={{0,96},{16,112},{32,0},{48,16},{64,32},{80,48},{96,64},{112,80},{1... | collective-permute-start | bytes 393224 | tf_op jit(solution)/shard_map/queries/ppermute | solution.py:226
  23.5 7.9 %collective-permute-start.3 = (f32[128,256]{1,0:T(8,128)S(1)}, f32[128,256]{1,0:T(8,128)S(1)}, u32[]{:S(2)}, u32[]{:S(2)}) collective-permute-start(f32[128,256]{1,0:T(8,128)S(1)} %get-tuple-element.22.q0), channel_id=1, source_target_pairs={{0,64},{16,80},{32,96},{48,112},{64,0},{80,16},{96,32},{112,48},{1... | collective-permute-start | bytes 393224 | tf_op jit(solution)/shard_map/queries/ppermute | solution.py:226
  24.1 8.7 %collective-permute-start.2 = (f32[128,256]{1,0:T(8,128)S(1)}, f32[128,256]{1,0:T(8,128)S(1)}, u32[]{:S(2)}, u32[]{:S(2)}) collective-permute-start(f32[128,256]{1,0:T(8,128)S(1)} %get-tuple-element.22.q0), channel_id=1, source_target_pairs={{0,32},{16,48},{32,64},{48,80},{64,96},{80,112},{96,0},{112,16},{1... | collective-permute-start | bytes 393224 | tf_op jit(solution)/shard_map/queries/ppermute | solution.py:226
  36.8 8.9 %collective-permute-start.5 = (f32[512,256]{1,0:T(8,128)S(1)}, f32[512,256]{1,0:T(8,128)S(1)}, u32[]{:S(2)}, u32[]{:S(2)}) collective-permute-start(f32[512,256]{1,0:T(8,128)S(1)} %get-tuple-element.24.near), channel_id=1, source_target_pairs={{0,1},{1,0},{2,3},{3,2},{4,5},{5,4},{6,7},{7,6},{8,9},{9,8},{10,11... | collective-permute-start | bytes 1572872 | tf_op jit(solution)/shard_map/encode/ppermute | solution.py:208

commit v5 on v4

--- a/solution.py
+++ b/solution.py
@@ -62,33 +62,49 @@
             for copy in block:
                 copy.start()
 
-    def multiply(e, from_a, from_g, slot):
-        at = pl.ds(slot * rows, 2 * rows)
-        so = lax.dot_general(held_pout[...], from_g[at, :], NT, preferred_element_type=jnp.float32)
-        si = lax.dot_general(held_pin[...], from_a[at, :], NT, preferred_element_type=jnp.float32)
-        for k in range(2):
-            out[e + k, :rank, :] = so[:, k * rows : (k + 1) * rows]
-            out[e + k, rank:, :] = si[:, k * rows : (k + 1) * rows]
-
-    if mine:
-        for e in range(0, ahead, 2):
-            multiply(e, ahead_a, ahead_g, e)
-    later = []
-    for e in range(skip, examples, 2):
-        for copy in blocks[e - skip] + blocks[e + 1 - skip]:
+    def push(e, accs, from_a, from_g, slot):
+        step = 0
+        for rows_in, weights, which in ((from_g, held_pout, 0), (from_a, held_pin, 1)):
+            for k in range(weights.shape[1] // 256):
+                cut = slice(256 * k, 256 * k + 256)
+                for unit in range(2):
+                    block = rows_in[pl.ds((slot + unit) * rows, rows), cut]
+                    pltpu.matmul_push_rhs(block, step % 2, unit, transpose=True)
+                    pltpu.matmul_acc_lhs(accs[2 * unit + which], weights[:, cut], load_staged_rhs=step % 2)
+                step += 1
+
+    def pop(e, accs):
+        for unit in range(2):
+            out[e + unit, :rank, :] = pltpu.matmul_pop(accs[2 * unit])
+            out[e + unit, rank:, :] = pltpu.matmul_pop(accs[2 * unit + 1])
+
+    def body(*accs):
+        later = []
+        for e in range(0, examples, 2):
+            turn = accs[4 * (e // 2 % 2) :][:4]
+            if e < skip:
+                push(e, turn, ahead_a, ahead_g, e)
+            else:
+                for copy in blocks[e - skip] + blocks[e + 1 - skip]:
+                    copy.wait()
+                if not mine and not later:
+                    later = [pltpu.make_async_copy(queries, passed, p_sem.at[2])]
+                    for k in range(ahead):
+                        to = pl.ds(k * rows, rows)
+                        here = pl.ds(pl.multiple_of(core * rows, rows), rows)
+                        later.append(pltpu.make_async_copy(grads.at[k, here, :], ahead_g.at[to, :], sem.at[2, k]))
+                        later.append(pltpu.make_async_copy(acts.at[k, here, :], ahead_a.at[to, :], sem.at[3, k]))
+                    for copy in later:
+                        copy.start()
+                push(e, turn, held_a, held_g, e - skip)
+            if e >= 2:
+                pop(e - 2, accs[4 * ((e - 2) // 2 % 2) :][:4])
+        pop(examples - 2, accs[4 * ((examples - 2) // 2 % 2) :][:4])
+        for copy in later:
             copy.wait()
-        if not mine and e == 2:
-            later = [pltpu.make_async_copy(queries, passed, p_sem.at[2])]
-            for k in range(ahead):
-                to = pl.ds(k * rows, rows)
-                here = pl.ds(pl.multiple_of(core * rows, rows), rows)
-                later.append(pltpu.make_async_copy(grads.at[k, here, :], ahead_g.at[to, :], sem.at[2, k]))
-                later.append(pltpu.make_async_copy(acts.at[k, here, :], ahead_a.at[to, :], sem.at[3, k]))
-            for copy in later:
-                copy.start()
-        multiply(e, held_a, held_g, e - skip)
-    for copy in later:
-        copy.wait()
+
+    units = [pltpu.ACC(unit)((rank, rows), jnp.float32) for _ in range(2) for unit in (0, 0, 1, 1)]
+    pl.run_scoped(body, *units)
 
 
 def project(mine, ahead, acts, grads, *more):

time: 56.1 us -> 55.5 us (0.989)
  Pallas kernels: 12.5 us -> 11.8 us
    pallas_call x2, Pallas kernels: 10.7 us -> 10.1 us  [project(): pl.pallas_call(functools.partial(project_kernel, mine, ahead), out_shape=...]
  transfers between devices with their start and end apart: 7 -> 7, of which waited for: 4 -> 4; matrix products, arithmetic and copies ran while one was open for 0% -> 0% of each run, Pallas kernels for 9% -> 8%
where the time goes in v5:
time: 55.5 us; the launch traced here: 55.2 us
  blocking collectives  17.9 us (32%)
  starting transfers between devices  13.3 us (24%)
  Pallas kernels  11.8 us (21%)
  waiting for transfers between devices  11.5 us (21%)
  other arithmetic  0.62 us (1%)
    pallas_call x2, Pallas kernels, project(): pl.pallas_call(functools.partial(project_kernel, mine, ahead), out_shape=...  10.1 us
    all_to_all x1, blocking collectives, per_device(): lax.all_to_all(part, 'tensor', 0, 0, tiled=True, axis_index_groups=CHIPS)  9.08 us
    all_to_all x1, blocking collectives, per_device(): slices = lax.all_to_all(encoded, 'tensor', 0, 0, tiled=True)  8.85 us
    ppermute x3, waiting for transfers between devices, per_device(): lax.ppermute(pair, 'dp', [(d, (d + 2 * dy) % 8) for d in range(8)])  7.7 us
    all_to_all x1, starting transfers between devices, per_device(): lax.all_to_all(total, 'tensor', 0, 0, tiled=True, axis_index_groups=CHIPS)  5.34 us
    ppermute x3, starting transfers between devices, per_device(): lax.ppermute(pair, 'dp', [(d, (d + 2 * dy) % 8) for d in range(8)])  4.62 us
    all_to_all x1, waiting for transfers between devices, per_device(): lax.all_to_all(total, 'tensor', 0, 0, tiled=True, axis_index_groups=CHIPS)  3.74 us
    ppermute x1, starting transfers between devices, per_device(): beside = lax.ppermute(queries, 'dp', [(d, d ^ 1) for d in range(8)])  3.19 us
  transfers between devices with their start and end apart: 7, of which 4 were waited for; matrix products, arithmetic and copies ran while one was open for 0% of the time, Pallas kernels for 8%

profile of v5, /device:TPU:0, one launch (start us, length us, event | category | flops | bytes accessed | tf_op | source)
XLA Modules:
  0.0 55.2 jit_solution(3785054459430129113)
XLA Ops:
  0.0 5.8 %project_other.1 = (f32[8,128,256]{2,1,0:T(8,128)S(1)}, f32[64,256]{1,0:T(8,128)S(1)}, bf16[64,1792]{1,0:T(8,128)(2,1)S(1)}, bf16[64,512]{1,0:T(8,128)(2,1)S(1)}...) custom-call(bf16[8,512,1792]{2,1,0:T(8,128)(2,1)} %acts.3, bf16[8,512,512]{2,1,0:T(8,128)(2,1)} %grads.3, ...), custom_call_target="tpu_custom_call" | custom-call | tf_op jit(solution)/shard_map/sides/project_other/pallas_call | solution.py:127
  5.8 0.1 collective-permute-start
  5.9 3.2 %collective-permute-start.1 = (f32[64,256]{1,0:T(8,128)S(1)}, f32[64,256]{1,0:T(8,128)S(1)}, u32[]{:S(2)}, u32[]{:S(2)}) collective-permute-start(f32[64,256]{1,0:T(8,128)S(1)} %get-tuple-element.20.queries), channel_id=1, source_target_pairs={{0,16},{16,0},{32,48},{48,32},{64,80},{80,64},{96,112},{112,96},{1... | collective-permute-start | bytes 196616 | tf_op jit(solution)/shard_map/sides/ppermute | solution.py:234
  9.1 4.3 %project_own.1.own = f32[8,128,256]{2,1,0:T(8,128)S(1)} custom-call(bf16[8,512,1792]{2,1,0:T(8,128)(2,1)} %acts.3, bf16[8,512,512]{2,1,0:T(8,128)(2,1)} %grads.3, bf16[64,1792]{1,0:T(8,128)(2,1)S(1)} %get-tuple-element.15.rest_0_, bf16[64,512]{1,0:T(8,128)(2,1)S(1)} %get-tuple-element.16.rest_1_, bf16[1024,1792]{1,0:T(8,128)(2,1)S(1)} %get-tuple-element.17.rest_2_, ...), custom_call_target="tpu_custom_call" | custom-call | tf_op jit(solution)/shard_map/sides/project_own/pallas_call | solution.py:127
  13.4 0.0 collective-permute-done.1.beside
  13.4 0.0 collective-permute-done.got
  13.4 1.1 %merge.1 = (f32[8,128,256]{2,1,0:T(8,128)}, f32[128,256]{1,0:T(8,128)S(1)}) custom-call(f32[8,128,256]{2,1,0:T(8,128)S(1)} %project_own.1.own, f32[8,128,256]{2,1,0:T(8,128)S(1)} %collective-permute-done.got, f32[64,256]{1,0:T(8,128)S(1)} %get-tuple-element.20.queries, f32[64,256]{1,0:T(8,128)S(1)} %collective-permute-done.1.beside), custom_call_target="tpu_custom_call" | custom-call | tf_op jit(solution)/shard_map/sides/merge/pallas_call | solution.py:148
  14.5 5.3 %all-to-all-start = ((f32[8,128,256]{2,1,0:T(8,128)}), f32[8,128,256]{2,1,0:T(8,128)S(1)}, u32[]{:S(2)}, u32[]{:S(2)}) async-start(f32[8,128,256]{2,1,0:T(8,128)} %get-tuple-element.21), calls=%async_computation | async-start | bytes 2097152 | tf_op jit(solution)/shard_map/sides/all_to_all | solution.py:238
  19.8 3.0 %collective-permute-start.4 = (f32[128,256]{1,0:T(8,128)S(1)}, f32[128,256]{1,0:T(8,128)S(1)}, u32[]{:S(2)}, u32[]{:S(2)}) collective-permute-start(f32[128,256]{1,0:T(8,128)S(1)} %get-tuple-element.22.q0), channel_id=1, source_target_pairs={{0,96},{16,112},{32,0},{48,16},{64,32},{80,48},{96,64},{112,80},{1... | collective-permute-start | bytes 393224 | tf_op jit(solution)/shard_map/queries/ppermute | solution.py:242
  22.8 0.6 %collective-permute-start.3 = (f32[128,256]{1,0:T(8,128)S(1)}, f32[128,256]{1,0:T(8,128)S(1)}, u32[]{:S(2)}, u32[]{:S(2)}) collective-permute-start(f32[128,256]{1,0:T(8,128)S(1)} %get-tuple-element.22.q0), channel_id=1, source_target_pairs={{0,64},{16,80},{32,96},{48,112},{64,0},{80,16},{96,32},{112,48},{1... | collective-permute-start | bytes 393224 | tf_op jit(solution)/shard_map/queries/ppermute | solution.py:242
  23.4 1.0 %collective-permute-start.2 = (f32[128,256]{1,0:T(8,128)S(1)}, f32[128,256]{1,0:T(8,128)S(1)}, u32[]{:S(2)}, u32[]{:S(2)}) collective-permute-start(f32[128,256]{1,0:T(8,128)S(1)} %get-tuple-element.22.q0), channel_id=1, source_target_pairs={{0,32},{16,48},{32,64},{48,80},{64,96},{80,112},{96,0},{112,16},{1... | collective-permute-start | bytes 393224 | tf_op jit(solution)/shard_map/queries/ppermute | solution.py:242
  24.4 4.0 %collective-permute-done.4.q3 = f32[128,256]{1,0:T(8,128)S(1)} collective-permute-done((f32[128,256]{1,0:T(8,128)S(1)}, f32[128,256]{1,0:T(8,128)S(1)}, u32[]{:S(2)}, u32[]{:S(2)}) %collective-permute-start.4) | collective-permute-done | bytes 131104 | tf_op jit(solution)/shard_map/queries/ppermute | solution.py:242
  28.4 2.3 %collective-permute-done.3.q2 = f32[128,256]{1,0:T(8,128)S(1)} collective-permute-done((f32[128,256]{1,0:T(8,128)S(1)}, f32[128,256]{1,0:T(8,128)S(1)}, u32[]{:S(2)}, u32[]{:S(2)}) %collective-permute-start.3) | collective-permute-done | bytes 131104 | tf_op jit(solution)/shard_map/queries/ppermute | solution.py:242
  30.7 1.4 %collective-permute-done.2.q1 = f32[128,256]{1,0:T(8,128)S(1)} collective-permute-done((f32[128,256]{1,0:T(8,128)S(1)}, f32[128,256]{1,0:T(8,128)S(1)}, u32[]{:S(2)}, u32[]{:S(2)}) %collective-permute-start.2) | collective-permute-done | bytes 131104 | tf_op jit(solution)/shard_map/queries/ppermute | solution.py:242
  32.1 3.7 %all-to-all-done.sides = f32[8,128,256]{2,1,0:T(8,128)S(1)} async-done(((f32[8,128,256]{2,1,0:T(8,128)}), f32[8,128,256]{2,1,0:T(8,128)S(1)}, u32[]{:S(2)}, u32[]{:S(2)}) %all-to-all-start) | async-done | bytes 1048608 | tf_op jit(solution)/shard_map/sides/all_to_all | solution.py:238
  35.9 0.2 encode.1
  36.1 0.1 collective-permute-start.5
  36.2 8.8 %all_to_all.15.slices = f32[16,8,128]{2,1,0:T(8,128)S(1)} all-to-all(f32[16,8,128]{2,1,0:T(8,128)S(1)} %get-tuple-element.23), channel_id=1, replica_groups=mesh['dp'=8,'tensor'=16] {'tensor'}, dimensions={0} | all-to-all | bytes 131072 | tf_op jit(solution)/shard_map/encode/all_to_all | solution.py:247
  45.1 0.0 collective-permute-done.5.far
  45.1 0.4 score.1
  45.5 9.1 %all_to_all.16 = f32[8,8,512]{2,1,0:T(8,128)S(1)} all-to-all(f32[8,8,512]{2,1,0:T(8,128)S(1)} %score.1), channel_id=1, replica_groups={{0,2,4,6,8,10,12,14},{1,3,5,7,9,11,13,15},{16,18,20,22,24,26,28,30},{17..., dimensions={0} | all-to-all | bytes 262144 | tf_op jit(solution)/shard_map/scores/all_to_all | solution.py:252
  54.6 0.6 %reduce_sum.9 = f32[8,512]{1,0:T(8,128)} reduce(f32[8,8,512]{2,1,0:T(8,128)S(1)} %all_to_all.16, f32[]{:T(128)} %constant.0.clone.1), dimensions={0}, to_apply=%region_0.0 | reduce | flops 28672 | bytes 147460 | tf_op jit(solution)/shard_map/scores/reduce_sum | solution.py:253
Async XLA Ops:
  5.8 7.6 %collective-permute-start = (f32[8,128,256]{2,1,0:T(8,128)S(1)}, f32[8,128,256]{2,1,0:T(8,128)S(1)}, u32[]{:S(2)}, u32[]{:S(2)}) collective-permute-start(f32[8,128,256]{2,1,0:T(8,128)S(1)} %get-tuple-element.19), channel_id=1, source_target_pairs={{0,1},{1,0},{2,3},{3,2},{4,5},{5,4},{6,7},{7,6},{8,9},{9,8},{10,11... | collective-permute-start | bytes 3145736 | tf_op jit(solution)/shard_map/sides/ppermute | solution.py:224
  5.9 7.5 %collective-permute-start.1 = (f32[64,256]{1,0:T(8,128)S(1)}, f32[64,256]{1,0:T(8,128)S(1)}, u32[]{:S(2)}, u32[]{:S(2)}) collective-permute-start(f32[64,256]{1,0:T(8,128)S(1)} %get-tuple-element.20.queries), channel_id=1, source_target_pairs={{0,16},{16,0},{32,48},{48,32},{64,80},{80,64},{96,112},{112,96},{1... | collective-permute-start | bytes 196616 | tf_op jit(solution)/shard_map/sides/ppermute | solution.py:234
  14.5 21.4 %all-to-all-start = ((f32[8,128,256]{2,1,0:T(8,128)}), f32[8,128,256]{2,1,0:T(8,128)S(1)}, u32[]{:S(2)}, u32[]{:S(2)}) async-start(f32[8,128,256]{2,1,0:T(8,128)} %get-tuple-element.21), calls=%async_computation | async-start | bytes 2097152 | tf_op jit(solution)/shard_map/sides/all_to_all | solution.py:238
  19.8 8.6 %collective-permute-start.4 = (f32[128,256]{1,0:T(8,128)S(1)}, f32[128,256]{1,0:T(8,128)S(1)}, u32[]{:S(2)}, u32[]{:S(2)}) collective-permute-start(f32[128,256]{1,0:T(8,128)S(1)} %get-tuple-element.22.q0), channel_id=1, source_target_pairs={{0,96},{16,112},{32,0},{48,16},{64,32},{80,48},{96,64},{112,80},{1... | collective-permute-start | bytes 393224 | tf_op jit(solution)/shard_map/queries/ppermute | solution.py:242
  22.8 7.9 %collective-permute-start.3 = (f32[128,256]{1,0:T(8,128)S(1)}, f32[128,256]{1,0:T(8,128)S(1)}, u32[]{:S(2)}, u32[]{:S(2)}) collective-permute-start(f32[128,256]{1,0:T(8,128)S(1)} %get-tuple-element.22.q0), channel_id=1, source_target_pairs={{0,64},{16,80},{32,96},{48,112},{64,0},{80,16},{96,32},{112,48},{1... | collective-permute-start | bytes 393224 | tf_op jit(solution)/shard_map/queries/ppermute | solution.py:242
  23.4 8.7 %collective-permute-start.2 = (f32[128,256]{1,0:T(8,128)S(1)}, f32[128,256]{1,0:T(8,128)S(1)}, u32[]{:S(2)}, u32[]{:S(2)}) collective-permute-start(f32[128,256]{1,0:T(8,128)S(1)} %get-tuple-element.22.q0), channel_id=1, source_target_pairs={{0,32},{16,48},{32,64},{48,80},{64,96},{80,112},{96,0},{112,16},{1... | collective-permute-start | bytes 393224 | tf_op jit(solution)/shard_map/queries/ppermute | solution.py:242
  36.1 8.9 %collective-permute-start.5 = (f32[512,256]{1,0:T(8,128)S(1)}, f32[512,256]{1,0:T(8,128)S(1)}, u32[]{:S(2)}, u32[]{:S(2)}) collective-permute-start(f32[512,256]{1,0:T(8,128)S(1)} %get-tuple-element.24.near), channel_id=1, source_target_pairs={{0,1},{1,0},{2,3},{3,2},{4,5},{5,4},{6,7},{7,6},{8,9},{9,8},{10,11... | collective-permute-start | bytes 1572872 | tf_op jit(solution)/shard_map/encode/ppermute | solution.py:224

commit v6 on v5

--- a/solution.py
+++ b/solution.py
@@ -9,7 +9,7 @@
 
 NT = (((1,), (1,)), ((), ()))
 CHIPS = [[c + 2 * chip for chip in range(8)] for c in range(2)]
-AHEAD = 4
+AHEAD = 2
 HBM = pl.BlockSpec(memory_space=pltpu.HBM)
 VMEM = pl.BlockSpec(memory_space=pltpu.VMEM)
 
@@ -58,7 +58,7 @@
             copy.start()
         for copy in weights:
             copy.wait()
-        for block in blocks[2:]:
+        for block in blocks[2:4]:
             for copy in block:
                 copy.start()
 
@@ -87,7 +87,11 @@
             else:
                 for copy in blocks[e - skip] + blocks[e + 1 - skip]:
                     copy.wait()
-                if not mine and not later:
+                if not mine:
+                    for block in blocks[e + 4 : e + 4 + 2]:
+                        for copy in block:
+                            copy.start()
+                if not mine and e + 4 + 2 >= examples and not later:
                     later = [pltpu.make_async_copy(queries, passed, p_sem.at[2])]
                     for k in range(ahead):
                         to = pl.ds(k * rows, rows)

time: 55.5 us -> 55.3 us (level)
  no operation moved by 1% of the time
where the time goes in v6:
time: 55.3 us; the launch traced here: 55.1 us
  blocking collectives  17.9 us (32%)
  starting transfers between devices  13.3 us (24%)
  Pallas kernels  11.7 us (21%)
  waiting for transfers between devices  11.4 us (21%)
  other arithmetic  0.62 us (1%)
    pallas_call x2, Pallas kernels, project(): pl.pallas_call(functools.partial(project_kernel, mine, ahead), out_shape=...  9.96 us
    all_to_all x1, blocking collectives, per_device(): lax.all_to_all(part, 'tensor', 0, 0, tiled=True, axis_index_groups=CHIPS)  9.08 us
    all_to_all x1, blocking collectives, per_device(): slices = lax.all_to_all(encoded, 'tensor', 0, 0, tiled=True)  8.85 us
    ppermute x3, waiting for transfers between devices, per_device(): lax.ppermute(pair, 'dp', [(d, (d + 2 * dy) % 8) for d in range(8)])  7.72 us
    all_to_all x1, starting transfers between devices, per_device(): lax.all_to_all(total, 'tensor', 0, 0, tiled=True, axis_index_groups=CHIPS)  5.34 us
    ppermute x3, starting transfers between devices, per_device(): lax.ppermute(pair, 'dp', [(d, (d + 2 * dy) % 8) for d in range(8)])  4.61 us
    all_to_all x1, waiting for transfers between devices, per_device(): lax.all_to_all(total, 'tensor', 0, 0, tiled=True, axis_index_groups=CHIPS)  3.72 us
    ppermute x1, starting transfers between devices, per_device(): beside = lax.ppermute(queries, 'dp', [(d, d ^ 1) for d in range(8)])  3.18 us
  transfers between devices with their start and end apart: 7, of which 4 were waited for; matrix products, arithmetic and copies ran while one was open for 0% of the time, Pallas kernels for 8%

profile of v6, /device:TPU:0, one launch (start us, length us, event | category | flops | bytes accessed | tf_op | source)
XLA Modules:
  0.0 55.1 jit_solution(16265948263272250340)
XLA Ops:
  0.0 5.7 %project_other.1 = (f32[8,128,256]{2,1,0:T(8,128)S(1)}, f32[64,256]{1,0:T(8,128)S(1)}, bf16[64,1792]{1,0:T(8,128)(2,1)S(1)}, bf16[64,512]{1,0:T(8,128)(2,1)S(1)}...) custom-call(bf16[8,512,1792]{2,1,0:T(8,128)(2,1)} %acts.3, bf16[8,512,512]{2,1,0:T(8,128)(2,1)} %grads.3, ...), custom_call_target="tpu_custom_call" | custom-call | tf_op jit(solution)/shard_map/sides/project_other/pallas_call | solution.py:131
  5.7 0.1 collective-permute-start
  5.8 3.2 %collective-permute-start.1 = (f32[64,256]{1,0:T(8,128)S(1)}, f32[64,256]{1,0:T(8,128)S(1)}, u32[]{:S(2)}, u32[]{:S(2)}) collective-permute-start(f32[64,256]{1,0:T(8,128)S(1)} %get-tuple-element.20.queries), channel_id=1, source_target_pairs={{0,16},{16,0},{32,48},{48,32},{64,80},{80,64},{96,112},{112,96},{1... | collective-permute-start | bytes 196616 | tf_op jit(solution)/shard_map/sides/ppermute | solution.py:238
  9.0 4.3 %project_own.1.own = f32[8,128,256]{2,1,0:T(8,128)S(1)} custom-call(bf16[8,512,1792]{2,1,0:T(8,128)(2,1)} %acts.3, bf16[8,512,512]{2,1,0:T(8,128)(2,1)} %grads.3, bf16[64,1792]{1,0:T(8,128)(2,1)S(1)} %get-tuple-element.15.rest_0_, bf16[64,512]{1,0:T(8,128)(2,1)S(1)} %get-tuple-element.16.rest_1_, bf16[512,1792]{1,0:T(8,128)(2,1)S(1)} %get-tuple-element.17.rest_2_, ...), custom_call_target="tpu_custom_call" | custom-call | tf_op jit(solution)/shard_map/sides/project_own/pallas_call | solution.py:131
  13.3 0.0 collective-permute-done.1.beside
  13.3 0.0 collective-permute-done.got
  13.3 1.1 %merge.1 = (f32[8,128,256]{2,1,0:T(8,128)}, f32[128,256]{1,0:T(8,128)S(1)}) custom-call(f32[8,128,256]{2,1,0:T(8,128)S(1)} %project_own.1.own, f32[8,128,256]{2,1,0:T(8,128)S(1)} %collective-permute-done.got, f32[64,256]{1,0:T(8,128)S(1)} %get-tuple-element.20.queries, f32[64,256]{1,0:T(8,128)S(1)} %collective-permute-done.1.beside), custom_call_target="tpu_custom_call" | custom-call | tf_op jit(solution)/shard_map/sides/merge/pallas_call | solution.py:152
  14.4 5.3 %all-to-all-start = ((f32[8,128,256]{2,1,0:T(8,128)}), f32[8,128,256]{2,1,0:T(8,128)S(1)}, u32[]{:S(2)}, u32[]{:S(2)}) async-start(f32[8,128,256]{2,1,0:T(8,128)} %get-tuple-element.21), calls=%async_computation | async-start | bytes 2097152 | tf_op jit(solution)/shard_map/sides/all_to_all | solution.py:242
  19.7 3.0 %collective-permute-start.4 = (f32[128,256]{1,0:T(8,128)S(1)}, f32[128,256]{1,0:T(8,128)S(1)}, u32[]{:S(2)}, u32[]{:S(2)}) collective-permute-start(f32[128,256]{1,0:T(8,128)S(1)} %get-tuple-element.22.q0), channel_id=1, source_target_pairs={{0,96},{16,112},{32,0},{48,16},{64,32},{80,48},{96,64},{112,80},{1... | collective-permute-start | bytes 393224 | tf_op jit(solution)/shard_map/queries/ppermute | solution.py:246
  22.7 0.6 %collective-permute-start.3 = (f32[128,256]{1,0:T(8,128)S(1)}, f32[128,256]{1,0:T(8,128)S(1)}, u32[]{:S(2)}, u32[]{:S(2)}) collective-permute-start(f32[128,256]{1,0:T(8,128)S(1)} %get-tuple-element.22.q0), channel_id=1, source_target_pairs={{0,64},{16,80},{32,96},{48,112},{64,0},{80,16},{96,32},{112,48},{1... | collective-permute-start | bytes 393224 | tf_op jit(solution)/shard_map/queries/ppermute | solution.py:246
  23.4 1.0 %collective-permute-start.2 = (f32[128,256]{1,0:T(8,128)S(1)}, f32[128,256]{1,0:T(8,128)S(1)}, u32[]{:S(2)}, u32[]{:S(2)}) collective-permute-start(f32[128,256]{1,0:T(8,128)S(1)} %get-tuple-element.22.q0), channel_id=1, source_target_pairs={{0,32},{16,48},{32,64},{48,80},{64,96},{80,112},{96,0},{112,16},{1... | collective-permute-start | bytes 393224 | tf_op jit(solution)/shard_map/queries/ppermute | solution.py:246
  24.3 4.0 %collective-permute-done.4.q3 = f32[128,256]{1,0:T(8,128)S(1)} collective-permute-done((f32[128,256]{1,0:T(8,128)S(1)}, f32[128,256]{1,0:T(8,128)S(1)}, u32[]{:S(2)}, u32[]{:S(2)}) %collective-permute-start.4) | collective-permute-done | bytes 131104 | tf_op jit(solution)/shard_map/queries/ppermute | solution.py:246
  28.3 2.3 %collective-permute-done.3.q2 = f32[128,256]{1,0:T(8,128)S(1)} collective-permute-done((f32[128,256]{1,0:T(8,128)S(1)}, f32[128,256]{1,0:T(8,128)S(1)}, u32[]{:S(2)}, u32[]{:S(2)}) %collective-permute-start.3) | collective-permute-done | bytes 131104 | tf_op jit(solution)/shard_map/queries/ppermute | solution.py:246
  30.6 1.4 %collective-permute-done.2.q1 = f32[128,256]{1,0:T(8,128)S(1)} collective-permute-done((f32[128,256]{1,0:T(8,128)S(1)}, f32[128,256]{1,0:T(8,128)S(1)}, u32[]{:S(2)}, u32[]{:S(2)}) %collective-permute-start.2) | collective-permute-done | bytes 131104 | tf_op jit(solution)/shard_map/queries/ppermute | solution.py:246
  32.0 3.7 %all-to-all-done.sides = f32[8,128,256]{2,1,0:T(8,128)S(1)} async-done(((f32[8,128,256]{2,1,0:T(8,128)}), f32[8,128,256]{2,1,0:T(8,128)S(1)}, u32[]{:S(2)}, u32[]{:S(2)}) %all-to-all-start) | async-done | bytes 1048608 | tf_op jit(solution)/shard_map/sides/all_to_all | solution.py:242
  35.8 0.2 encode.1
  36.0 0.1 collective-permute-start.5
  36.1 8.8 %all_to_all.15.slices = f32[16,8,128]{2,1,0:T(8,128)S(1)} all-to-all(f32[16,8,128]{2,1,0:T(8,128)S(1)} %get-tuple-element.23), channel_id=1, replica_groups=mesh['dp'=8,'tensor'=16] {'tensor'}, dimensions={0} | all-to-all | bytes 131072 | tf_op jit(solution)/shard_map/encode/all_to_all | solution.py:251
  45.0 0.0 collective-permute-done.5.far
  45.0 0.4 score.1
  45.4 9.1 %all_to_all.16 = f32[8,8,512]{2,1,0:T(8,128)S(1)} all-to-all(f32[8,8,512]{2,1,0:T(8,128)S(1)} %score.1), channel_id=1, replica_groups={{0,2,4,6,8,10,12,14},{1,3,5,7,9,11,13,15},{16,18,20,22,24,26,28,30},{17..., dimensions={0} | all-to-all | bytes 262144 | tf_op jit(solution)/shard_map/scores/all_to_all | solution.py:256
  54.5 0.6 %reduce_sum.9 = f32[8,512]{1,0:T(8,128)} reduce(f32[8,8,512]{2,1,0:T(8,128)S(1)} %all_to_all.16, f32[]{:T(128)} %constant.0.clone.1), dimensions={0}, to_apply=%region_0.0 | reduce | flops 28672 | bytes 147460 | tf_op jit(solution)/shard_map/scores/reduce_sum | solution.py:257
Async XLA Ops:
  5.7 7.6 %collective-permute-start = (f32[8,128,256]{2,1,0:T(8,128)S(1)}, f32[8,128,256]{2,1,0:T(8,128)S(1)}, u32[]{:S(2)}, u32[]{:S(2)}) collective-permute-start(f32[8,128,256]{2,1,0:T(8,128)S(1)} %get-tuple-element.19), channel_id=1, source_target_pairs={{0,1},{1,0},{2,3},{3,2},{4,5},{5,4},{6,7},{7,6},{8,9},{9,8},{10,11... | collective-permute-start | bytes 3145736 | tf_op jit(solution)/shard_map/sides/ppermute | solution.py:228
  5.8 7.5 %collective-permute-start.1 = (f32[64,256]{1,0:T(8,128)S(1)}, f32[64,256]{1,0:T(8,128)S(1)}, u32[]{:S(2)}, u32[]{:S(2)}) collective-permute-start(f32[64,256]{1,0:T(8,128)S(1)} %get-tuple-element.20.queries), channel_id=1, source_target_pairs={{0,16},{16,0},{32,48},{48,32},{64,80},{80,64},{96,112},{112,96},{1... | collective-permute-start | bytes 196616 | tf_op jit(solution)/shard_map/sides/ppermute | solution.py:238
  14.4 21.4 %all-to-all-start = ((f32[8,128,256]{2,1,0:T(8,128)}), f32[8,128,256]{2,1,0:T(8,128)S(1)}, u32[]{:S(2)}, u32[]{:S(2)}) async-start(f32[8,128,256]{2,1,0:T(8,128)} %get-tuple-element.21), calls=%async_computation | async-start | bytes 2097152 | tf_op jit(solution)/shard_map/sides/all_to_all | solution.py:242
  19.7 8.6 %collective-permute-start.4 = (f32[128,256]{1,0:T(8,128)S(1)}, f32[128,256]{1,0:T(8,128)S(1)}, u32[]{:S(2)}, u32[]{:S(2)}) collective-permute-start(f32[128,256]{1,0:T(8,128)S(1)} %get-tuple-element.22.q0), channel_id=1, source_target_pairs={{0,96},{16,112},{32,0},{48,16},{64,32},{80,48},{96,64},{112,80},{1... | collective-permute-start | bytes 393224 | tf_op jit(solution)/shard_map/queries/ppermute | solution.py:246
  22.7 7.9 %collective-permute-start.3 = (f32[128,256]{1,0:T(8,128)S(1)}, f32[128,256]{1,0:T(8,128)S(1)}, u32[]{:S(2)}, u32[]{:S(2)}) collective-permute-start(f32[128,256]{1,0:T(8,128)S(1)} %get-tuple-element.22.q0), channel_id=1, source_target_pairs={{0,64},{16,80},{32,96},{48,112},{64,0},{80,16},{96,32},{112,48},{1... | collective-permute-start | bytes 393224 | tf_op jit(solution)/shard_map/queries/ppermute | solution.py:246
  23.4 8.7 %collective-permute-start.2 = (f32[128,256]{1,0:T(8,128)S(1)}, f32[128,256]{1,0:T(8,128)S(1)}, u32[]{:S(2)}, u32[]{:S(2)}) collective-permute-start(f32[128,256]{1,0:T(8,128)S(1)} %get-tuple-element.22.q0), channel_id=1, source_target_pairs={{0,32},{16,48},{32,64},{48,80},{64,96},{80,112},{96,0},{112,16},{1... | collective-permute-start | bytes 393224 | tf_op jit(solution)/shard_map/queries/ppermute | solution.py:246
  36.0 8.9 %collective-permute-start.5 = (f32[512,256]{1,0:T(8,128)S(1)}, f32[512,256]{1,0:T(8,128)S(1)}, u32[]{:S(2)}, u32[]{:S(2)}) collective-permute-start(f32[512,256]{1,0:T(8,128)S(1)} %get-tuple-element.24.near), channel_id=1, source_target_pairs={{0,1},{1,0},{2,3},{3,2},{4,5},{5,4},{6,7},{7,6},{8,9},{9,8},{10,11... | collective-permute-start | bytes 1572872 | tf_op jit(solution)/shard_map/encode/ppermute | solution.py:228

commit v7 on v6

--- a/solution.py
+++ b/solution.py
@@ -9,6 +9,7 @@
 
 NT = (((1,), (1,)), ((), ()))
 CHIPS = [[c + 2 * chip for chip in range(8)] for c in range(2)]
+ALONG = (0, 1, 3, 2)
 AHEAD = 2
 HBM = pl.BlockSpec(memory_space=pltpu.HBM)
 VMEM = pl.BlockSpec(memory_space=pltpu.VMEM)
@@ -32,15 +33,19 @@
     else:
         pin, pout, queries, out, passed, held_pin, held_pout, ahead_a, ahead_g, held_a, held_g, sem, p_sem = rest
     examples, rank, rows = out.shape[0], out.shape[1] // 2, out.shape[2]
-    core = lax.axis_index("tensor") % 2
+    t = lax.axis_index("tensor")
+    core = t % 2
     part = core if mine else 1 - core
 
-    def fetch(e, part, to_a, to_g, slot):
-        here = pl.ds(pl.multiple_of(part * rows, rows), rows)
+    def spot(u, part):
+        return 2 * ((t // 4 + ALONG[u // 2]) % 4) + (t // 2 + part) % 2, pl.ds(u % 2 * rows, rows)
+
+    def fetch(u, part, to_a, to_g, slot):
+        e, here = spot(u, part)
         to = pl.ds(slot * rows, rows)
         return [
-            pltpu.make_async_copy(grads.at[e, here, :], to_g.at[to, :], sem.at[0, e]),
-            pltpu.make_async_copy(acts.at[e, here, :], to_a.at[to, :], sem.at[1, e]),
+            pltpu.make_async_copy(grads.at[e, here, :], to_g.at[to, :], sem.at[0, u]),
+            pltpu.make_async_copy(acts.at[e, here, :], to_a.at[to, :], sem.at[1, u]),
         ]
 
     skip = ahead if mine else 0
@@ -95,9 +100,9 @@
                     later = [pltpu.make_async_copy(queries, passed, p_sem.at[2])]
                     for k in range(ahead):
                         to = pl.ds(k * rows, rows)
-                        here = pl.ds(pl.multiple_of(core * rows, rows), rows)
-                        later.append(pltpu.make_async_copy(grads.at[k, here, :], ahead_g.at[to, :], sem.at[2, k]))
-                        later.append(pltpu.make_async_copy(acts.at[k, here, :], ahead_a.at[to, :], sem.at[3, k]))
+                        at, here = spot(k, core)
+                        later.append(pltpu.make_async_copy(grads.at[at, here, :], ahead_g.at[to, :], sem.at[2, k]))
+                        later.append(pltpu.make_async_copy(acts.at[at, here, :], ahead_a.at[to, :], sem.at[3, k]))
                     for copy in later:
                         copy.start()
                 push(e, turn, held_a, held_g, e - skip)
@@ -139,8 +144,10 @@
     )(in_hbm(acts), in_hbm(grads), *more)
 
 
-def merge_kernel(own, got, queries, beside, total, pair):
-    total[...] = own[...] + got[...]
+def merge_kernel(own, got, queries, beside, *outs):
+    for k in range(4):
+        outs[k][...] = own[2 * k : 2 * k + 2] + got[2 * k : 2 * k + 2]
+    pair = outs[4]
     n = queries.shape[0]
     x_hi = lax.axis_index("dp") % 2
     pair[pl.ds(pl.multiple_of(x_hi * n, n), n), :] = queries[...]
@@ -151,18 +158,50 @@
     n, k = queries.shape
     return pl.pallas_call(
         merge_kernel,
-        out_shape=[pltpu.VMEM(own.shape, jnp.float32), pltpu.VMEM((2 * n, k), jnp.float32)],
+        out_shape=[shape(2, *own.shape[1:])] * 4 + [shape(2 * n, k)],
+        in_specs=[VMEM] * 4,
+        out_specs=[VMEM] * 5,
+        compiler_params=limit(8),
+        name="merge",
+    )(own, got, queries, beside)
+
+
+def relay_kernel(arrived, pair, out):
+    out[...] = pair[...]
+
+
+def relay(arrived, pair):
+    return pl.pallas_call(
+        relay_kernel,
+        out_shape=shape(*pair.shape),
+        in_specs=[pl.BlockSpec(memory_space=pl.ANY), VMEM],
+        out_specs=VMEM,
+        compiler_params=limit(8),
+        name="relay",
+    )(arrived, pair)
+
+
+def halve_kernel(a, b, c, d, keep, send):
+    core = lax.axis_index("tensor") % 2
+    keep[...] = (a[core] + d[core]) + (b[core] + c[core])
+    send[...] = (a[1 - core] + d[1 - core]) + (b[1 - core] + c[1 - core])
+
+
+def halve(*sides):
+    return pl.pallas_call(
+        halve_kernel,
+        out_shape=[shape(*sides[0].shape[1:])] * 2,
         in_specs=[VMEM] * 4,
         out_specs=[VMEM] * 2,
         compiler_params=limit(8),
-        name="merge",
-    )(own, got, queries, beside)
-
-
-def encode_kernel(sides, q0, q1, q2, q3, out, near):
+        name="halve",
+    )(*sides)
+
+
+def encode_kernel(keep, got, q0, q1, q2, q3, out, near):
     for dy, block in enumerate((q0, q1, q2, q3)):
         near[pl.ds(dy * block.shape[0], block.shape[0]), :] = block[...]
-    total = ((sides[0] + sides[1]) + (sides[2] + sides[3])) + ((sides[4] + sides[5]) + (sides[6] + sides[7]))
+    total = keep[...] + got[...]
     rank = total.shape[0] // 2
     enc = lax.dot_general(
         total[:rank], total[rank:], NT, precision=lax.Precision.HIGHEST, preferred_element_type=jnp.float32
@@ -172,16 +211,16 @@
         out[t, :, :rank] = enc[8 * (t // 2) : 8 * (t // 2) + 8, :]
 
 
-def encode(sides, *blocks):
+def encode(keep, got, blocks):
     n, k = blocks[0].shape
     return pl.pallas_call(
         encode_kernel,
         out_shape=[shape(16, 8, 128), shape(4 * n, k)],
-        in_specs=[VMEM] * 5,
+        in_specs=[VMEM] * 6,
         out_specs=[VMEM] * 2,
         compiler_params=limit(8),
         name="encode",
-    )(sides, *blocks)
+    )(keep, got, *blocks)
 
 
 def score_kernel(scale, slices, near, far, out, tiles):
@@ -228,6 +267,13 @@
     return lax.ppermute(value, "tensor", [(t, t ^ 1) for t in range(16)])
 
 
+def to_line(value, dz):
+    def to(t):
+        return (t + 4 * dz) % 16 ^ (2 * (t % 2))
+
+    return lax.ppermute(value, "tensor", [(t, to(t)) for t in range(16)])
+
+
 def per_device(acts, grads, proj_in, proj_out, queries):
     length = acts.shape[1]
     rank = proj_in.shape[1]
@@ -238,8 +284,11 @@
         beside = lax.ppermute(queries, "dp", [(d, d ^ 1) for d in range(8)])
         got = to_core(other)
         (own,) = project(True, AHEAD, acts, grads, *first)
-        total, pair = merge(own, got, queries, beside)
-        sides = lax.all_to_all(total, "tensor", 0, 0, tiled=True, axis_index_groups=CHIPS)
+        *sides, pair = merge(own, got, queries, beside)
+        sides = [to_line(v, dz) for v, dz in zip(sides, ALONG)]
+        pair = relay(sides[0], pair)
+        keep, send = halve(*sides)
+        got = to_core(send)
 
     with jax.named_scope("queries"):
         blocks = [pair] + [
@@ -247,7 +296,7 @@
         ]
 
     with jax.named_scope("encode"):
-        encoded, near = encode(sides, *blocks)
+        encoded, near = encode(keep, got, blocks)
         slices = lax.all_to_all(encoded, "tensor", 0, 0, tiled=True)
         far = to_core(near)
 

time: 55.3 us -> 54.7 us (0.989)
  starting transfers between devices: 13.3 us -> 18 us
  waiting for transfers between devices: 11.4 us -> 6.85 us
  Pallas kernels: 11.7 us -> 11.1 us
    ppermute x3, waiting for transfers between devices: 7.72 us -> 0.01 us  [per_device(): lax.ppermute(pair, 'dp', [(d, (d + 2 * dy) % 8) for d in range(8)])]
    ppermute x0 -> x4, starting transfers between devices: none -> 6.64 us  [to_line(): return lax.ppermute(value, 'tensor', [(t, to(t)) for t in range(16)])]
    ppermute x0 -> x4, waiting for transfers between devices: none -> 5.86 us  [to_line(): return lax.ppermute(value, 'tensor', [(t, to(t)) for t in range(16)])]
    all_to_all x1 -> x0, starting transfers between devices: 5.34 us -> none  [per_device(): lax.all_to_all(total, 'tensor', 0, 0, tiled=True, axis_index_groups=CHIPS)]
    all_to_all x1 -> x0, waiting for transfers between devices: 3.72 us -> none  [per_device(): lax.all_to_all(total, 'tensor', 0, 0, tiled=True, axis_index_groups=CHIPS)]
    ppermute x2 -> x3, starting transfers between devices: 0.17 us -> 3.49 us  [to_core(): return lax.ppermute(value, 'tensor', [(t, t ^ 1) for t in range(16)])]
    ppermute x2 -> x3, waiting for transfers between devices: 0.01 us -> 0.98 us  [to_core(): return lax.ppermute(value, 'tensor', [(t, t ^ 1) for t in range(16)])]
    pallas_call x1 -> x3, Pallas kernels: 1.08 us -> 0.18 us  [the longest x1 0.12 us: merge(): pl.pallas_call(merge_kernel, out_shape=[shape(2, *own.shape[1:])] * 4 + [...]
  transfers between devices with their start and end apart: 7 -> 11, of which waited for: 4 -> 2; matrix products, arithmetic and copies ran while one was open for 0% -> 0% of each run, Pallas kernels for 8% -> 8%
where the time goes in v7:
time: 54.7 us; the launch traced here: 54.5 us
  starting transfers between devices  18 us (33%)
  blocking collectives  17.8 us (33%)
  Pallas kernels  11.1 us (20%)
  waiting for transfers between devices  6.85 us (13%)
  other arithmetic  0.62 us (1%)
    pallas_call x2, Pallas kernels, project(): pl.pallas_call(functools.partial(project_kernel, mine, ahead), out_shape=...  10.3 us
    all_to_all x1, blocking collectives, per_device(): lax.all_to_all(part, 'tensor', 0, 0, tiled=True, axis_index_groups=CHIPS)  9.08 us
    all_to_all x1, blocking collectives, per_device(): slices = lax.all_to_all(encoded, 'tensor', 0, 0, tiled=True)  8.71 us
    ppermute x4, starting transfers between devices, to_line(): return lax.ppermute(value, 'tensor', [(t, to(t)) for t in range(16)])  6.64 us
    ppermute x4, waiting for transfers between devices, to_line(): return lax.ppermute(value, 'tensor', [(t, to(t)) for t in range(16)])  5.86 us
    ppermute x3, starting transfers between devices, per_device(): lax.ppermute(pair, 'dp', [(d, (d + 2 * dy) % 8) for d in range(8)])  4.69 us
    ppermute x3, starting transfers between devices, to_core(): return lax.ppermute(value, 'tensor', [(t, t ^ 1) for t in range(16)])  3.49 us
    ppermute x1, starting transfers between devices, per_device(): beside = lax.ppermute(queries, 'dp', [(d, d ^ 1) for d in range(8)])  3.18 us
  transfers between devices with their start and end apart: 11, of which 2 were waited for; matrix products, arithmetic and copies ran while one was open for 0% of the time, Pallas kernels for 8%

profile of v7, /device:TPU:0, one launch (start us, length us, event | category | flops | bytes accessed | tf_op | source)
XLA Modules:
  0.0 54.5 jit_solution(2062969804732359727)
XLA Ops:
  0.0 6.0 %project_other.1 = (f32[8,128,256]{2,1,0:T(8,128)S(1)}, f32[64,256]{1,0:T(8,128)S(1)}, bf16[64,1792]{1,0:T(8,128)(2,1)S(1)}, bf16[64,512]{1,0:T(8,128)(2,1)S(1)}...) custom-call(bf16[8,512,1792]{2,1,0:T(8,128)(2,1)} %acts.3, bf16[8,512,512]{2,1,0:T(8,128)(2,1)} %grads.3, ...), custom_call_target="tpu_custom_call" | custom-call | tf_op jit(solution)/shard_map/sides/project_other/pallas_call | solution.py:136
  6.0 0.1 collective-permute-start
  6.1 3.2 %collective-permute-start.1 = (f32[64,256]{1,0:T(8,128)S(1)}, f32[64,256]{1,0:T(8,128)S(1)}, u32[]{:S(2)}, u32[]{:S(2)}) collective-permute-start(f32[64,256]{1,0:T(8,128)S(1)} %get-tuple-element.25.queries), channel_id=1, source_target_pairs={{0,16},{16,0},{32,48},{48,32},{64,80},{80,64},{96,112},{112,96},{1... | collective-permute-start | bytes 196616 | tf_op jit(solution)/shard_map/sides/ppermute | solution.py:284
  9.3 4.3 %project_own.1.own = f32[8,128,256]{2,1,0:T(8,128)S(1)} custom-call(bf16[8,512,1792]{2,1,0:T(8,128)(2,1)} %acts.3, bf16[8,512,512]{2,1,0:T(8,128)(2,1)} %grads.3, bf16[64,1792]{1,0:T(8,128)(2,1)S(1)} %get-tuple-element.20.rest_0_, bf16[64,512]{1,0:T(8,128)(2,1)S(1)} %get-tuple-element.21.rest_1_, bf16[512,1792]{1,0:T(8,128)(2,1)S(1)} %get-tuple-element.22.rest_2_, ...), custom_call_target="tpu_custom_call" | custom-call | tf_op jit(solution)/shard_map/sides/project_own/pallas_call | solution.py:136
  13.6 0.0 collective-permute-done.1.beside
  13.6 0.0 collective-permute-done.got
  13.6 0.1 merge.1
  13.7 0.7 %collective-permute-start.2 = (f32[2,128,256]{2,1,0:T(8,128)S(1)}, f32[2,128,256]{2,1,0:T(8,128)S(1)}, u32[]{:S(2)}, u32[]{:S(2)}) collective-permute-start(f32[2,128,256]{2,1,0:T(8,128)S(1)} %get-tuple-element.26), channel_id=1, source_target_pairs={{0,0},{1,3},{2,2},{3,1},{4,4},{5,7},{6,6},{7,5},{8,8},{9,11},{10,1... | collective-permute-start | bytes 786440 | tf_op jit(solution)/shard_map/sides/ppermute | solution.py:274
  14.4 2.0 %collective-permute-start.3 = (f32[2,128,256]{2,1,0:T(8,128)S(1)}, f32[2,128,256]{2,1,0:T(8,128)S(1)}, u32[]{:S(2)}, u32[]{:S(2)}) collective-permute-start(f32[2,128,256]{2,1,0:T(8,128)S(1)} %get-tuple-element.27), channel_id=1, source_target_pairs={{0,4},{1,7},{2,6},{3,5},{4,8},{5,11},{6,10},{7,9},{8,12},{9,15},{1... | collective-permute-start | bytes 786440 | tf_op jit(solution)/shard_map/sides/ppermute | solution.py:274
  16.4 2.2 %collective-permute-start.4 = (f32[2,128,256]{2,1,0:T(8,128)S(1)}, f32[2,128,256]{2,1,0:T(8,128)S(1)}, u32[]{:S(2)}, u32[]{:S(2)}) collective-permute-start(f32[2,128,256]{2,1,0:T(8,128)S(1)} %get-tuple-element.28), channel_id=1, source_target_pairs={{0,12},{1,15},{2,14},{3,13},{4,0},{5,3},{6,2},{7,1},{8,4},{9,7},{1... | collective-permute-start | bytes 786440 | tf_op jit(solution)/shard_map/sides/ppermute | solution.py:274
  18.6 1.8 %collective-permute-start.5 = (f32[2,128,256]{2,1,0:T(8,128)S(1)}, f32[2,128,256]{2,1,0:T(8,128)S(1)}, u32[]{:S(2)}, u32[]{:S(2)}) collective-permute-start(f32[2,128,256]{2,1,0:T(8,128)S(1)} %get-tuple-element.29), channel_id=1, source_target_pairs={{0,8},{1,11},{2,10},{3,9},{4,12},{5,15},{6,14},{7,13},{8,0},{9,3},... | collective-permute-start | bytes 786440 | tf_op jit(solution)/shard_map/sides/ppermute | solution.py:274
  20.4 0.0 collective-permute-done.2.a.arrived
  20.4 3.1 %collective-permute-start.9 = (f32[128,256]{1,0:T(8,128)S(1)}, f32[128,256]{1,0:T(8,128)S(1)}, u32[]{:S(2)}, u32[]{:S(2)}) collective-permute-start(f32[128,256]{1,0:T(8,128)S(1)} %relay.1.q0), channel_id=1, source_target_pairs={{0,96},{16,112},{32,0},{48,16},{64,32},{80,48},{96,64},{112,80},{1... | collective-permute-start | bytes 393224 | tf_op jit(solution)/shard_map/queries/ppermute | solution.py:295
  23.5 0.6 %collective-permute-start.8 = (f32[128,256]{1,0:T(8,128)S(1)}, f32[128,256]{1,0:T(8,128)S(1)}, u32[]{:S(2)}, u32[]{:S(2)}) collective-permute-start(f32[128,256]{1,0:T(8,128)S(1)} %relay.1.q0), channel_id=1, source_target_pairs={{0,64},{16,80},{32,96},{48,112},{64,0},{80,16},{96,32},{112,48},{1... | collective-permute-start | bytes 393224 | tf_op jit(solution)/shard_map/queries/ppermute | solution.py:295
  24.1 0.0 collective-permute-done.3.b
  24.1 1.0 %collective-permute-start.7 = (f32[128,256]{1,0:T(8,128)S(1)}, f32[128,256]{1,0:T(8,128)S(1)}, u32[]{:S(2)}, u32[]{:S(2)}) collective-permute-start(f32[128,256]{1,0:T(8,128)S(1)} %relay.1.q0), channel_id=1, source_target_pairs={{0,32},{16,48},{32,64},{48,80},{64,96},{80,112},{96,0},{112,16},{1... | collective-permute-start | bytes 393224 | tf_op jit(solution)/shard_map/queries/ppermute | solution.py:295
  25.1 5.9 %collective-permute-done.4.c = f32[2,128,256]{2,1,0:T(8,128)S(1)} collective-permute-done((f32[2,128,256]{2,1,0:T(8,128)S(1)}, f32[2,128,256]{2,1,0:T(8,128)S(1)}, u32[]{:S(2)}, u32[]{:S(2)}) %collective-permute-start.4) | collective-permute-done | bytes 262176 | tf_op jit(solution)/shard_map/sides/ppermute | solution.py:274
  30.9 0.0 collective-permute-done.5.d
  30.9 0.1 halve.1
  31.0 3.0 %collective-permute-start.6 = (f32[128,256]{1,0:T(8,128)S(1)}, f32[128,256]{1,0:T(8,128)S(1)}, u32[]{:S(2)}, u32[]{:S(2)}) collective-permute-start(f32[128,256]{1,0:T(8,128)S(1)} %get-tuple-element.31), channel_id=1, source_target_pairs={{0,1},{1,0},{2,3},{3,2},{4,5},{5,4},{6,7},{7,6},{8,9},{9,8},{10,11... | collective-permute-start | bytes 393224 | tf_op jit(solution)/shard_map/sides/ppermute | solution.py:267
  34.0 0.0 collective-permute-done.9.q3
  34.0 0.0 collective-permute-done.8.q2
  34.0 0.0 collective-permute-done.7.q1
  34.0 1.0 %collective-permute-done.6.got = f32[128,256]{1,0:T(8,128)S(1)} collective-permute-done((f32[128,256]{1,0:T(8,128)S(1)}, f32[128,256]{1,0:T(8,128)S(1)}, u32[]{:S(2)}, u32[]{:S(2)}) %collective-permute-start.6) | collective-permute-done | bytes 131104 | tf_op jit(solution)/shard_map/sides/ppermute | solution.py:267
  34.9 0.2 encode.1
  35.2 0.4 collective-permute-start.10
  35.6 8.7 %all_to_all.10.slices = f32[16,8,128]{2,1,0:T(8,128)S(1)} all-to-all(f32[16,8,128]{2,1,0:T(8,128)S(1)} %get-tuple-element.33), channel_id=1, replica_groups=mesh['dp'=8,'tensor'=16] {'tensor'}, dimensions={0} | all-to-all | bytes 131072 | tf_op jit(solution)/shard_map/encode/all_to_all | solution.py:300
  44.3 0.0 collective-permute-done.10.far
  44.3 0.4 score.1
  44.8 9.1 %all_to_all.11 = f32[8,8,512]{2,1,0:T(8,128)S(1)} all-to-all(f32[8,8,512]{2,1,0:T(8,128)S(1)} %score.1), channel_id=1, replica_groups={{0,2,4,6,8,10,12,14},{1,3,5,7,9,11,13,15},{16,18,20,22,24,26,28,30},{17..., dimensions={0} | all-to-all | bytes 262144 | tf_op jit(solution)/shard_map/scores/all_to_all | solution.py:305
  53.8 0.6 %reduce_sum.9 = f32[8,512]{1,0:T(8,128)} reduce(f32[8,8,512]{2,1,0:T(8,128)S(1)} %all_to_all.11, f32[]{:T(128)} %constant.0.clone.1), dimensions={0}, to_apply=%region_0.0 | reduce | flops 28672 | bytes 147460 | tf_op jit(solution)/shard_map/scores/reduce_sum | solution.py:306
  (1 shorter events, 0.0 us)
Async XLA Ops:
  6.0 7.6 %collective-permute-start = (f32[8,128,256]{2,1,0:T(8,128)S(1)}, f32[8,128,256]{2,1,0:T(8,128)S(1)}, u32[]{:S(2)}, u32[]{:S(2)}) collective-permute-start(f32[8,128,256]{2,1,0:T(8,128)S(1)} %get-tuple-element.24), channel_id=1, source_target_pairs={{0,1},{1,0},{2,3},{3,2},{4,5},{5,4},{6,7},{7,6},{8,9},{9,8},{10,11... | collective-permute-start | bytes 3145736 | tf_op jit(solution)/shard_map/sides/ppermute | solution.py:267
  6.1 7.5 %collective-permute-start.1 = (f32[64,256]{1,0:T(8,128)S(1)}, f32[64,256]{1,0:T(8,128)S(1)}, u32[]{:S(2)}, u32[]{:S(2)}) collective-permute-start(f32[64,256]{1,0:T(8,128)S(1)} %get-tuple-element.25.queries), channel_id=1, source_target_pairs={{0,16},{16,0},{32,48},{48,32},{64,80},{80,64},{96,112},{112,96},{1... | collective-permute-start | bytes 196616 | tf_op jit(solution)/shard_map/sides/ppermute | solution.py:284
  13.7 6.7 %collective-permute-start.2 = (f32[2,128,256]{2,1,0:T(8,128)S(1)}, f32[2,128,256]{2,1,0:T(8,128)S(1)}, u32[]{:S(2)}, u32[]{:S(2)}) collective-permute-start(f32[2,128,256]{2,1,0:T(8,128)S(1)} %get-tuple-element.26), channel_id=1, source_target_pairs={{0,0},{1,3},{2,2},{3,1},{4,4},{5,7},{6,6},{7,5},{8,8},{9,11},{10,1... | collective-permute-start | bytes 786440 | tf_op jit(solution)/shard_map/sides/ppermute | solution.py:274
  14.4 9.7 %collective-permute-start.3 = (f32[2,128,256]{2,1,0:T(8,128)S(1)}, f32[2,128,256]{2,1,0:T(8,128)S(1)}, u32[]{:S(2)}, u32[]{:S(2)}) collective-permute-start(f32[2,128,256]{2,1,0:T(8,128)S(1)} %get-tuple-element.27), channel_id=1, source_target_pairs={{0,4},{1,7},{2,6},{3,5},{4,8},{5,11},{6,10},{7,9},{8,12},{9,15},{1... | collective-permute-start | bytes 786440 | tf_op jit(solution)/shard_map/sides/ppermute | solution.py:274
  16.4 14.6 %collective-permute-start.4 = (f32[2,128,256]{2,1,0:T(8,128)S(1)}, f32[2,128,256]{2,1,0:T(8,128)S(1)}, u32[]{:S(2)}, u32[]{:S(2)}) collective-permute-start(f32[2,128,256]{2,1,0:T(8,128)S(1)} %get-tuple-element.28), channel_id=1, source_target_pairs={{0,12},{1,15},{2,14},{3,13},{4,0},{5,3},{6,2},{7,1},{8,4},{9,7},{1... | collective-permute-start | bytes 786440 | tf_op jit(solution)/shard_map/sides/ppermute | solution.py:274
  18.6 12.4 %collective-permute-start.5 = (f32[2,128,256]{2,1,0:T(8,128)S(1)}, f32[2,128,256]{2,1,0:T(8,128)S(1)}, u32[]{:S(2)}, u32[]{:S(2)}) collective-permute-start(f32[2,128,256]{2,1,0:T(8,128)S(1)} %get-tuple-element.29), channel_id=1, source_target_pairs={{0,8},{1,11},{2,10},{3,9},{4,12},{5,15},{6,14},{7,13},{8,0},{9,3},... | collective-permute-start | bytes 786440 | tf_op jit(solution)/shard_map/sides/ppermute | solution.py:274
  20.4 13.6 %collective-permute-start.9 = (f32[128,256]{1,0:T(8,128)S(1)}, f32[128,256]{1,0:T(8,128)S(1)}, u32[]{:S(2)}, u32[]{:S(2)}) collective-permute-start(f32[128,256]{1,0:T(8,128)S(1)} %relay.1.q0), channel_id=1, source_target_pairs={{0,96},{16,112},{32,0},{48,16},{64,32},{80,48},{96,64},{112,80},{1... | collective-permute-start | bytes 393224 | tf_op jit(solution)/shard_map/queries/ppermute | solution.py:295
  23.5 10.5 %collective-permute-start.8 = (f32[128,256]{1,0:T(8,128)S(1)}, f32[128,256]{1,0:T(8,128)S(1)}, u32[]{:S(2)}, u32[]{:S(2)}) collective-permute-start(f32[128,256]{1,0:T(8,128)S(1)} %relay.1.q0), channel_id=1, source_target_pairs={{0,64},{16,80},{32,96},{48,112},{64,0},{80,16},{96,32},{112,48},{1... | collective-permute-start | bytes 393224 | tf_op jit(solution)/shard_map/queries/ppermute | solution.py:295
  24.1 9.9 %collective-permute-start.7 = (f32[128,256]{1,0:T(8,128)S(1)}, f32[128,256]{1,0:T(8,128)S(1)}, u32[]{:S(2)}, u32[]{:S(2)}) collective-permute-start(f32[128,256]{1,0:T(8,128)S(1)} %relay.1.q0), channel_id=1, source_target_pairs={{0,32},{16,48},{32,64},{48,80},{64,96},{80,112},{96,0},{112,16},{1... | collective-permute-start | bytes 393224 | tf_op jit(solution)/shard_map/queries/ppermute | solution.py:295
  31.0 4.0 %collective-permute-start.6 = (f32[128,256]{1,0:T(8,128)S(1)}, f32[128,256]{1,0:T(8,128)S(1)}, u32[]{:S(2)}, u32[]{:S(2)}) collective-permute-start(f32[128,256]{1,0:T(8,128)S(1)} %get-tuple-element.31), channel_id=1, source_target_pairs={{0,1},{1,0},{2,3},{3,2},{4,5},{5,4},{6,7},{7,6},{8,9},{9,8},{10,11... | collective-permute-start | bytes 393224 | tf_op jit(solution)/shard_map/sides/ppermute | solution.py:267
  35.2 9.2 %collective-permute-start.10 = (f32[512,256]{1,0:T(8,128)S(1)}, f32[512,256]{1,0:T(8,128)S(1)}, u32[]{:S(2)}, u32[]{:S(2)}) collective-permute-start(f32[512,256]{1,0:T(8,128)S(1)} %get-tuple-element.34.near), channel_id=1, source_target_pairs={{0,1},{1,0},{2,3},{3,2},{4,5},{5,4},{6,7},{7,6},{8,9},{9,8},{10,11... | collective-permute-start | bytes 1572872 | tf_op jit(solution)/shard_map/encode/ppermute | solution.py:267

commit v8 on v7

--- a/solution.py
+++ b/solution.py
@@ -206,16 +206,16 @@
     enc = lax.dot_general(
         total[:rank], total[rank:], NT, precision=lax.Precision.HIGHEST, preferred_element_type=jnp.float32
     )
-    out[...] = jnp.zeros_like(out)
     for t in range(16):
-        out[t, :, :rank] = enc[8 * (t // 2) : 8 * (t // 2) + 8, :]
+        g = 8 * (t // 2)
+        out[t] = jnp.concatenate([enc[g : g + 4, :], enc[g + 4 : g + 8, :]], axis=1)
 
 
 def encode(keep, got, blocks):
     n, k = blocks[0].shape
     return pl.pallas_call(
         encode_kernel,
-        out_shape=[shape(16, 8, 128), shape(4 * n, k)],
+        out_shape=[shape(16, 4, 128), shape(4 * n, k)],
         in_specs=[VMEM] * 6,
         out_specs=[VMEM] * 2,
         compiler_params=limit(8),
@@ -227,9 +227,10 @@
     core = lax.axis_index("tensor") % 2
     y = lax.axis_index("dp") // 2
     for e in range(8):
-        tiles[pl.ds(8 * e, 8), :] = slices[2 * e] + slices[2 * e + 1]
-    rows = [tiles[pl.ds(i, 8, stride=8), :][:, :64] for i in range(8)]
-    low, high = jnp.concatenate(rows[:4], axis=1), jnp.concatenate(rows[4:], axis=1)
+        tiles[pl.ds(4 * e, 4), :] = slices[2 * e] + slices[2 * e + 1]
+    rows = [tiles[pl.ds(i, 8, stride=4), :] for i in range(4)]
+    low = jnp.concatenate([row[:, :64] for row in rows], axis=1)
+    high = jnp.concatenate([row[:, 64:] for row in rows], axis=1)
     mine = jnp.where(core == 0, low, high) * scale
     theirs = jnp.where(core == 0, high, low) * scale
 
@@ -257,7 +258,7 @@
         out_shape=shape(8, 8, 512),
         in_specs=[VMEM] * 3,
         out_specs=VMEM,
-        scratch_shapes=[pltpu.VMEM((64, 128), jnp.float32)],
+        scratch_shapes=[pltpu.VMEM((32, 128), jnp.float32)],
         compiler_params=limit(8),
         name="score",
     )(slices, near, far)

time: 54.7 us -> 54.7 us (level)
  no operation moved by 1% of the time
where the time goes in v8:
time: 54.7 us; the launch traced here: 54.5 us
  starting transfers between devices  18 us (33%)
  blocking collectives  17.7 us (32%)
  Pallas kernels  11.2 us (20%)
  waiting for transfers between devices  6.85 us (13%)
  other arithmetic  0.62 us (1%)
    pallas_call x2, Pallas kernels, project(): pl.pallas_call(functools.partial(project_kernel, mine, ahead), out_shape=...  10.3 us
    all_to_all x1, blocking collectives, per_device(): lax.all_to_all(part, 'tensor', 0, 0, tiled=True, axis_index_groups=CHIPS)  9.08 us
    all_to_all x1, blocking collectives, per_device(): slices = lax.all_to_all(encoded, 'tensor', 0, 0, tiled=True)  8.63 us
    ppermute x4, starting transfers between devices, to_line(): return lax.ppermute(value, 'tensor', [(t, to(t)) for t in range(16)])  6.64 us
    ppermute x4, waiting for transfers between devices, to_line(): return lax.ppermute(value, 'tensor', [(t, to(t)) for t in range(16)])  5.86 us
    ppermute x3, starting transfers between devices, per_device(): lax.ppermute(pair, 'dp', [(d, (d + 2 * dy) % 8) for d in range(8)])  4.69 us
    ppermute x3, starting transfers between devices, to_core(): return lax.ppermute(value, 'tensor', [(t, t ^ 1) for t in range(16)])  3.49 us
    ppermute x1, starting transfers between devices, per_device(): beside = lax.ppermute(queries, 'dp', [(d, d ^ 1) for d in range(8)])  3.18 us
  transfers between devices with their start and end apart: 11, of which 2 were waited for; matrix products, arithmetic and copies ran while one was open for 0% of the time, Pallas kernels for 8%

profile of v8, /device:TPU:0, one launch (start us, length us, event | category | flops | bytes accessed | tf_op | source)
XLA Modules:
  0.0 54.5 jit_solution(11746303648652194458)
XLA Ops:
  0.0 6.0 %project_other.1 = (f32[8,128,256]{2,1,0:T(8,128)S(1)}, f32[64,256]{1,0:T(8,128)S(1)}, bf16[64,1792]{1,0:T(8,128)(2,1)S(1)}, bf16[64,512]{1,0:T(8,128)(2,1)S(1)}...) custom-call(bf16[8,512,1792]{2,1,0:T(8,128)(2,1)} %acts.3, bf16[8,512,512]{2,1,0:T(8,128)(2,1)} %grads.3, ...), custom_call_target="tpu_custom_call" | custom-call | tf_op jit(solution)/shard_map/sides/project_other/pallas_call | solution.py:136
  6.0 0.1 collective-permute-start
  6.1 3.2 %collective-permute-start.1 = (f32[64,256]{1,0:T(8,128)S(1)}, f32[64,256]{1,0:T(8,128)S(1)}, u32[]{:S(2)}, u32[]{:S(2)}) collective-permute-start(f32[64,256]{1,0:T(8,128)S(1)} %get-tuple-element.25.queries), channel_id=1, source_target_pairs={{0,16},{16,0},{32,48},{48,32},{64,80},{80,64},{96,112},{112,96},{1... | collective-permute-start | bytes 196616 | tf_op jit(solution)/shard_map/sides/ppermute | solution.py:285
  9.3 4.3 %project_own.1.own = f32[8,128,256]{2,1,0:T(8,128)S(1)} custom-call(bf16[8,512,1792]{2,1,0:T(8,128)(2,1)} %acts.3, bf16[8,512,512]{2,1,0:T(8,128)(2,1)} %grads.3, bf16[64,1792]{1,0:T(8,128)(2,1)S(1)} %get-tuple-element.20.rest_0_, bf16[64,512]{1,0:T(8,128)(2,1)S(1)} %get-tuple-element.21.rest_1_, bf16[512,1792]{1,0:T(8,128)(2,1)S(1)} %get-tuple-element.22.rest_2_, ...), custom_call_target="tpu_custom_call" | custom-call | tf_op jit(solution)/shard_map/sides/project_own/pallas_call | solution.py:136
  13.6 0.0 collective-permute-done.1.beside
  13.6 0.0 collective-permute-done.got
  13.6 0.1 merge.1
  13.7 0.7 %collective-permute-start.2 = (f32[2,128,256]{2,1,0:T(8,128)S(1)}, f32[2,128,256]{2,1,0:T(8,128)S(1)}, u32[]{:S(2)}, u32[]{:S(2)}) collective-permute-start(f32[2,128,256]{2,1,0:T(8,128)S(1)} %get-tuple-element.26), channel_id=1, source_target_pairs={{0,0},{1,3},{2,2},{3,1},{4,4},{5,7},{6,6},{7,5},{8,8},{9,11},{10,1... | collective-permute-start | bytes 786440 | tf_op jit(solution)/shard_map/sides/ppermute | solution.py:275
  14.4 2.0 %collective-permute-start.3 = (f32[2,128,256]{2,1,0:T(8,128)S(1)}, f32[2,128,256]{2,1,0:T(8,128)S(1)}, u32[]{:S(2)}, u32[]{:S(2)}) collective-permute-start(f32[2,128,256]{2,1,0:T(8,128)S(1)} %get-tuple-element.27), channel_id=1, source_target_pairs={{0,4},{1,7},{2,6},{3,5},{4,8},{5,11},{6,10},{7,9},{8,12},{9,15},{1... | collective-permute-start | bytes 786440 | tf_op jit(solution)/shard_map/sides/ppermute | solution.py:275
  16.4 2.2 %collective-permute-start.4 = (f32[2,128,256]{2,1,0:T(8,128)S(1)}, f32[2,128,256]{2,1,0:T(8,128)S(1)}, u32[]{:S(2)}, u32[]{:S(2)}) collective-permute-start(f32[2,128,256]{2,1,0:T(8,128)S(1)} %get-tuple-element.28), channel_id=1, source_target_pairs={{0,12},{1,15},{2,14},{3,13},{4,0},{5,3},{6,2},{7,1},{8,4},{9,7},{1... | collective-permute-start | bytes 786440 | tf_op jit(solution)/shard_map/sides/ppermute | solution.py:275
  18.6 1.8 %collective-permute-start.5 = (f32[2,128,256]{2,1,0:T(8,128)S(1)}, f32[2,128,256]{2,1,0:T(8,128)S(1)}, u32[]{:S(2)}, u32[]{:S(2)}) collective-permute-start(f32[2,128,256]{2,1,0:T(8,128)S(1)} %get-tuple-element.29), channel_id=1, source_target_pairs={{0,8},{1,11},{2,10},{3,9},{4,12},{5,15},{6,14},{7,13},{8,0},{9,3},... | collective-permute-start | bytes 786440 | tf_op jit(solution)/shard_map/sides/ppermute | solution.py:275
  20.4 0.0 collective-permute-done.2.a.arrived
  20.4 3.1 %collective-permute-start.9 = (f32[128,256]{1,0:T(8,128)S(1)}, f32[128,256]{1,0:T(8,128)S(1)}, u32[]{:S(2)}, u32[]{:S(2)}) collective-permute-start(f32[128,256]{1,0:T(8,128)S(1)} %relay.1.q0), channel_id=1, source_target_pairs={{0,96},{16,112},{32,0},{48,16},{64,32},{80,48},{96,64},{112,80},{1... | collective-permute-start | bytes 393224 | tf_op jit(solution)/shard_map/queries/ppermute | solution.py:296
  23.5 0.6 %collective-permute-start.8 = (f32[128,256]{1,0:T(8,128)S(1)}, f32[128,256]{1,0:T(8,128)S(1)}, u32[]{:S(2)}, u32[]{:S(2)}) collective-permute-start(f32[128,256]{1,0:T(8,128)S(1)} %relay.1.q0), channel_id=1, source_target_pairs={{0,64},{16,80},{32,96},{48,112},{64,0},{80,16},{96,32},{112,48},{1... | collective-permute-start | bytes 393224 | tf_op jit(solution)/shard_map/queries/ppermute | solution.py:296
  24.1 0.0 collective-permute-done.3.b
  24.1 1.0 %collective-permute-start.7 = (f32[128,256]{1,0:T(8,128)S(1)}, f32[128,256]{1,0:T(8,128)S(1)}, u32[]{:S(2)}, u32[]{:S(2)}) collective-permute-start(f32[128,256]{1,0:T(8,128)S(1)} %relay.1.q0), channel_id=1, source_target_pairs={{0,32},{16,48},{32,64},{48,80},{64,96},{80,112},{96,0},{112,16},{1... | collective-permute-start | bytes 393224 | tf_op jit(solution)/shard_map/queries/ppermute | solution.py:296
  25.1 5.9 %collective-permute-done.4.c = f32[2,128,256]{2,1,0:T(8,128)S(1)} collective-permute-done((f32[2,128,256]{2,1,0:T(8,128)S(1)}, f32[2,128,256]{2,1,0:T(8,128)S(1)}, u32[]{:S(2)}, u32[]{:S(2)}) %collective-permute-start.4) | collective-permute-done | bytes 262176 | tf_op jit(solution)/shard_map/sides/ppermute | solution.py:275
  30.9 0.0 collective-permute-done.5.d
  30.9 0.1 halve.1
  31.0 3.0 %collective-permute-start.6 = (f32[128,256]{1,0:T(8,128)S(1)}, f32[128,256]{1,0:T(8,128)S(1)}, u32[]{:S(2)}, u32[]{:S(2)}) collective-permute-start(f32[128,256]{1,0:T(8,128)S(1)} %get-tuple-element.31), channel_id=1, source_target_pairs={{0,1},{1,0},{2,3},{3,2},{4,5},{5,4},{6,7},{7,6},{8,9},{9,8},{10,11... | collective-permute-start | bytes 393224 | tf_op jit(solution)/shard_map/sides/ppermute | solution.py:268
  34.0 0.0 collective-permute-done.9.q3
  34.0 0.0 collective-permute-done.8.q2
  34.0 0.0 collective-permute-done.7.q1
  34.0 1.0 %collective-permute-done.6.got = f32[128,256]{1,0:T(8,128)S(1)} collective-permute-done((f32[128,256]{1,0:T(8,128)S(1)}, f32[128,256]{1,0:T(8,128)S(1)}, u32[]{:S(2)}, u32[]{:S(2)}) %collective-permute-start.6) | collective-permute-done | bytes 131104 | tf_op jit(solution)/shard_map/sides/ppermute | solution.py:268
  34.9 0.3 encode.1
  35.3 0.4 collective-permute-start.10
  35.7 8.6 %all_to_all.10.slices = f32[16,4,128]{2,1,0:T(4,128)S(1)} all-to-all(f32[16,4,128]{2,1,0:T(4,128)S(1)} %get-tuple-element.33), channel_id=1, replica_groups=mesh['dp'=8,'tensor'=16] {'tensor'}, dimensions={0} | all-to-all | bytes 65536 | tf_op jit(solution)/shard_map/encode/all_to_all | solution.py:301
  44.3 0.0 collective-permute-done.10.far
  44.3 0.4 score.1
  44.8 9.1 %all_to_all.11 = f32[8,8,512]{2,1,0:T(8,128)S(1)} all-to-all(f32[8,8,512]{2,1,0:T(8,128)S(1)} %score.1), channel_id=1, replica_groups={{0,2,4,6,8,10,12,14},{1,3,5,7,9,11,13,15},{16,18,20,22,24,26,28,30},{17..., dimensions={0} | all-to-all | bytes 262144 | tf_op jit(solution)/shard_map/scores/all_to_all | solution.py:306
  53.8 0.6 %reduce_sum.9 = f32[8,512]{1,0:T(8,128)} reduce(f32[8,8,512]{2,1,0:T(8,128)S(1)} %all_to_all.11, f32[]{:T(128)} %constant.0.clone.1), dimensions={0}, to_apply=%region_0.0 | reduce | flops 28672 | bytes 147460 | tf_op jit(solution)/shard_map/scores/reduce_sum | solution.py:307
  (1 shorter events, 0.0 us)
Async XLA Ops:
  6.0 7.6 %collective-permute-start = (f32[8,128,256]{2,1,0:T(8,128)S(1)}, f32[8,128,256]{2,1,0:T(8,128)S(1)}, u32[]{:S(2)}, u32[]{:S(2)}) collective-permute-start(f32[8,128,256]{2,1,0:T(8,128)S(1)} %get-tuple-element.24), channel_id=1, source_target_pairs={{0,1},{1,0},{2,3},{3,2},{4,5},{5,4},{6,7},{7,6},{8,9},{9,8},{10,11... | collective-permute-start | bytes 3145736 | tf_op jit(solution)/shard_map/sides/ppermute | solution.py:268
  6.1 7.5 %collective-permute-start.1 = (f32[64,256]{1,0:T(8,128)S(1)}, f32[64,256]{1,0:T(8,128)S(1)}, u32[]{:S(2)}, u32[]{:S(2)}) collective-permute-start(f32[64,256]{1,0:T(8,128)S(1)} %get-tuple-element.25.queries), channel_id=1, source_target_pairs={{0,16},{16,0},{32,48},{48,32},{64,80},{80,64},{96,112},{112,96},{1... | collective-permute-start | bytes 196616 | tf_op jit(solution)/shard_map/sides/ppermute | solution.py:285
  13.7 6.7 %collective-permute-start.2 = (f32[2,128,256]{2,1,0:T(8,128)S(1)}, f32[2,128,256]{2,1,0:T(8,128)S(1)}, u32[]{:S(2)}, u32[]{:S(2)}) collective-permute-start(f32[2,128,256]{2,1,0:T(8,128)S(1)} %get-tuple-element.26), channel_id=1, source_target_pairs={{0,0},{1,3},{2,2},{3,1},{4,4},{5,7},{6,6},{7,5},{8,8},{9,11},{10,1... | collective-permute-start | bytes 786440 | tf_op jit(solution)/shard_map/sides/ppermute | solution.py:275
  14.4 9.7 %collective-permute-start.3 = (f32[2,128,256]{2,1,0:T(8,128)S(1)}, f32[2,128,256]{2,1,0:T(8,128)S(1)}, u32[]{:S(2)}, u32[]{:S(2)}) collective-permute-start(f32[2,128,256]{2,1,0:T(8,128)S(1)} %get-tuple-element.27), channel_id=1, source_target_pairs={{0,4},{1,7},{2,6},{3,5},{4,8},{5,11},{6,10},{7,9},{8,12},{9,15},{1... | collective-permute-start | bytes 786440 | tf_op jit(solution)/shard_map/sides/ppermute | solution.py:275
  16.4 14.6 %collective-permute-start.4 = (f32[2,128,256]{2,1,0:T(8,128)S(1)}, f32[2,128,256]{2,1,0:T(8,128)S(1)}, u32[]{:S(2)}, u32[]{:S(2)}) collective-permute-start(f32[2,128,256]{2,1,0:T(8,128)S(1)} %get-tuple-element.28), channel_id=1, source_target_pairs={{0,12},{1,15},{2,14},{3,13},{4,0},{5,3},{6,2},{7,1},{8,4},{9,7},{1... | collective-permute-start | bytes 786440 | tf_op jit(solution)/shard_map/sides/ppermute | solution.py:275
  18.6 12.4 %collective-permute-start.5 = (f32[2,128,256]{2,1,0:T(8,128)S(1)}, f32[2,128,256]{2,1,0:T(8,128)S(1)}, u32[]{:S(2)}, u32[]{:S(2)}) collective-permute-start(f32[2,128,256]{2,1,0:T(8,128)S(1)} %get-tuple-element.29), channel_id=1, source_target_pairs={{0,8},{1,11},{2,10},{3,9},{4,12},{5,15},{6,14},{7,13},{8,0},{9,3},... | collective-permute-start | bytes 786440 | tf_op jit(solution)/shard_map/sides/ppermute | solution.py:275
  20.4 13.6 %collective-permute-start.9 = (f32[128,256]{1,0:T(8,128)S(1)}, f32[128,256]{1,0:T(8,128)S(1)}, u32[]{:S(2)}, u32[]{:S(2)}) collective-permute-start(f32[128,256]{1,0:T(8,128)S(1)} %relay.1.q0), channel_id=1, source_target_pairs={{0,96},{16,112},{32,0},{48,16},{64,32},{80,48},{96,64},{112,80},{1... | collective-permute-start | bytes 393224 | tf_op jit(solution)/shard_map/queries/ppermute | solution.py:296
  23.5 10.5 %collective-permute-start.8 = (f32[128,256]{1,0:T(8,128)S(1)}, f32[128,256]{1,0:T(8,128)S(1)}, u32[]{:S(2)}, u32[]{:S(2)}) collective-permute-start(f32[128,256]{1,0:T(8,128)S(1)} %relay.1.q0), channel_id=1, source_target_pairs={{0,64},{16,80},{32,96},{48,112},{64,0},{80,16},{96,32},{112,48},{1... | collective-permute-start | bytes 393224 | tf_op jit(solution)/shard_map/queries/ppermute | solution.py:296
  24.1 9.9 %collective-permute-start.7 = (f32[128,256]{1,0:T(8,128)S(1)}, f32[128,256]{1,0:T(8,128)S(1)}, u32[]{:S(2)}, u32[]{:S(2)}) collective-permute-start(f32[128,256]{1,0:T(8,128)S(1)} %relay.1.q0), channel_id=1, source_target_pairs={{0,32},{16,48},{32,64},{48,80},{64,96},{80,112},{96,0},{112,16},{1... | collective-permute-start | bytes 393224 | tf_op jit(solution)/shard_map/queries/ppermute | solution.py:296
  31.0 4.0 %collective-permute-start.6 = (f32[128,256]{1,0:T(8,128)S(1)}, f32[128,256]{1,0:T(8,128)S(1)}, u32[]{:S(2)}, u32[]{:S(2)}) collective-permute-start(f32[128,256]{1,0:T(8,128)S(1)} %get-tuple-element.31), channel_id=1, source_target_pairs={{0,1},{1,0},{2,3},{3,2},{4,5},{5,4},{6,7},{7,6},{8,9},{9,8},{10,11... | collective-permute-start | bytes 393224 | tf_op jit(solution)/shard_map/sides/ppermute | solution.py:268
  35.3 9.1 %collective-permute-start.10 = (f32[512,256]{1,0:T(8,128)S(1)}, f32[512,256]{1,0:T(8,128)S(1)}, u32[]{:S(2)}, u32[]{:S(2)}) collective-permute-start(f32[512,256]{1,0:T(8,128)S(1)} %get-tuple-element.34.near), channel_id=1, source_target_pairs={{0,1},{1,0},{2,3},{3,2},{4,5},{5,4},{6,7},{7,6},{8,9},{9,8},{10,11... | collective-permute-start | bytes 1572872 | tf_op jit(solution)/shard_map/encode/ppermute | solution.py:268

commit v9 on v8

--- a/solution.py
+++ b/solution.py
@@ -63,7 +63,7 @@
             copy.start()
         for copy in weights:
             copy.wait()
-        for block in blocks[2:4]:
+        for block in blocks[2:6]:
             for copy in block:
                 copy.start()
 
@@ -93,10 +93,10 @@
                 for copy in blocks[e - skip] + blocks[e + 1 - skip]:
                     copy.wait()
                 if not mine:
-                    for block in blocks[e + 4 : e + 4 + 2]:
+                    for block in blocks[e + 6 : e + 6 + 2]:
                         for copy in block:
                             copy.start()
-                if not mine and e + 4 + 2 >= examples and not later:
+                if not mine and e + 6 + 2 >= examples and not later:
                     later = [pltpu.make_async_copy(queries, passed, p_sem.at[2])]
                     for k in range(ahead):
                         to = pl.ds(k * rows, rows)

time: 54.7 us -> 54.4 us (level)
  no operation moved by 1% of the time
where the time goes in v9:
time: 54.4 us; the launch traced here: 54.1 us
  starting transfers between devices  18 us (33%)
  blocking collectives  17.7 us (33%)
  Pallas kernels  10.8 us (20%)
  waiting for transfers between devices  6.86 us (13%)
  other arithmetic  0.62 us (1%)
    pallas_call x2, Pallas kernels, project(): pl.pallas_call(functools.partial(project_kernel, mine, ahead), out_shape=...  9.94 us
    all_to_all x1, blocking collectives, per_device(): lax.all_to_all(part, 'tensor', 0, 0, tiled=True, axis_index_groups=CHIPS)  9.08 us
    all_to_all x1, blocking collectives, per_device(): slices = lax.all_to_all(encoded, 'tensor', 0, 0, tiled=True)  8.63 us
    ppermute x4, starting transfers between devices, to_line(): return lax.ppermute(value, 'tensor', [(t, to(t)) for t in range(16)])  6.66 us
    ppermute x4, waiting for transfers between devices, to_line(): return lax.ppermute(value, 'tensor', [(t, to(t)) for t in range(16)])  5.87 us
    ppermute x3, starting transfers between devices, per_device(): lax.ppermute(pair, 'dp', [(d, (d + 2 * dy) % 8) for d in range(8)])  4.68 us
    ppermute x3, starting transfers between devices, to_core(): return lax.ppermute(value, 'tensor', [(t, t ^ 1) for t in range(16)])  3.49 us
    ppermute x1, starting transfers between devices, per_device(): beside = lax.ppermute(queries, 'dp', [(d, d ^ 1) for d in range(8)])  3.18 us
  transfers between devices with their start and end apart: 11, of which 2 were waited for; matrix products, arithmetic and copies ran while one was open for 0% of the time, Pallas kernels for 8%

profile of v9, /device:TPU:0, one launch (start us, length us, event | category | flops | bytes accessed | tf_op | source)
XLA Modules:
  0.0 54.1 jit_solution(2930138524976195727)
XLA Ops:
  0.0 5.7 %project_other.1 = (f32[8,128,256]{2,1,0:T(8,128)S(1)}, f32[64,256]{1,0:T(8,128)S(1)}, bf16[64,1792]{1,0:T(8,128)(2,1)S(1)}, bf16[64,512]{1,0:T(8,128)(2,1)S(1)}...) custom-call(bf16[8,512,1792]{2,1,0:T(8,128)(2,1)} %acts.3, bf16[8,512,512]{2,1,0:T(8,128)(2,1)} %grads.3, ...), custom_call_target="tpu_custom_call" | custom-call | tf_op jit(solution)/shard_map/sides/project_other/pallas_call | solution.py:136
  5.7 0.1 collective-permute-start
  5.8 3.2 %collective-permute-start.1 = (f32[64,256]{1,0:T(8,128)S(1)}, f32[64,256]{1,0:T(8,128)S(1)}, u32[]{:S(2)}, u32[]{:S(2)}) collective-permute-start(f32[64,256]{1,0:T(8,128)S(1)} %get-tuple-element.25.queries), channel_id=1, source_target_pairs={{0,16},{16,0},{32,48},{48,32},{64,80},{80,64},{96,112},{112,96},{1... | collective-permute-start | bytes 196616 | tf_op jit(solution)/shard_map/sides/ppermute | solution.py:285
  9.0 4.3 %project_own.1.own = f32[8,128,256]{2,1,0:T(8,128)S(1)} custom-call(bf16[8,512,1792]{2,1,0:T(8,128)(2,1)} %acts.3, bf16[8,512,512]{2,1,0:T(8,128)(2,1)} %grads.3, bf16[64,1792]{1,0:T(8,128)(2,1)S(1)} %get-tuple-element.20.rest_0_, bf16[64,512]{1,0:T(8,128)(2,1)S(1)} %get-tuple-element.21.rest_1_, bf16[512,1792]{1,0:T(8,128)(2,1)S(1)} %get-tuple-element.22.rest_2_, ...), custom_call_target="tpu_custom_call" | custom-call | tf_op jit(solution)/shard_map/sides/project_own/pallas_call | solution.py:136
  13.2 0.0 collective-permute-done.1.beside
  13.2 0.0 collective-permute-done.got
  13.3 0.1 merge.1
  13.4 0.7 %collective-permute-start.2 = (f32[2,128,256]{2,1,0:T(8,128)S(1)}, f32[2,128,256]{2,1,0:T(8,128)S(1)}, u32[]{:S(2)}, u32[]{:S(2)}) collective-permute-start(f32[2,128,256]{2,1,0:T(8,128)S(1)} %get-tuple-element.26), channel_id=1, source_target_pairs={{0,0},{1,3},{2,2},{3,1},{4,4},{5,7},{6,6},{7,5},{8,8},{9,11},{10,1... | collective-permute-start | bytes 786440 | tf_op jit(solution)/shard_map/sides/ppermute | solution.py:275
  14.1 2.0 %collective-permute-start.3 = (f32[2,128,256]{2,1,0:T(8,128)S(1)}, f32[2,128,256]{2,1,0:T(8,128)S(1)}, u32[]{:S(2)}, u32[]{:S(2)}) collective-permute-start(f32[2,128,256]{2,1,0:T(8,128)S(1)} %get-tuple-element.27), channel_id=1, source_target_pairs={{0,4},{1,7},{2,6},{3,5},{4,8},{5,11},{6,10},{7,9},{8,12},{9,15},{1... | collective-permute-start | bytes 786440 | tf_op jit(solution)/shard_map/sides/ppermute | solution.py:275
  16.1 2.2 %collective-permute-start.4 = (f32[2,128,256]{2,1,0:T(8,128)S(1)}, f32[2,128,256]{2,1,0:T(8,128)S(1)}, u32[]{:S(2)}, u32[]{:S(2)}) collective-permute-start(f32[2,128,256]{2,1,0:T(8,128)S(1)} %get-tuple-element.28), channel_id=1, source_target_pairs={{0,12},{1,15},{2,14},{3,13},{4,0},{5,3},{6,2},{7,1},{8,4},{9,7},{1... | collective-permute-start | bytes 786440 | tf_op jit(solution)/shard_map/sides/ppermute | solution.py:275
  18.3 1.8 %collective-permute-start.5 = (f32[2,128,256]{2,1,0:T(8,128)S(1)}, f32[2,128,256]{2,1,0:T(8,128)S(1)}, u32[]{:S(2)}, u32[]{:S(2)}) collective-permute-start(f32[2,128,256]{2,1,0:T(8,128)S(1)} %get-tuple-element.29), channel_id=1, source_target_pairs={{0,8},{1,11},{2,10},{3,9},{4,12},{5,15},{6,14},{7,13},{8,0},{9,3},... | collective-permute-start | bytes 786440 | tf_op jit(solution)/shard_map/sides/ppermute | solution.py:275
  20.0 0.0 collective-permute-done.2.a.arrived
  20.1 3.1 %collective-permute-start.9 = (f32[128,256]{1,0:T(8,128)S(1)}, f32[128,256]{1,0:T(8,128)S(1)}, u32[]{:S(2)}, u32[]{:S(2)}) collective-permute-start(f32[128,256]{1,0:T(8,128)S(1)} %relay.1.q0), channel_id=1, source_target_pairs={{0,96},{16,112},{32,0},{48,16},{64,32},{80,48},{96,64},{112,80},{1... | collective-permute-start | bytes 393224 | tf_op jit(solution)/shard_map/queries/ppermute | solution.py:296
  23.1 0.6 %collective-permute-start.8 = (f32[128,256]{1,0:T(8,128)S(1)}, f32[128,256]{1,0:T(8,128)S(1)}, u32[]{:S(2)}, u32[]{:S(2)}) collective-permute-start(f32[128,256]{1,0:T(8,128)S(1)} %relay.1.q0), channel_id=1, source_target_pairs={{0,64},{16,80},{32,96},{48,112},{64,0},{80,16},{96,32},{112,48},{1... | collective-permute-start | bytes 393224 | tf_op jit(solution)/shard_map/queries/ppermute | solution.py:296
  23.8 0.0 collective-permute-done.3.b
  23.8 1.0 %collective-permute-start.7 = (f32[128,256]{1,0:T(8,128)S(1)}, f32[128,256]{1,0:T(8,128)S(1)}, u32[]{:S(2)}, u32[]{:S(2)}) collective-permute-start(f32[128,256]{1,0:T(8,128)S(1)} %relay.1.q0), channel_id=1, source_target_pairs={{0,32},{16,48},{32,64},{48,80},{64,96},{80,112},{96,0},{112,16},{1... | collective-permute-start | bytes 393224 | tf_op jit(solution)/shard_map/queries/ppermute | solution.py:296
  24.7 5.9 %collective-permute-done.4.c = f32[2,128,256]{2,1,0:T(8,128)S(1)} collective-permute-done((f32[2,128,256]{2,1,0:T(8,128)S(1)}, f32[2,128,256]{2,1,0:T(8,128)S(1)}, u32[]{:S(2)}, u32[]{:S(2)}) %collective-permute-start.4) | collective-permute-done | bytes 262176 | tf_op jit(solution)/shard_map/sides/ppermute | solution.py:275
  30.6 0.0 collective-permute-done.5.d
  30.6 0.1 halve.1
  30.7 3.0 %collective-permute-start.6 = (f32[128,256]{1,0:T(8,128)S(1)}, f32[128,256]{1,0:T(8,128)S(1)}, u32[]{:S(2)}, u32[]{:S(2)}) collective-permute-start(f32[128,256]{1,0:T(8,128)S(1)} %get-tuple-element.31), channel_id=1, source_target_pairs={{0,1},{1,0},{2,3},{3,2},{4,5},{5,4},{6,7},{7,6},{8,9},{9,8},{10,11... | collective-permute-start | bytes 393224 | tf_op jit(solution)/shard_map/sides/ppermute | solution.py:268
  33.6 0.0 collective-permute-done.9.q3
  33.6 0.0 collective-permute-done.8.q2
  33.6 0.0 collective-permute-done.7.q1
  33.6 1.0 %collective-permute-done.6.got = f32[128,256]{1,0:T(8,128)S(1)} collective-permute-done((f32[128,256]{1,0:T(8,128)S(1)}, f32[128,256]{1,0:T(8,128)S(1)}, u32[]{:S(2)}, u32[]{:S(2)}) %collective-permute-start.6) | collective-permute-done | bytes 131104 | tf_op jit(solution)/shard_map/sides/ppermute | solution.py:268
  34.6 0.3 encode.1
  34.9 0.4 collective-permute-start.10
  35.4 8.6 %all_to_all.10.slices = f32[16,4,128]{2,1,0:T(4,128)S(1)} all-to-all(f32[16,4,128]{2,1,0:T(4,128)S(1)} %get-tuple-element.33), channel_id=1, replica_groups=mesh['dp'=8,'tensor'=16] {'tensor'}, dimensions={0} | all-to-all | bytes 65536 | tf_op jit(solution)/shard_map/encode/all_to_all | solution.py:301
  44.0 0.0 collective-permute-done.10.far
  44.0 0.4 score.1
  44.4 9.1 %all_to_all.11 = f32[8,8,512]{2,1,0:T(8,128)S(1)} all-to-all(f32[8,8,512]{2,1,0:T(8,128)S(1)} %score.1), channel_id=1, replica_groups={{0,2,4,6,8,10,12,14},{1,3,5,7,9,11,13,15},{16,18,20,22,24,26,28,30},{17..., dimensions={0} | all-to-all | bytes 262144 | tf_op jit(solution)/shard_map/scores/all_to_all | solution.py:306
  53.5 0.6 %reduce_sum.9 = f32[8,512]{1,0:T(8,128)} reduce(f32[8,8,512]{2,1,0:T(8,128)S(1)} %all_to_all.11, f32[]{:T(128)} %constant.0.clone.1), dimensions={0}, to_apply=%region_0.0 | reduce | flops 28672 | bytes 147460 | tf_op jit(solution)/shard_map/scores/reduce_sum | solution.py:307
  (1 shorter events, 0.0 us)
Async XLA Ops:
  5.7 7.6 %collective-permute-start = (f32[8,128,256]{2,1,0:T(8,128)S(1)}, f32[8,128,256]{2,1,0:T(8,128)S(1)}, u32[]{:S(2)}, u32[]{:S(2)}) collective-permute-start(f32[8,128,256]{2,1,0:T(8,128)S(1)} %get-tuple-element.24), channel_id=1, source_target_pairs={{0,1},{1,0},{2,3},{3,2},{4,5},{5,4},{6,7},{7,6},{8,9},{9,8},{10,11... | collective-permute-start | bytes 3145736 | tf_op jit(solution)/shard_map/sides/ppermute | solution.py:268
  5.8 7.4 %collective-permute-start.1 = (f32[64,256]{1,0:T(8,128)S(1)}, f32[64,256]{1,0:T(8,128)S(1)}, u32[]{:S(2)}, u32[]{:S(2)}) collective-permute-start(f32[64,256]{1,0:T(8,128)S(1)} %get-tuple-element.25.queries), channel_id=1, source_target_pairs={{0,16},{16,0},{32,48},{48,32},{64,80},{80,64},{96,112},{112,96},{1... | collective-permute-start | bytes 196616 | tf_op jit(solution)/shard_map/sides/ppermute | solution.py:285
  13.4 6.7 %collective-permute-start.2 = (f32[2,128,256]{2,1,0:T(8,128)S(1)}, f32[2,128,256]{2,1,0:T(8,128)S(1)}, u32[]{:S(2)}, u32[]{:S(2)}) collective-permute-start(f32[2,128,256]{2,1,0:T(8,128)S(1)} %get-tuple-element.26), channel_id=1, source_target_pairs={{0,0},{1,3},{2,2},{3,1},{4,4},{5,7},{6,6},{7,5},{8,8},{9,11},{10,1... | collective-permute-start | bytes 786440 | tf_op jit(solution)/shard_map/sides/ppermute | solution.py:275
  14.1 9.7 %collective-permute-start.3 = (f32[2,128,256]{2,1,0:T(8,128)S(1)}, f32[2,128,256]{2,1,0:T(8,128)S(1)}, u32[]{:S(2)}, u32[]{:S(2)}) collective-permute-start(f32[2,128,256]{2,1,0:T(8,128)S(1)} %get-tuple-element.27), channel_id=1, source_target_pairs={{0,4},{1,7},{2,6},{3,5},{4,8},{5,11},{6,10},{7,9},{8,12},{9,15},{1... | collective-permute-start | bytes 786440 | tf_op jit(solution)/shard_map/sides/ppermute | solution.py:275
  16.1 14.6 %collective-permute-start.4 = (f32[2,128,256]{2,1,0:T(8,128)S(1)}, f32[2,128,256]{2,1,0:T(8,128)S(1)}, u32[]{:S(2)}, u32[]{:S(2)}) collective-permute-start(f32[2,128,256]{2,1,0:T(8,128)S(1)} %get-tuple-element.28), channel_id=1, source_target_pairs={{0,12},{1,15},{2,14},{3,13},{4,0},{5,3},{6,2},{7,1},{8,4},{9,7},{1... | collective-permute-start | bytes 786440 | tf_op jit(solution)/shard_map/sides/ppermute | solution.py:275
  18.3 12.4 %collective-permute-start.5 = (f32[2,128,256]{2,1,0:T(8,128)S(1)}, f32[2,128,256]{2,1,0:T(8,128)S(1)}, u32[]{:S(2)}, u32[]{:S(2)}) collective-permute-start(f32[2,128,256]{2,1,0:T(8,128)S(1)} %get-tuple-element.29), channel_id=1, source_target_pairs={{0,8},{1,11},{2,10},{3,9},{4,12},{5,15},{6,14},{7,13},{8,0},{9,3},... | collective-permute-start | bytes 786440 | tf_op jit(solution)/shard_map/sides/ppermute | solution.py:275
  20.1 13.6 %collective-permute-start.9 = (f32[128,256]{1,0:T(8,128)S(1)}, f32[128,256]{1,0:T(8,128)S(1)}, u32[]{:S(2)}, u32[]{:S(2)}) collective-permute-start(f32[128,256]{1,0:T(8,128)S(1)} %relay.1.q0), channel_id=1, source_target_pairs={{0,96},{16,112},{32,0},{48,16},{64,32},{80,48},{96,64},{112,80},{1... | collective-permute-start | bytes 393224 | tf_op jit(solution)/shard_map/queries/ppermute | solution.py:296
  23.1 10.5 %collective-permute-start.8 = (f32[128,256]{1,0:T(8,128)S(1)}, f32[128,256]{1,0:T(8,128)S(1)}, u32[]{:S(2)}, u32[]{:S(2)}) collective-permute-start(f32[128,256]{1,0:T(8,128)S(1)} %relay.1.q0), channel_id=1, source_target_pairs={{0,64},{16,80},{32,96},{48,112},{64,0},{80,16},{96,32},{112,48},{1... | collective-permute-start | bytes 393224 | tf_op jit(solution)/shard_map/queries/ppermute | solution.py:296
  23.8 9.9 %collective-permute-start.7 = (f32[128,256]{1,0:T(8,128)S(1)}, f32[128,256]{1,0:T(8,128)S(1)}, u32[]{:S(2)}, u32[]{:S(2)}) collective-permute-start(f32[128,256]{1,0:T(8,128)S(1)} %relay.1.q0), channel_id=1, source_target_pairs={{0,32},{16,48},{32,64},{48,80},{64,96},{80,112},{96,0},{112,16},{1... | collective-permute-start | bytes 393224 | tf_op jit(solution)/shard_map/queries/ppermute | solution.py:296
  30.7 4.0 %collective-permute-start.6 = (f32[128,256]{1,0:T(8,128)S(1)}, f32[128,256]{1,0:T(8,128)S(1)}, u32[]{:S(2)}, u32[]{:S(2)}) collective-permute-start(f32[128,256]{1,0:T(8,128)S(1)} %get-tuple-element.31), channel_id=1, source_target_pairs={{0,1},{1,0},{2,3},{3,2},{4,5},{5,4},{6,7},{7,6},{8,9},{9,8},{10,11... | collective-permute-start | bytes 393224 | tf_op jit(solution)/shard_map/sides/ppermute | solution.py:268
  34.9 9.1 %collective-permute-start.10 = (f32[512,256]{1,0:T(8,128)S(1)}, f32[512,256]{1,0:T(8,128)S(1)}, u32[]{:S(2)}, u32[]{:S(2)}) collective-permute-start(f32[512,256]{1,0:T(8,128)S(1)} %get-tuple-element.34.near), channel_id=1, source_target_pairs={{0,1},{1,0},{2,3},{3,2},{4,5},{5,4},{6,7},{7,6},{8,9},{9,8},{10,11... | collective-permute-start | bytes 1572872 | tf_op jit(solution)/shard_map/encode/ppermute | solution.py:268
